TPU v7x, 512 devices: a whole 4x8x8 slice. The times are simulated.
512 devices in a mesh: chan: 64 (over y, x, core), band: 8 (over z).
Axes of the slice: x: 4, y: 8, z: 8, core: 2. Of those that a mesh axis runs over, the one named last changes fastest.
Arguments:
- traces: bfloat16 [64, 128, 32768], P(None, 'band', 'chan'), may hold values from -6 to 6
- window_starts: int32 [64], replicated, may hold values from 0 to 32512
- tile_offsets: int32 [64, 4], P('chan'), may hold values from 0 to 3, as said below
- tile_count: int32 [64], P('chan'), may hold values from 1 to 4, as said below
Outputs:
- correlations: bfloat16 [64, 4, 128, 128, 201], P('chan', None, 'band')
Inputs may be any that keep to these rules, and one draw needn't show every extreme that they name: `tile_offsets`: in row c the first tile_count[c] entries are distinct offsets d in increasing order with c + d < 64; the other entries are 0. `tile_count`: block 0 has all 4 slots live; the last block has one.
All inputs are finite; a program needn't handle non-finite values.
Results may differ from a plain program's by a relative error of at most 0.0077.
Values may be sent and summed in bfloat16 or wider, within the bound.
No kernel may reach another device: no remote copies, remote signals or barrier semaphores. Data moves between devices by JAX's collectives and lax.ppermute only.
A program may use at most 64 MiB of HBM per device.

v0:
```python
import math

import jax
import jax.numpy as jnp
from jax import lax
from jax.sharding import PartitionSpec as P

CB = 128
RANGE = 300
WIN = 256
LAGS = 201
DMAX = 3
TMAX = 4


EPS = 1e-06


def passed_along(block, axis, distance):
    devices = range(lax.axis_size(axis))
    route = [(i - distance, i) for i in devices if i - distance in devices]
    return lax.ppermute(block, axis, route)


def band_tables(bands):
    times = jnp.arange(WIN, dtype=jnp.int32)
    bins = jnp.arange(WIN // 2, dtype=jnp.int32)
    width = WIN // 2 // bands
    hann = 0.5 - 0.5 * jnp.cos(2.0 * math.pi * times.astype(jnp.float32) / WIN)
    phase = 2.0 * math.pi * (times[:, None] * bins[None, :] % WIN).astype(jnp.float32) / WIN
    forward = jnp.stack(
        [hann[:, None] * jnp.cos(phase), -hann[:, None] * jnp.sin(phase)], axis=1
    ).astype(jnp.bfloat16)
    forward = forward.reshape(WIN, 2, bands, width).transpose(0, 2, 1, 3).reshape(WIN, WIN)
    shifts = jnp.arange(LAGS, dtype=jnp.int32) - (LAGS - 1) // 2
    turn = 2.0 * math.pi * (bins[:, None] * shifts[None, :] % WIN).astype(jnp.float32) / WIN
    factor = jnp.where(bins == 0, 1.0, 2.0).astype(jnp.float32)[:, None]
    inverse = jnp.stack([factor * jnp.cos(turn), -factor * jnp.sin(turn)], axis=0).astype(
        jnp.bfloat16
    )
    inverse = inverse.reshape(2, bands, width, LAGS).transpose(1, 0, 2, 3).reshape(WIN, LAGS)
    return (forward, inverse)


def local(traces, window_starts, tile_offsets, tile_count):
    bands = lax.axis_size("band")
    width = WIN // 2 // bands
    forward, inverse = band_tables(bands)
    regrouped = lax.all_to_all(traces, "chan", split_axis=0, concat_axis=2, tiled=True)
    series = regrouped[0]
    windows = jax.vmap(lambda begin: lax.dynamic_slice_in_dim(series, begin, WIN, 1))(window_starts)
    spectra = jnp.einsum(
        "wct,tk->kcw", windows, forward, preferred_element_type=jnp.float32
    ).astype(jnp.bfloat16)
    banded = lax.all_to_all(spectra, "band", split_axis=0, concat_axis=1, tiled=True)
    count_win = banded.shape[2]
    parts = banded.astype(jnp.float32).reshape(2, width, CB, count_win)
    power = jnp.mean(parts[0] * parts[0] + parts[1] * parts[1], axis=2)
    whitened = (parts * lax.rsqrt(power + EPS)[None, :, :, None]).astype(jnp.bfloat16)
    received = [whitened]
    for offset in range(1, DMAX + 1):
        got = passed_along(whitened, "chan", -offset)
        received.append(got)
    stacked = jnp.stack(received)
    offsets = tile_offsets[0]
    columns = jnp.take(stacked, offsets, axis=0)
    swapped = jnp.stack([-whitened[1], whitened[0]])
    real_part = jnp.einsum(
        "xfiw,txfjw->tfij", whitened, columns, preferred_element_type=jnp.float32
    )
    imag_part = jnp.einsum("xfiw,txfjw->tfij", swapped, columns, preferred_element_type=jnp.float32)
    rows_idx = jnp.arange(CB, dtype=jnp.int32)
    slots = jnp.arange(TMAX, dtype=jnp.int32)
    spread = offsets[:, None, None] * CB + rows_idx[None, None, :] - rows_idx[None, :, None]
    keep = ((spread > 0) & (spread <= RANGE) & (slots < tile_count[0])[:, None, None]).astype(
        jnp.float32
    )
    cross = (jnp.stack([real_part, imag_part], axis=1) / count_win * keep[:, None, None]).astype(
        jnp.bfloat16
    )
    cross = cross.reshape(TMAX, 2 * width, CB, CB)
    lagged = lax.all_to_all(cross, "band", split_axis=2, concat_axis=1, tiled=True)
    result = jnp.einsum("tkij,kl->tijl", lagged, inverse, preferred_element_type=jnp.float32)
    return result.astype(jnp.bfloat16)[None]


def solution(mesh):
    placed = (P(None, "band", "chan"), P(), P("chan", None), P("chan"))
    return jax.shard_map(
        local,
        mesh=mesh,
        in_specs=placed,
        out_specs=P("chan", None, "band", None, None),
        check_vma=False,
    )
```

profile of v0, /device:TPU:80, one launch (start us, length us, event | category | flops | bytes accessed | tf_op | source)
XLA Modules:
  0.0 330.3 jit_solution(1179082594780539591)
XLA Ops:
  0.0 10.6 %all-to-all-start = ((bf16[64,16,512]{2,1,0:T(8,128)(2,1)}), bf16[64,16,512]{2,1,0:T(8,128)(2,1)S(1)}, u32[]{:S(2)}, u32[]{:S(2)}) async-start(bf16[64,16,512]{2,1,0:T(8,128)(2,1)} %param.4), calls=%async_computation | async-start | bytes 2097152 | tf_op jit(solution)/shard_map/all_to_all | solution.py:49
  12.0 27.0 %all-to-all-done = bf16[64,16,512]{2,1,0:T(8,128)(2,1)S(1)} async-done(((bf16[64,16,512]{2,1,0:T(8,128)(2,1)}), bf16[64,16,512]{2,1,0:T(8,128)(2,1)S(1)}, u32[]{:S(2)}, u32[]{:S(2)}) %all-to-all-start) | async-done | bytes 1048608 | tf_op jit(solution)/shard_map/all_to_all | solution.py:49
  39.1 86.7 %while.1 = (s32[]{:T(128)}, bf16[16,32768]{1,0:T(8,128)(2,1)S(1)}, s32[64,2]{0,1:T(2,128)S(1)}, bf16[64,16,256]{2,1,0:T(8,128)(2,1)S(1)}, s32[]{:T(128)}) while((s32[]{:T(128)}, bf16[16,32768]{1,0:T(8,128)(2,1)S(1)}, s32[64,2]{0,1:T(2,128)S(1)}, bf16[64,16,256]{2,1,0:T(8,128)(2,1)S(1)}, s32[]{:T(128)}) %tuple.24), condition=%wide.while_cond, body=%wide.while_body.sunk | while | flops 2 | bytes 16481 | solution.py:51
  53.4 0.7 bitcast_dynamic-update-slice_fusion.2
  56.1 0.7 bitcast_dynamic-update-slice_fusion.2
  58.8 0.7 bitcast_dynamic-update-slice_fusion.2
  61.5 0.7 bitcast_dynamic-update-slice_fusion.2
  126.2 1.0 copy.43
  127.1 1.5 reshape.421
  128.6 10.0 %all-to-all-start.1 = ((bf16[8,2,16384]{2,1,0:T(2,128)(2,1)}), bf16[8,2,16384]{2,1,0:T(2,128)(2,1)S(1)}, u32[]{:S(2)}, u32[]{:S(2)}) async-start(bf16[8,2,16384]{2,1,0:T(2,128)(2,1)} %reshape.421), calls=%async_computation.1 | async-start | bytes 1048576 | tf_op jit(solution)/shard_map/all_to_all | solution.py:55
  138.9 14.3 %all-to-all-done.1 = bf16[8,2,16384]{2,1,0:T(2,128)(2,1)S(1)} async-done(((bf16[8,2,16384]{2,1,0:T(2,128)(2,1)}), bf16[8,2,16384]{2,1,0:T(2,128)(2,1)S(1)}, u32[]{:S(2)}, u32[]{:S(2)}) %all-to-all-start.1) | async-done | bytes 524320 | tf_op jit(solution)/shard_map/all_to_all | solution.py:55
  154.7 1.6 copy.48
  156.4 1.4 multiply_convert_fusion.1
  157.7 1.9 collective-permute-start
  159.7 5.4 %collective-permute-start.1 = (bf16[2,16,128,64]{2,3,0,1:T(8,128)(2,1)S(1)}, bf16[2,16,128,64]{2,3,0,1:T(8,128)(2,1)}, u32[]{:S(2)}, u32[]{:S(2)}) collective-permute-start(bf16[2,16,128,64]{2,3,0,1:T(8,128)(2,1)S(1)} %multiply_convert_fusion.1), channel_id=1, source_target_pairs={{16,0},{24,8},{32,16},{40,24},{48,32},{56,40},{64,48},{72,56},{80,... | collective-permute-start | bytes 1572872 | tf_op jit(solution)/shard_map/ppermute | solution.py:22
  165.1 2.3 collective-permute-start.2
  167.4 1.6 copy.46
  169.1 1.4 multiply_convert_fusion.2
  170.4 19.2 %collective-permute-done.1 = bf16[2,16,128,64]{2,3,0,1:T(8,128)(2,1)} collective-permute-done((bf16[2,16,128,64]{2,3,0,1:T(8,128)(2,1)S(1)}, bf16[2,16,128,64]{2,3,0,1:T(8,128)(2,1)}, u32[]{:S(2)}, u32[]{:S(2)}) %collective-permute-start.1) | collective-permute-done | bytes 524320 | tf_op jit(solution)/shard_map/ppermute | solution.py:22
  189.6 4.8 %collective-permute-done.2 = bf16[2,16,128,64]{2,3,0,1:T(8,128)(2,1)} collective-permute-done((bf16[2,16,128,64]{2,3,0,1:T(8,128)(2,1)S(1)}, bf16[2,16,128,64]{2,3,0,1:T(8,128)(2,1)}, u32[]{:S(2)}, u32[]{:S(2)}) %collective-permute-start.2) | collective-permute-done | bytes 524320 | tf_op jit(solution)/shard_map/ppermute | solution.py:22
  194.4 2.9 pad_maximum_fusion.1
  197.3 2.5 gather_fusion
  199.8 0.9 convolution_bitcast_fusion.1
  200.8 0.9 convolution_bitcast_fusion
  201.7 3.8 %pad_maximum_fusion = f32[4,2,16,128,128]{3,4,0,2,1:T(8,128)} fusion(f32[4,1,16,128,128]{3,4,0,2,1:T(8,128)S(1)} %convolution_bitcast_fusion, f32[4,1,16,128,128]{3,4,0,2,1:T(8,128)S(1)} %convolution_bitcast_fusion.1), kind=kLoop, calls=%fused_computation.3 | loop fusion | flops 2097152 | bytes 16777216 | tf_op jit(solution)/shard_map/stack | solution.py:78
  205.5 10.3 %copy.51 = f32[4,32,128,128]{3,1,0,2:T(8,128)} copy(f32[4,32,128,128]{2,3,0,1:T(8,128)} %bitcast.82) | data formatting | bytes 16777216 | tf_op jit(solution)/shard_map/stack | solution.py:78
  215.8 6.7 %multiply_convert_fusion = bf16[4,32,128,128]{3,1,0,2:T(8,128)(2,1)} fusion(f32[4,32,128,128]{3,1,0,2:T(8,128)} %copy.51, f32[4,128,128]{2,0,1:T(4,128)S(1)} %fusion.13), kind=kLoop, calls=%fused_computation.4 | loop fusion | flops 4194304 | bytes 12845056 | tf_op jit(solution)/shard_map/convert_element_type | solution.py:78
  222.5 9.0 %all-to-all-start.2 = ((bf16[4,32,128,128]{3,1,0,2:T(8,128)(2,1)}), bf16[4,32,128,128]{3,1,0,2:T(8,128)(2,1)}, u32[]{:S(2)}, u32[]{:S(2)}) async-start(bf16[4,32,128,128]{3,1,0,2:T(8,128)(2,1)} %multiply_convert_fusion), calls=%async_computation.2 | async-start | bytes 8388608 | tf_op jit(solution)/shard_map/all_to_all | solution.py:82
  232.1 91.0 %all-to-all-done.2 = bf16[4,32,128,128]{3,1,0,2:T(8,128)(2,1)} async-done(((bf16[4,32,128,128]{3,1,0,2:T(8,128)(2,1)}), bf16[4,32,128,128]{3,1,0,2:T(8,128)(2,1)}, u32[]{:S(2)}, u32[]{:S(2)}) %all-to-all-start.2) | async-done | bytes 4194336 | tf_op jit(solution)/shard_map/all_to_all | solution.py:82
  323.2 3.5 %copy.53 = bf16[4,8,32,16,128]{4,2,1,3,0:T(8,128)(2,1)S(1)} copy(bf16[4,8,32,16,128]{4,2,0,3,1:T(8,128)(2,1)} %bitcast.34) | data formatting | bytes 8388608 | tf_op jit(solution)/shard_map/all_to_all | solution.py:82
  326.6 1.1 convert_bitcast_fusion
  327.7 2.6 copy.55
  (221 shorter events, 87.4 us)
Async XLA Ops:
  0.0 11.3 %copy-start = (s32[64]{0:T(128)S(1)}, s32[64]{0:T(128)}, u32[]{:S(2)}) copy-start(s32[64]{0:T(128)} %param.5) | copy-start | bytes 772
  0.0 12.0 %copy-start.1 = (s32[1,4]{1,0:T(1,128)S(1)}, s32[1,4]{1,0:T(1,128)}, u32[]{:S(2)}) copy-start(s32[1,4]{1,0:T(1,128)} %param.6) | copy-start | bytes 52
  0.0 39.1 %all-to-all-start = ((bf16[64,16,512]{2,1,0:T(8,128)(2,1)}), bf16[64,16,512]{2,1,0:T(8,128)(2,1)S(1)}, u32[]{:S(2)}, u32[]{:S(2)}) async-start(bf16[64,16,512]{2,1,0:T(8,128)(2,1)} %param.4), calls=%async_computation | async-start | bytes 2097152 | tf_op jit(solution)/shard_map/all_to_all | solution.py:49
  128.6 24.6 %all-to-all-start.1 = ((bf16[8,2,16384]{2,1,0:T(2,128)(2,1)}), bf16[8,2,16384]{2,1,0:T(2,128)(2,1)S(1)}, u32[]{:S(2)}, u32[]{:S(2)}) async-start(bf16[8,2,16384]{2,1,0:T(2,128)(2,1)} %reshape.421), calls=%async_computation.1 | async-start | bytes 1048576 | tf_op jit(solution)/shard_map/all_to_all | solution.py:55
  157.7 12.7 %collective-permute-start = (bf16[2,16,128,64]{2,3,0,1:T(8,128)(2,1)S(1)}, bf16[2,16,128,64]{2,3,0,1:T(8,128)(2,1)}, u32[]{:S(2)}, u32[]{:S(2)}) collective-permute-start(bf16[2,16,128,64]{2,3,0,1:T(8,128)(2,1)S(1)} %multiply_convert_fusion.1), channel_id=1, source_target_pairs={{8,0},{16,8},{24,16},{32,24},{40,32},{48,40},{56,48},{64,56},{72,6... | collective-permute-start | bytes 1572872 | tf_op jit(solution)/shard_map/ppermute | solution.py:22
  159.7 30.0 %collective-permute-start.1 = (bf16[2,16,128,64]{2,3,0,1:T(8,128)(2,1)S(1)}, bf16[2,16,128,64]{2,3,0,1:T(8,128)(2,1)}, u32[]{:S(2)}, u32[]{:S(2)}) collective-permute-start(bf16[2,16,128,64]{2,3,0,1:T(8,128)(2,1)S(1)} %multiply_convert_fusion.1), channel_id=1, source_target_pairs={{16,0},{24,8},{32,16},{40,24},{48,32},{56,40},{64,48},{72,56},{80,... | collective-permute-start | bytes 1572872 | tf_op jit(solution)/shard_map/ppermute | solution.py:22
  165.1 29.3 %collective-permute-start.2 = (bf16[2,16,128,64]{2,3,0,1:T(8,128)(2,1)S(1)}, bf16[2,16,128,64]{2,3,0,1:T(8,128)(2,1)}, u32[]{:S(2)}, u32[]{:S(2)}) collective-permute-start(bf16[2,16,128,64]{2,3,0,1:T(8,128)(2,1)S(1)} %multiply_convert_fusion.1), channel_id=1, source_target_pairs={{24,0},{32,8},{40,16},{48,24},{56,32},{64,40},{72,48},{80,56},{88,... | collective-permute-start | bytes 1572872 | tf_op jit(solution)/shard_map/ppermute | solution.py:22
  222.5 100.7 %all-to-all-start.2 = ((bf16[4,32,128,128]{3,1,0,2:T(8,128)(2,1)}), bf16[4,32,128,128]{3,1,0,2:T(8,128)(2,1)}, u32[]{:S(2)}, u32[]{:S(2)}) async-start(bf16[4,32,128,128]{3,1,0,2:T(8,128)(2,1)} %multiply_convert_fusion), calls=%async_computation.2 | async-start | bytes 8388608 | tf_op jit(solution)/shard_map/all_to_all | solution.py:82
where the time goes:
time: 332 us; the launch traced here: 330 us
  waiting for transfers between devices  156 us (47%)
  local copies, waits for them, and re-layouts  112 us (34%)
  starting transfers between devices  39.3 us (12%)
  other arithmetic  18.4 us (6%)
    all_to_all x1, waiting for transfers between devices, local(): lax.all_to_all(cross, 'band', split_axis=2, concat_axis=1, tiled=True)  91 us
    gather x192, local copies, waits for them, and re-layouts  86.6 us
    all_to_all x1, waiting for transfers between devices, local(): lax.all_to_all(traces, 'chan', split_axis=0, concat_axis=2, tiled=True)  27 us
    ppermute x3, waiting for transfers between devices, passed_along(): return lax.ppermute(block, axis, route)  23.9 us
    all_to_all x1, waiting for transfers between devices, local(): lax.all_to_all(spectra, 'band', split_axis=0, concat_axis=1, tiled=True)  14.3 us
    all_to_all x1, starting transfers between devices, local(): lax.all_to_all(traces, 'chan', split_axis=0, concat_axis=2, tiled=True)  10.6 us
    another operation x1, local copies, waits for them, and re-layouts, local(): jnp.stack([real_part, imag_part], axis=1) / count_win * keep[:, None, None]  10.3 us
    all_to_all x1, starting transfers between devices, local(): lax.all_to_all(spectra, 'band', split_axis=0, concat_axis=1, tiled=True)  9.97 us
  transfers between devices with their start and end apart: 6, of which 5 were waited for; matrix products, arithmetic and copies ran while one was open for 1% of the time, Pallas kernels for 0%

commit v1 on v0

v1 whole, which is shorter than its diff:
```python
import math

import jax
import jax.numpy as jnp
import numpy as np
from jax import lax
from jax.experimental import pallas as pl
from jax.experimental.pallas import tpu as pltpu
from jax.sharding import PartitionSpec as P

CB = 128
RANGE = 300
WIN = 256
HALF = WIN // 2
LAGS = 201
NWIN = 64
TMAX = 4
LANES = 128
LAG_ROWS = 208
EPS = 1e-06
MIB = 1 << 20


def tables(bands):
    f32 = np.float32
    turn = f32(2.0 * math.pi)
    times = np.arange(WIN)
    bins = np.arange(HALF)
    hann = f32(0.5) - f32(0.5) * np.cos(turn * times.astype(f32) / f32(WIN))
    phase = turn * (times[:, None] * bins[None, :] % WIN).astype(f32) / f32(WIN)
    forward = np.concatenate([hann[:, None] * np.cos(phase), -hann[:, None] * np.sin(phase)], axis=1)
    shifts = np.arange(LAGS) - (LAGS - 1) // 2
    angle = turn * (bins[:, None] * shifts[None, :] % WIN).astype(f32) / f32(WIN)
    factor = np.where(bins == 0, 1.0, 2.0).astype(f32)[:, None]
    inverse = np.stack([factor * np.cos(angle), -factor * np.sin(angle)], axis=0)
    width = HALF // bands
    inverse = inverse.reshape(2, bands, width, LAGS).transpose(1, 0, 2, 3).reshape(WIN, LAGS)
    inverse = np.pad(inverse.T, ((0, LAG_ROWS - LAGS), (0, 0)))
    return (
        jnp.asarray(forward.T.astype(jnp.bfloat16)),
        jnp.asarray(inverse.astype(jnp.bfloat16)),
    )


NT = (((1,), (1,)), ((), ()))
NN = (((1,), (0,)), ((), ()))


def dot(a, b, dims):
    return lax.dot_general(a, b, dims, preferred_element_type=jnp.float32)


def spectra_kernel(starts, traces, forward, out, seg0, seg1, white):
    rows, samples = traces.shape[1], traces.shape[2]
    chunks = samples // LANES
    last = traces.shape[0] * chunks - 1
    lane = lax.broadcasted_iota(jnp.int32, (rows, LANES), 1)

    def cut(w, carry):
        begin = starts[w]
        first = begin // LANES
        shift = begin % LANES

        def chunk(index):
            index = jnp.minimum(index, last)
            at = pl.multiple_of((index % chunks) * LANES, LANES)
            piece = traces[index // chunks, :, pl.ds(at, LANES)].astype(jnp.float32)
            return pltpu.roll(piece, (LANES - shift) % LANES, 1)

        a, b, c = chunk(first), chunk(first + 1), chunk(first + 2)
        inside = lane < LANES - shift
        seg0[pl.ds(w, rows, stride=NWIN), :] = jnp.where(inside, a, b)
        seg1[pl.ds(w, rows, stride=NWIN), :] = jnp.where(inside, b, c)
        return carry

    lax.fori_loop(0, NWIN, cut, 0, unroll=4)
    real_lane = lax.broadcasted_iota(jnp.int32, (HALF, 2 * LANES), 1) % LANES < NWIN

    def transform(pair, carry):
        at = pl.multiple_of(pair * LANES, LANES)
        both = jnp.concatenate([seg0[pl.ds(at, LANES), :], seg1[pl.ds(at, LANES), :]], axis=1)
        both = both.astype(jnp.bfloat16).reshape(2, NWIN, WIN)
        twice = jnp.concatenate([both, both], axis=1).reshape(4 * NWIN, WIN)
        result = dot(forward[...], twice, NT)
        spectra = jnp.where(real_lane, result[:HALF], result[HALF:])
        spectra = spectra.astype(jnp.bfloat16).astype(jnp.float32)
        for half in range(2):
            mine = spectra[:, half * LANES : (half + 1) * LANES]
            power = jnp.sum(mine * mine, axis=1, keepdims=True) * (1.0 / NWIN)
            white[pl.ds(2 * pair + half, HALF, stride=rows), :] = mine * lax.rsqrt(power + EPS)
        return carry

    lax.fori_loop(0, rows // 2, transform, 0)
    out[...] = white[...].astype(jnp.bfloat16).reshape(out.shape)


def whitened_rows(starts, series, forward, bands):
    rows = series.shape[1]
    width = HALF // bands
    return pl.pallas_call(
        spectra_kernel,
        out_shape=jax.ShapeDtypeStruct((bands, width, rows, LANES), jnp.bfloat16),
        in_specs=[
            pl.BlockSpec(memory_space=pltpu.SMEM),
            pl.BlockSpec(memory_space=pltpu.VMEM),
            pl.BlockSpec(memory_space=pltpu.VMEM),
        ],
        out_specs=pl.BlockSpec(memory_space=pltpu.VMEM),
        scratch_shapes=[
            pltpu.VMEM((rows * NWIN, LANES), jnp.float32),
            pltpu.VMEM((rows * NWIN, LANES), jnp.float32),
            pltpu.VMEM((HALF * rows, LANES), jnp.float32),
        ],
        compiler_params=pltpu.CompilerParams(vmem_limit_bytes=16 * MIB),
    )(starts, series, forward)


def both_sides(own, f):
    mine = own[:, f].reshape(CB, LANES)
    wide = mine.astype(jnp.float32)
    lane = lax.broadcasted_iota(jnp.int32, (CB, LANES), 1)
    turned = pltpu.roll(wide, NWIN, 1)
    turned = jnp.where(lane < NWIN, -turned, turned).astype(jnp.bfloat16)
    return mine, jnp.concatenate([mine, turned], axis=0)


def near_kernel(own, next1, out, held):
    bands, width, rows = own.shape[:3]

    def one(f, carry):
        mine, sides = both_sides(own, f)
        result = dot(sides, next1[:, f].reshape(CB, LANES), NT) * (1.0 / NWIN)
        held[pl.ds(f, CB, stride=2 * width), :] = result[:CB]
        held[pl.ds(width + f, CB, stride=2 * width), :] = result[CB:]
        return carry

    lax.fori_loop(0, width, one, 0)
    out[...] = held[...].astype(jnp.bfloat16).reshape(out.shape)


def far_kernel(own, next2, next3, out, held0, held1):
    bands, width, rows = own.shape[:3]
    half = rows // 2
    tail = next3.shape[0]
    step = 2 * width
    row_index = lax.broadcasted_iota(jnp.int32, (CB, LANES), 0)
    column = lax.broadcasted_iota(jnp.int32, (CB, LANES), 1)
    after = column > row_index
    left = lax.broadcasted_iota(jnp.int32, (bands, half, LANES), 2) < LANES // 2
    blank = jnp.zeros((CB // 2 - tail * rows, LANES), jnp.bfloat16)

    def one(f, carry):
        mine, sides = both_sides(own, f)
        second = next2[:, f].reshape(CB, LANES)
        low = second[: CB // 2]
        third = next3[:, f].reshape(tail * rows, LANES)
        mixed = jnp.concatenate([mine, second[CB // 2 :], third, blank, low, low], axis=0)
        result = dot(sides, mixed, NT) * (1.0 / NWIN)
        for part in range(2):
            of = result[part * CB : (part + 1) * CB]
            shared = jnp.where(after, of[:, :CB], of[:, CB : 2 * CB])
            split = of[:, 2 * CB :].reshape(bands, 2, half, LANES)
            folded = jnp.where(left, split[:, 0], split[:, 1]).reshape(bands * half, LANES)
            held0[pl.ds(part * width + f, CB, stride=step), :] = shared
            held1[pl.ds(part * width + f, CB // 2, stride=step), :] = folded
        return carry

    lax.fori_loop(0, width, one, 0)
    out[:, :rows] = held0[...].astype(jnp.bfloat16).reshape(bands, rows, step, LANES)
    out[:, rows:] = held1[...].astype(jnp.bfloat16).reshape(bands, half, step, LANES)


def vmem_call(kernel, out_shape, scratch, limit, *args):
    return pl.pallas_call(
        kernel,
        out_shape=jax.ShapeDtypeStruct(out_shape, jnp.bfloat16),
        in_specs=[pl.BlockSpec(memory_space=pltpu.VMEM)] * len(args),
        out_specs=pl.BlockSpec(memory_space=pltpu.VMEM),
        scratch_shapes=[pltpu.VMEM(shape, jnp.float32) for shape in scratch],
        compiler_params=pltpu.CompilerParams(vmem_limit_bytes=limit),
    )(*args)


def lag_kernel(info, near, far, inverse, out, held):
    bands, rows, step = near.shape[:3]
    half = rows // 2
    depth = bands * step
    first = info[2 * TMAX]
    column = lax.broadcasted_iota(jnp.int32, (LAG_ROWS, LANES), 1)
    table = inverse[...]

    def put(offset, row, value):
        held[info[offset], pl.ds(row, LAGS, stride=rows), :] = value[:LAGS]

    def one(low_row, carry):
        high_row = low_row + half
        pieces = [
            near[:, low_row],
            near[:, high_row],
            far[:, low_row],
            far[:, high_row],
            far[:, rows + low_row],
        ]
        pieces = [piece.reshape(depth, LANES) for piece in pieces]
        near_pair = dot(table, jnp.concatenate(pieces[:2], axis=1), NN)
        shared_pair = dot(table, jnp.concatenate(pieces[2:4], axis=1), NN)
        folded = dot(table, pieces[4], NN)
        for k, row in enumerate((low_row, high_row)):
            put(1, row, near_pair[:, k * LANES : (k + 1) * LANES])
            shared = shared_pair[:, k * LANES : (k + 1) * LANES]
            i = first + row
            put(0, row, jnp.where(column > i, shared, 0.0))
            turned = pltpu.roll(shared, LANES // 2, 1)
            lower = folded if k == 0 else pltpu.roll(folded, LANES // 2, 1)
            joined = jnp.where(column < LANES // 2, lower, turned)
            put(2, row, jnp.where(column <= i + RANGE - 2 * CB, joined, 0.0))
            put(3, row, jnp.where(column <= i + RANGE - 3 * CB, turned, 0.0))
        return carry

    lax.fori_loop(0, half, one, 0)
    for slot in range(TMAX):
        live = info[TMAX + slot] > 0

        @pl.when(live)
        def _():
            out[slot] = held[slot].astype(jnp.bfloat16).reshape(LAGS, rows, LANES)

        @pl.when(jnp.logical_not(live))
        def _():
            out[slot] = jnp.zeros((LAGS, rows, LANES), jnp.bfloat16)


def lags(info, near, far, inverse):
    rows = near.shape[1]
    return pl.pallas_call(
        lag_kernel,
        out_shape=jax.ShapeDtypeStruct((TMAX, LAGS, rows, LANES), jnp.bfloat16),
        in_specs=[pl.BlockSpec(memory_space=pltpu.SMEM)]
        + [pl.BlockSpec(memory_space=pltpu.VMEM)] * 3,
        out_specs=pl.BlockSpec(memory_space=pltpu.VMEM),
        scratch_shapes=[pltpu.VMEM((TMAX + 1, LAGS * rows, LANES), jnp.float32)],
        compiler_params=pltpu.CompilerParams(vmem_limit_bytes=32 * MIB),
    )(info, near, far, inverse)


def passed_along(block, axis, distance):
    devices = range(lax.axis_size(axis))
    route = [(i - distance, i) for i in devices if i - distance in devices]
    return lax.ppermute(block, axis, route)


def exchanged(block, axis):
    return lax.all_to_all(block, axis, split_axis=0, concat_axis=0, tiled=True)


def local(traces, window_starts, tile_offsets, tile_count):
    bands = lax.axis_size("band")
    rows = CB // bands
    width = HALF // bands
    forward, inverse = tables(bands)
    series = exchanged(traces, "chan")
    own = exchanged(whitened_rows(window_starts, series, forward, bands), "band")
    next1 = passed_along(own, "chan", -1)
    next2 = passed_along(own, "chan", -2)
    reach = -(-(RANGE - 2 * CB) // rows)
    next3 = passed_along(own[:reach], "chan", -3)
    tile = (bands, rows, 2 * width, LANES)
    near = vmem_call(near_kernel, tile, [(CB * 2 * width, LANES)], 16 * MIB, own, next1)
    near = exchanged(near, "band")
    far = vmem_call(
        far_kernel,
        (bands, rows + rows // 2, 2 * width, LANES),
        [(CB * 2 * width, LANES), (CB // 2 * 2 * width, LANES)],
        24 * MIB,
        own,
        next2,
        next3,
    )
    far = exchanged(far, "band")
    live = jnp.arange(TMAX) < tile_count[0]
    holds = (tile_offsets[0][None, :] == jnp.arange(TMAX)[:, None]) & live[None, :]
    slot_of = jnp.where(holds.any(axis=1), jnp.argmax(holds, axis=1), TMAX)
    first = (lax.axis_index("band") * rows)[None]
    info = jnp.concatenate([slot_of, live, first]).astype(jnp.int32)
    result = lags(info, near, far, inverse)
    return result.transpose(0, 2, 3, 1)[None]


def solution(mesh):
    placed = (P(None, "band", "chan"), P(), P("chan", None), P("chan"))
    return jax.shard_map(
        local,
        mesh=mesh,
        in_specs=placed,
        out_specs=P("chan", None, "band", None, None),
        check_vma=False,
    )
```

time: 332 us -> 177 us (0.53)
  the two profiles are of different devices: /device:TPU:80 before, /device:TPU:17 now
where the time goes in v1:
time: 177 us; the launch traced here: 176 us
  waiting for transfers between devices  62.8 us (35%)
  blocking collectives  61.9 us (35%)
  Pallas kernels  27.1 us (15%)
  starting transfers between devices  22.9 us (13%)
    all_to_all x2, blocking collectives, exchanged(): return lax.all_to_all(block, axis, split_axis=0, concat_axis=0, tiled=True)  61.9 us
    all_to_all x2, waiting for transfers between devices, exchanged(): return lax.all_to_all(block, axis, split_axis=0, concat_axis=0, tiled=True)  39.1 us
    ppermute x3, waiting for transfers between devices, passed_along(): return lax.ppermute(block, axis, route)  23.6 us
    pallas_call x2, Pallas kernels, vmem_call(): pl.pallas_call(kernel, out_shape=jax.ShapeDtypeStruct(out_shape, jnp.bflo...  12.7 us
    ppermute x3, starting transfers between devices, passed_along(): return lax.ppermute(block, axis, route)  12.5 us
    all_to_all x2, starting transfers between devices, exchanged(): return lax.all_to_all(block, axis, split_axis=0, concat_axis=0, tiled=True)  10.4 us
    pallas_call x1, Pallas kernels, lags(): pl.pallas_call(lag_kernel, out_shape=jax.ShapeDtypeStruct((TMAX, LAGS, ro...  7.69 us
    pallas_call x1, Pallas kernels, whitened_rows(): pl.pallas_call(spectra_kernel, out_shape=jax.ShapeDtypeStruct((bands, wid...  6.72 us
  transfers between devices with their start and end apart: 5, of which 4 were waited for; matrix products, arithmetic and copies ran while one was open for 0% of the time, Pallas kernels for 4%

profile of v1, /device:TPU:17, one launch (start us, length us, event | category | flops | bytes accessed | tf_op | source)
XLA Modules:
  0.0 176.3 jit_solution(15778860961220226854)
XLA Ops:
  0.0 0.0 copy-start
  0.0 0.0 copy-start.2
  0.0 37.6 %all_to_all.20.traces = bf16[64,16,512]{2,1,0:T(8,128)(2,1)S(1)} all-to-all(bf16[64,16,512]{2,1,0:T(8,128)(2,1)} %param.6), channel_id=1, replica_groups=mesh['chan'=64,'band'=8] {'chan'}, dimensions={0} | all-to-all | bytes 2097152 | tf_op jit(solution)/shard_map/all_to_all | solution.py:253
  37.6 0.0 copy-done
  37.6 0.0 copy-done.2
  37.6 6.7 %shard_map.64 = bf16[8,16,16,128]{3,2,1,0:T(8,128)(2,1)S(1)} custom-call(s32[64]{0:T(128)S(1)} %copy-done.2, bf16[64,16,512]{2,1,0:T(8,128)(2,1)S(1)} %all_to_all.20.traces, bf16[256,256]{1,0:T(8,128)(2,1)S(1)} %copy-done), custom_call_target="tpu_custom_call" | custom-call | tf_op jit(solution)/shard_map/pallas_call | solution.py:100
  44.4 24.3 %all_to_all.21.own = bf16[8,16,16,128]{3,2,1,0:T(8,128)(2,1)S(1)} all-to-all(bf16[8,16,16,128]{3,2,1,0:T(8,128)(2,1)S(1)} %shard_map.64), channel_id=1, replica_groups=mesh['chan'=64,'band'=8] {'band'}, dimensions={0} | all-to-all | bytes 1048576 | tf_op jit(solution)/shard_map/all_to_all | solution.py:253
  68.6 5.9 %collective-permute-start = (bf16[8,16,16,128]{3,2,1,0:T(8,128)(2,1)S(1)}, bf16[8,16,16,128]{3,2,1,0:T(8,128)(2,1)S(1)}, u32[]{:S(2)}, u32[]{:S(2)}) collective-permute-start(bf16[8,16,16,128]{3,2,1,0:T(8,128)(2,1)S(1)} %all_to_all.21.own), channel_id=1, source_target_pairs={{8,0},{16,8},{24,16},{32,24},{40,32},{48,40},{56,48},{64,56},{72,6... | collective-permute-start | bytes 1572872 | tf_op jit(solution)/shard_map/ppermute | solution.py:249
  74.5 8.5 %collective-permute-done.next1 = bf16[8,16,16,128]{3,2,1,0:T(8,128)(2,1)S(1)} collective-permute-done((bf16[8,16,16,128]{3,2,1,0:T(8,128)(2,1)S(1)}, bf16[8,16,16,128]{3,2,1,0:T(8,128)(2,1)S(1)}, u32[]{:S(2)}, u32[]{:S(2)}) %collective-permute-start) | collective-permute-done | bytes 524320 | tf_op jit(solution)/shard_map/ppermute | solution.py:249
  83.0 5.8 %shard_map.65 = bf16[8,16,32,128]{3,2,1,0:T(8,128)(2,1)} custom-call(bf16[8,16,16,128]{3,2,1,0:T(8,128)(2,1)S(1)} %all_to_all.21.own, bf16[8,16,16,128]{3,2,1,0:T(8,128)(2,1)S(1)} %collective-permute-done.next1), custom_call_target="tpu_custom_call" | custom-call | tf_op jit(solution)/shard_map/pallas_call | solution.py:174
  88.8 3.6 %all-to-all-start.2 = ((bf16[8,16,32,128]{3,2,1,0:T(8,128)(2,1)}), bf16[8,16,32,128]{3,2,1,0:T(8,128)(2,1)S(1)}, u32[]{:S(2)}, u32[]{:S(2)}) async-start(bf16[8,16,32,128]{3,2,1,0:T(8,128)(2,1)} %shard_map.65), calls=%async_computation.2 | async-start | bytes 2097152 | tf_op jit(solution)/shard_map/all_to_all | solution.py:253
  92.4 4.7 %collective-permute-start.1 = (bf16[8,16,16,128]{3,2,1,0:T(8,128)(2,1)S(1)}, bf16[8,16,16,128]{3,2,1,0:T(8,128)(2,1)S(1)}, u32[]{:S(2)}, u32[]{:S(2)}) collective-permute-start(bf16[8,16,16,128]{3,2,1,0:T(8,128)(2,1)S(1)} %all_to_all.21.own), channel_id=1, source_target_pairs={{16,0},{24,8},{32,16},{40,24},{48,32},{56,40},{64,48},{72,56},{80,... | collective-permute-start | bytes 1572872 | tf_op jit(solution)/shard_map/ppermute | solution.py:249
  97.1 1.9 %collective-permute-start.2 = (bf16[3,16,16,128]{3,2,1,0:T(8,128)(2,1)S(1)}, bf16[3,16,16,128]{3,2,1,0:T(8,128)(2,1)S(1)}, u32[]{:S(2)}, u32[]{:S(2)}) collective-permute-start(bf16[3,16,16,128]{3,2,1,0:T(8,128)(2,1)S(1)} %slice.4), channel_id=1, source_target_pairs={{24,0},{32,8},{40,16},{48,24},{56,32},{64,40},{72,48},{80,56},{88,... | collective-permute-start | bytes 589832 | tf_op jit(solution)/shard_map/ppermute | solution.py:249
  99.1 15.1 %collective-permute-done.2.next3 = bf16[3,16,16,128]{3,2,1,0:T(8,128)(2,1)S(1)} collective-permute-done((bf16[3,16,16,128]{3,2,1,0:T(8,128)(2,1)S(1)}, bf16[3,16,16,128]{3,2,1,0:T(8,128)(2,1)S(1)}, u32[]{:S(2)}, u32[]{:S(2)}) %collective-permute-start.2) | collective-permute-done | bytes 196640 | tf_op jit(solution)/shard_map/ppermute | solution.py:249
  114.2 0.0 collective-permute-done.1.next2
  114.2 6.9 %shard_map.66 = bf16[8,24,32,128]{3,2,1,0:T(8,128)(2,1)} custom-call(bf16[8,16,16,128]{3,2,1,0:T(8,128)(2,1)S(1)} %all_to_all.21.own, bf16[8,16,16,128]{3,2,1,0:T(8,128)(2,1)S(1)} %collective-permute-done.1.next2, bf16[3,16,16,128]{3,2,1,0:T(8,128)(2,1)S(1)} %collective-permute-done.2.next3), custom_call_target="tpu_custom_call" | custom-call | tf_op jit(solution)/shard_map/pallas_call | solution.py:174
  121.1 0.0 copy-start.3
  121.1 0.0 copy-start.1
  121.1 0.2 all-to-all-done.2.near
  121.3 6.8 %all-to-all-start.3 = ((bf16[8,24,32,128]{3,2,1,0:T(8,128)(2,1)}), bf16[8,24,32,128]{3,2,1,0:T(8,128)(2,1)S(1)}, u32[]{:S(2)}, u32[]{:S(2)}) async-start(bf16[8,24,32,128]{3,2,1,0:T(8,128)(2,1)} %shard_map.66), calls=%async_computation.3 | async-start | bytes 3145728 | tf_op jit(solution)/shard_map/all_to_all | solution.py:253
  128.8 0.0 copy-done.3
  128.8 0.1 fusion.1
  128.9 0.6 iota_reduce_fusion
  129.5 0.1 pad_add_fusion.info
  129.6 39.0 %all-to-all-done.3.far = bf16[8,24,32,128]{3,2,1,0:T(8,128)(2,1)S(1)} async-done(((bf16[8,24,32,128]{3,2,1,0:T(8,128)(2,1)}), bf16[8,24,32,128]{3,2,1,0:T(8,128)(2,1)S(1)}, u32[]{:S(2)}, u32[]{:S(2)}) %all-to-all-start.3) | async-done | bytes 1572896 | tf_op jit(solution)/shard_map/all_to_all | solution.py:253
  168.6 0.0 copy-done.1
  168.6 7.7 %shard_map.67 = bf16[4,201,16,128]{3,2,1,0:T(8,128)(2,1)} custom-call(s32[9]{0:T(128)S(1)} %pad_add_fusion.info, bf16[8,16,32,128]{3,2,1,0:T(8,128)(2,1)S(1)} %all-to-all-done.2.near, bf16[8,24,32,128]{3,2,1,0:T(8,128)(2,1)S(1)} %all-to-all-done.3.far, bf16[208,256]{1,0:T(8,128)(2,1)S(1)} %copy-done.1), custom_call_target="tpu_custom_call" | custom-call | tf_op jit(solution)/shard_map/pallas_call | solution.py:235
  (4 shorter events, 0.0 us)
Async XLA Ops:
  0.0 37.6 %copy-start = (bf16[256,256]{1,0:T(8,128)(2,1)S(1)}, bf16[256,256]{1,0:T(8,128)(2,1)}, u32[]{:S(2)}) copy-start(bf16[256,256]{1,0:T(8,128)(2,1)} %constant.19.clone.forward) | copy-start | bytes 393220
  0.0 37.6 %copy-start.2 = (s32[64]{0:T(128)S(1)}, s32[64]{0:T(128)}, u32[]{:S(2)}) copy-start(s32[64]{0:T(128)} %starts.1) | copy-start | bytes 772
  68.6 14.4 %collective-permute-start = (bf16[8,16,16,128]{3,2,1,0:T(8,128)(2,1)S(1)}, bf16[8,16,16,128]{3,2,1,0:T(8,128)(2,1)S(1)}, u32[]{:S(2)}, u32[]{:S(2)}) collective-permute-start(bf16[8,16,16,128]{3,2,1,0:T(8,128)(2,1)S(1)} %all_to_all.21.own), channel_id=1, source_target_pairs={{8,0},{16,8},{24,16},{32,24},{40,32},{48,40},{56,48},{64,56},{72,6... | collective-permute-start | bytes 1572872 | tf_op jit(solution)/shard_map/ppermute | solution.py:249
  88.8 32.4 %all-to-all-start.2 = ((bf16[8,16,32,128]{3,2,1,0:T(8,128)(2,1)}), bf16[8,16,32,128]{3,2,1,0:T(8,128)(2,1)S(1)}, u32[]{:S(2)}, u32[]{:S(2)}) async-start(bf16[8,16,32,128]{3,2,1,0:T(8,128)(2,1)} %shard_map.65), calls=%async_computation.2 | async-start | bytes 2097152 | tf_op jit(solution)/shard_map/all_to_all | solution.py:253
  92.4 21.8 %collective-permute-start.1 = (bf16[8,16,16,128]{3,2,1,0:T(8,128)(2,1)S(1)}, bf16[8,16,16,128]{3,2,1,0:T(8,128)(2,1)S(1)}, u32[]{:S(2)}, u32[]{:S(2)}) collective-permute-start(bf16[8,16,16,128]{3,2,1,0:T(8,128)(2,1)S(1)} %all_to_all.21.own), channel_id=1, source_target_pairs={{16,0},{24,8},{32,16},{40,24},{48,32},{56,40},{64,48},{72,56},{80,... | collective-permute-start | bytes 1572872 | tf_op jit(solution)/shard_map/ppermute | solution.py:249
  97.1 17.1 %collective-permute-start.2 = (bf16[3,16,16,128]{3,2,1,0:T(8,128)(2,1)S(1)}, bf16[3,16,16,128]{3,2,1,0:T(8,128)(2,1)S(1)}, u32[]{:S(2)}, u32[]{:S(2)}) collective-permute-start(bf16[3,16,16,128]{3,2,1,0:T(8,128)(2,1)S(1)} %slice.4), channel_id=1, source_target_pairs={{24,0},{32,8},{40,16},{48,24},{56,32},{64,40},{72,48},{80,56},{88,... | collective-permute-start | bytes 589832 | tf_op jit(solution)/shard_map/ppermute | solution.py:249
  121.1 7.7 %copy-start.3 = (s32[1,4]{1,0:T(1,128)S(1)}, s32[1,4]{1,0:T(1,128)}, u32[]{:S(2)}) copy-start(s32[1,4]{1,0:T(1,128)} %param.8) | copy-start | bytes 52
  121.1 47.5 %copy-start.1 = (bf16[208,256]{1,0:T(8,128)(2,1)S(1)}, bf16[208,256]{1,0:T(8,128)(2,1)}, u32[]{:S(2)}) copy-start(bf16[208,256]{1,0:T(8,128)(2,1)} %constant.20.clone.inverse) | copy-start | bytes 319492
  121.3 47.3 %all-to-all-start.3 = ((bf16[8,24,32,128]{3,2,1,0:T(8,128)(2,1)}), bf16[8,24,32,128]{3,2,1,0:T(8,128)(2,1)S(1)}, u32[]{:S(2)}, u32[]{:S(2)}) async-start(bf16[8,24,32,128]{3,2,1,0:T(8,128)(2,1)} %shard_map.66), calls=%async_computation.3 | async-start | bytes 3145728 | tf_op jit(solution)/shard_map/all_to_all | solution.py:253

commit v2 on v1

--- a/solution.py
+++ b/solution.py
@@ -73,7 +73,7 @@
         seg1[pl.ds(w, rows, stride=NWIN), :] = jnp.where(inside, b, c)
         return carry
 
-    lax.fori_loop(0, NWIN, cut, 0, unroll=4)
+    lax.fori_loop(0, NWIN, cut, 0, unroll=True)
     real_lane = lax.broadcasted_iota(jnp.int32, (HALF, 2 * LANES), 1) % LANES < NWIN
 
     def transform(pair, carry):
@@ -90,7 +90,7 @@
             white[pl.ds(2 * pair + half, HALF, stride=rows), :] = mine * lax.rsqrt(power + EPS)
         return carry
 
-    lax.fori_loop(0, rows // 2, transform, 0)
+    lax.fori_loop(0, rows // 2, transform, 0, unroll=True)
     out[...] = white[...].astype(jnp.bfloat16).reshape(out.shape)
 
 
@@ -134,11 +134,11 @@
         held[pl.ds(width + f, CB, stride=2 * width), :] = result[CB:]
         return carry
 
-    lax.fori_loop(0, width, one, 0)
+    lax.fori_loop(0, width, one, 0, unroll=True)
     out[...] = held[...].astype(jnp.bfloat16).reshape(out.shape)
 
 
-def far_kernel(own, next2, next3, out, held0, held1):
+def far_kernel(own, next2_even, next2_odd, next3, out, held0, held1):
     bands, width, rows = own.shape[:3]
     half = rows // 2
     tail = next3.shape[0]
@@ -151,7 +151,7 @@
 
     def one(f, carry):
         mine, sides = both_sides(own, f)
-        second = next2[:, f].reshape(CB, LANES)
+        second = (next2_even[:, f] + next2_odd[:, f]).reshape(CB, LANES)
         low = second[: CB // 2]
         third = next3[:, f].reshape(tail * rows, LANES)
         mixed = jnp.concatenate([mine, second[CB // 2 :], third, blank, low, low], axis=0)
@@ -165,7 +165,7 @@
             held1[pl.ds(part * width + f, CB // 2, stride=step), :] = folded
         return carry
 
-    lax.fori_loop(0, width, one, 0)
+    lax.fori_loop(0, width, one, 0, unroll=True)
     out[:, :rows] = held0[...].astype(jnp.bfloat16).reshape(bands, rows, step, LANES)
     out[:, rows:] = held1[...].astype(jnp.bfloat16).reshape(bands, half, step, LANES)
 
@@ -181,53 +181,71 @@
     )(*args)
 
 
-def lag_kernel(info, near, far, inverse, out, held):
+def near_lag_kernel(near, inverse, out, held):
     bands, rows, step = near.shape[:3]
+    table = inverse[...]
+
+    def one(pair, carry):
+        pieces = [near[:, 2 * pair + k].reshape(bands * step, LANES) for k in range(2)]
+        result = dot(table, jnp.concatenate(pieces, axis=1), NN)
+        for k in range(2):
+            value = result[:LAGS, k * LANES : (k + 1) * LANES]
+            held[pl.ds(2 * pair + k, LAGS, stride=rows), :] = value
+        return carry
+
+    lax.fori_loop(0, rows // 2, one, 0, unroll=True)
+    out[...] = held[...].astype(jnp.bfloat16).reshape(out.shape)
+
+
+def lag_kernel(info, near, far, inverse, out, held, done, sems):
+    bands, rows, step = far.shape[0], near.shape[1], far.shape[2]
     half = rows // 2
     depth = bands * step
     first = info[2 * TMAX]
     column = lax.broadcasted_iota(jnp.int32, (LAG_ROWS, LANES), 1)
     table = inverse[...]
 
-    def put(offset, row, value):
-        held[info[offset], pl.ds(row, LAGS, stride=rows), :] = value[:LAGS]
+    def send(offset, source):
+        slot = info[offset]
+
+        @pl.when(slot < TMAX)
+        def _():
+            pltpu.make_async_copy(source, out.at[slot], sems.at[slot]).start()
+
+    send(1, near)
+    done[0] = jnp.zeros(done.shape[1:], jnp.bfloat16)
+    for slot in range(TMAX):
+
+        @pl.when(info[TMAX + slot] == 0)
+        def _():
+            pltpu.make_async_copy(done.at[0], out.at[slot], sems.at[slot]).start()
+
+    def put(place, row, value):
+        held[place, pl.ds(row, LAGS, stride=rows), :] = value[:LAGS]
 
     def one(low_row, carry):
         high_row = low_row + half
-        pieces = [
-            near[:, low_row],
-            near[:, high_row],
-            far[:, low_row],
-            far[:, high_row],
-            far[:, rows + low_row],
-        ]
+        pieces = [far[:, low_row], far[:, high_row], far[:, rows + low_row]]
         pieces = [piece.reshape(depth, LANES) for piece in pieces]
-        near_pair = dot(table, jnp.concatenate(pieces[:2], axis=1), NN)
-        shared_pair = dot(table, jnp.concatenate(pieces[2:4], axis=1), NN)
-        folded = dot(table, pieces[4], NN)
+        shared_pair = dot(table, jnp.concatenate(pieces[:2], axis=1), NN)
+        folded = dot(table, pieces[2], NN)
         for k, row in enumerate((low_row, high_row)):
-            put(1, row, near_pair[:, k * LANES : (k + 1) * LANES])
             shared = shared_pair[:, k * LANES : (k + 1) * LANES]
             i = first + row
             put(0, row, jnp.where(column > i, shared, 0.0))
             turned = pltpu.roll(shared, LANES // 2, 1)
             lower = folded if k == 0 else pltpu.roll(folded, LANES // 2, 1)
             joined = jnp.where(column < LANES // 2, lower, turned)
-            put(2, row, jnp.where(column <= i + RANGE - 2 * CB, joined, 0.0))
-            put(3, row, jnp.where(column <= i + RANGE - 3 * CB, turned, 0.0))
-        return carry
-
-    lax.fori_loop(0, half, one, 0)
+            put(1, row, jnp.where(column <= i + RANGE - 2 * CB, joined, 0.0))
+            put(2, row, jnp.where(column <= i + RANGE - 3 * CB, turned, 0.0))
+        return carry
+
+    lax.fori_loop(0, half, one, 0, unroll=True)
+    for place, offset in enumerate((0, 2, 3)):
+        done[1 + place] = held[place].astype(jnp.bfloat16).reshape(LAGS, rows, LANES)
+        send(offset, done.at[1 + place])
     for slot in range(TMAX):
-        live = info[TMAX + slot] > 0
-
-        @pl.when(live)
-        def _():
-            out[slot] = held[slot].astype(jnp.bfloat16).reshape(LAGS, rows, LANES)
-
-        @pl.when(jnp.logical_not(live))
-        def _():
-            out[slot] = jnp.zeros((LAGS, rows, LANES), jnp.bfloat16)
+        pltpu.make_async_copy(done.at[0], out.at[slot], sems.at[slot]).wait()
 
 
 def lags(info, near, far, inverse):
@@ -237,16 +255,20 @@
         out_shape=jax.ShapeDtypeStruct((TMAX, LAGS, rows, LANES), jnp.bfloat16),
         in_specs=[pl.BlockSpec(memory_space=pltpu.SMEM)]
         + [pl.BlockSpec(memory_space=pltpu.VMEM)] * 3,
-        out_specs=pl.BlockSpec(memory_space=pltpu.VMEM),
-        scratch_shapes=[pltpu.VMEM((TMAX + 1, LAGS * rows, LANES), jnp.float32)],
+        out_specs=pl.BlockSpec(memory_space=pl.ANY),
+        scratch_shapes=[
+            pltpu.VMEM((TMAX - 1, LAGS * rows, LANES), jnp.float32),
+            pltpu.VMEM((TMAX, LAGS, rows, LANES), jnp.bfloat16),
+            pltpu.SemaphoreType.DMA((TMAX,)),
+        ],
         compiler_params=pltpu.CompilerParams(vmem_limit_bytes=32 * MIB),
     )(info, near, far, inverse)
 
 
-def passed_along(block, axis, distance):
-    devices = range(lax.axis_size(axis))
-    route = [(i - distance, i) for i in devices if i - distance in devices]
-    return lax.ppermute(block, axis, route)
+def from_ahead(block, distance, parity=None):
+    count = lax.axis_size("chan")
+    route = [(i + distance, i) for i in range(count - distance) if parity is None or i % 2 == parity]
+    return lax.ppermute(block, "chan", route)
 
 
 def exchanged(block, axis):
@@ -260,20 +282,23 @@
     forward, inverse = tables(bands)
     series = exchanged(traces, "chan")
     own = exchanged(whitened_rows(window_starts, series, forward, bands), "band")
-    next1 = passed_along(own, "chan", -1)
-    next2 = passed_along(own, "chan", -2)
+    next1 = from_ahead(own, 1)
+    next2 = (from_ahead(next1, 1, 0), from_ahead(own, 2, 1))
     reach = -(-(RANGE - 2 * CB) // rows)
-    next3 = passed_along(own[:reach], "chan", -3)
+    next3 = from_ahead(own[:reach], 3)
     tile = (bands, rows, 2 * width, LANES)
     near = vmem_call(near_kernel, tile, [(CB * 2 * width, LANES)], 16 * MIB, own, next1)
     near = exchanged(near, "band")
+    near = vmem_call(
+        near_lag_kernel, (LAGS, rows, LANES), [(LAGS * rows, LANES)], 16 * MIB, near, inverse
+    )
     far = vmem_call(
         far_kernel,
         (bands, rows + rows // 2, 2 * width, LANES),
         [(CB * 2 * width, LANES), (CB // 2 * 2 * width, LANES)],
         24 * MIB,
         own,
-        next2,
+        *next2,
         next3,
     )
     far = exchanged(far, "band")

time: 177 us -> 162 us (0.915)
  the two profiles are of different devices: /device:TPU:17 before, /device:TPU:9 now
where the time goes in v2:
time: 162 us
  blocking collectives  66.3 us (41%)
  waiting for transfers between devices  59.5 us (37%)
  starting transfers between devices  18.1 us (11%)
  Pallas kernels  16.3 us (10%)
    all_to_all x2, blocking collectives, exchanged(): return lax.all_to_all(block, axis, split_axis=0, concat_axis=0, tiled=True)  66.3 us
    all_to_all x2, waiting for transfers between devices, exchanged(): return lax.all_to_all(block, axis, split_axis=0, concat_axis=0, tiled=True)  44.8 us
    ppermute x4, waiting for transfers between devices, from_ahead(): return lax.ppermute(block, 'chan', route)  14.7 us
    ppermute x4, starting transfers between devices, from_ahead(): return lax.ppermute(block, 'chan', route)  10.8 us
    pallas_call x3, Pallas kernels, vmem_call(): pl.pallas_call(kernel, out_shape=jax.ShapeDtypeStruct(out_shape, jnp.bflo...  8.33 us
    all_to_all x2, starting transfers between devices, exchanged(): return lax.all_to_all(block, axis, split_axis=0, concat_axis=0, tiled=True)  7.32 us
    pallas_call x1, Pallas kernels, lags(): pl.pallas_call(lag_kernel, out_shape=jax.ShapeDtypeStruct((TMAX, LAGS, ro...  4.07 us
    pallas_call x1, Pallas kernels, whitened_rows(): pl.pallas_call(spectra_kernel, out_shape=jax.ShapeDtypeStruct((bands, wid...  3.88 us
  transfers between devices with their start and end apart: 6, of which 4 were waited for; matrix products, arithmetic and copies ran while one was open for 1% of the time, Pallas kernels for 3%

profile of v2, /device:TPU:9, one launch (start us, length us, event | category | flops | bytes accessed | tf_op | source)
XLA Modules:
  0.0 162.0 jit_solution(13810550785721986864)
XLA Ops:
  0.0 0.0 copy-start.1
  0.0 0.0 copy-start.2
  0.0 39.0 %all_to_all.20.traces = bf16[64,16,512]{2,1,0:T(8,128)(2,1)S(1)} all-to-all(bf16[64,16,512]{2,1,0:T(8,128)(2,1)} %param.6), channel_id=1, replica_groups=mesh['chan'=64,'band'=8] {'chan'}, dimensions={0} | all-to-all | bytes 2097152 | tf_op jit(solution)/shard_map/all_to_all | solution.py:275
  39.1 0.0 copy-done.1
  39.1 0.0 copy-done.2
  39.1 3.9 %shard_map.64 = bf16[8,16,16,128]{3,2,1,0:T(8,128)(2,1)S(1)} custom-call(s32[64]{0:T(128)S(1)} %copy-done.2, bf16[64,16,512]{2,1,0:T(8,128)(2,1)S(1)} %all_to_all.20.traces, bf16[256,256]{1,0:T(8,128)(2,1)S(1)} %copy-done.1), custom_call_target="tpu_custom_call" | custom-call | tf_op jit(solution)/shard_map/pallas_call | solution.py:100
  42.9 27.3 %all_to_all.21.own = bf16[8,16,16,128]{3,2,1,0:T(8,128)(2,1)S(1)} all-to-all(bf16[8,16,16,128]{3,2,1,0:T(8,128)(2,1)S(1)} %shard_map.64), channel_id=1, replica_groups=mesh['chan'=64,'band'=8] {'band'}, dimensions={0} | all-to-all | bytes 1048576 | tf_op jit(solution)/shard_map/all_to_all | solution.py:275
  70.2 2.9 %collective-permute-start = (bf16[8,16,16,128]{3,2,1,0:T(8,128)(2,1)S(1)}, bf16[8,16,16,128]{3,2,1,0:T(8,128)(2,1)S(1)}, u32[]{:S(2)}, u32[]{:S(2)}) collective-permute-start(bf16[8,16,16,128]{3,2,1,0:T(8,128)(2,1)S(1)} %all_to_all.21.own), channel_id=1, source_target_pairs={{8,0},{16,8},{24,16},{32,24},{40,32},{48,40},{56,48},{64,56},{72,6... | collective-permute-start | bytes 1572872 | tf_op jit(solution)/shard_map/ppermute | solution.py:271
  73.1 7.6 %collective-permute-done.next1 = bf16[8,16,16,128]{3,2,1,0:T(8,128)(2,1)S(1)} collective-permute-done((bf16[8,16,16,128]{3,2,1,0:T(8,128)(2,1)S(1)}, bf16[8,16,16,128]{3,2,1,0:T(8,128)(2,1)S(1)}, u32[]{:S(2)}, u32[]{:S(2)}) %collective-permute-start) | collective-permute-done | bytes 524320 | tf_op jit(solution)/shard_map/ppermute | solution.py:271
  80.7 3.0 %shard_map.65 = bf16[8,16,32,128]{3,2,1,0:T(8,128)(2,1)} custom-call(bf16[8,16,16,128]{3,2,1,0:T(8,128)(2,1)S(1)} %all_to_all.21.own, bf16[8,16,16,128]{3,2,1,0:T(8,128)(2,1)S(1)} %collective-permute-done.next1), custom_call_target="tpu_custom_call" | custom-call | tf_op jit(solution)/shard_map/pallas_call | solution.py:174
  83.7 3.6 %all-to-all-start.2 = ((bf16[8,16,32,128]{3,2,1,0:T(8,128)(2,1)}), bf16[8,16,32,128]{3,2,1,0:T(8,128)(2,1)S(1)}, u32[]{:S(2)}, u32[]{:S(2)}) async-start(bf16[8,16,32,128]{3,2,1,0:T(8,128)(2,1)} %shard_map.65), calls=%async_computation.2 | async-start | bytes 2097152 | tf_op jit(solution)/shard_map/all_to_all | solution.py:275
  87.2 4.7 %collective-permute-start.2 = (bf16[8,16,16,128]{3,2,1,0:T(8,128)(2,1)S(1)}, bf16[8,16,16,128]{3,2,1,0:T(8,128)(2,1)S(1)}, u32[]{:S(2)}, u32[]{:S(2)}) collective-permute-start(bf16[8,16,16,128]{3,2,1,0:T(8,128)(2,1)S(1)} %all_to_all.21.own), channel_id=1, source_target_pairs={{24,8},{40,24},{56,40},{72,56},{88,72},{104,88},{120,104},{136,120... | collective-permute-start | bytes 1572872 | tf_op jit(solution)/shard_map/ppermute | solution.py:271
  91.9 1.3 collective-permute-start.1
  93.3 1.9 %collective-permute-start.3 = (bf16[3,16,16,128]{3,2,1,0:T(8,128)(2,1)S(1)}, bf16[3,16,16,128]{3,2,1,0:T(8,128)(2,1)S(1)}, u32[]{:S(2)}, u32[]{:S(2)}) collective-permute-start(bf16[3,16,16,128]{3,2,1,0:T(8,128)(2,1)S(1)} %slice.4), channel_id=1, source_target_pairs={{24,0},{32,8},{40,16},{48,24},{56,32},{64,40},{72,48},{80,56},{88,... | collective-permute-start | bytes 589832 | tf_op jit(solution)/shard_map/ppermute | solution.py:271
  95.2 7.2 %collective-permute-done.3.next3 = bf16[3,16,16,128]{3,2,1,0:T(8,128)(2,1)S(1)} collective-permute-done((bf16[3,16,16,128]{3,2,1,0:T(8,128)(2,1)S(1)}, bf16[3,16,16,128]{3,2,1,0:T(8,128)(2,1)S(1)}, u32[]{:S(2)}, u32[]{:S(2)}) %collective-permute-start.3) | collective-permute-done | bytes 196640 | tf_op jit(solution)/shard_map/ppermute | solution.py:271
  102.3 0.0 collective-permute-done.2.next2_odd
  102.4 0.0 collective-permute-done.1.next2_even
  102.4 4.6 %shard_map.67 = bf16[8,24,32,128]{3,2,1,0:T(8,128)(2,1)} custom-call(bf16[8,16,16,128]{3,2,1,0:T(8,128)(2,1)S(1)} %all_to_all.21.own, bf16[8,16,16,128]{3,2,1,0:T(8,128)(2,1)S(1)} %collective-permute-done.1.next2_even, bf16[8,16,16,128]{3,2,1,0:T(8,128)(2,1)S(1)} %collective-permute-done.2.next2_odd, bf16[3,16,16,128]{3,2,1,0:T(8,128)(2,1)S(1)} %collective-permute-done.3.next3), custom_call_target="tpu_custom_call" | custom-call | tf_op jit(solution)/shard_map/pallas_call | solution.py:174
  106.9 0.0 copy-start.3
  106.9 0.0 copy-start
  106.9 9.1 %all-to-all-done.2.near = bf16[8,16,32,128]{3,2,1,0:T(8,128)(2,1)S(1)} async-done(((bf16[8,16,32,128]{3,2,1,0:T(8,128)(2,1)}), bf16[8,16,32,128]{3,2,1,0:T(8,128)(2,1)S(1)}, u32[]{:S(2)}, u32[]{:S(2)}) %all-to-all-start.2) | async-done | bytes 1048608 | tf_op jit(solution)/shard_map/all_to_all | solution.py:275
  116.0 3.8 %all-to-all-start.3 = ((bf16[8,24,32,128]{3,2,1,0:T(8,128)(2,1)}), bf16[8,24,32,128]{3,2,1,0:T(8,128)(2,1)S(1)}, u32[]{:S(2)}, u32[]{:S(2)}) async-start(bf16[8,24,32,128]{3,2,1,0:T(8,128)(2,1)} %shard_map.67), calls=%async_computation.3 | async-start | bytes 3145728 | tf_op jit(solution)/shard_map/all_to_all | solution.py:275
  120.5 0.0 copy-done.3
  120.5 0.1 fusion.1
  120.6 0.6 iota_reduce_fusion
  121.3 0.1 pad_add_fusion.info
  121.3 0.0 copy-done
  121.3 0.8 shard_map.66.near
  122.1 35.7 %all-to-all-done.3.far = bf16[8,24,32,128]{3,2,1,0:T(8,128)(2,1)S(1)} async-done(((bf16[8,24,32,128]{3,2,1,0:T(8,128)(2,1)}), bf16[8,24,32,128]{3,2,1,0:T(8,128)(2,1)S(1)}, u32[]{:S(2)}, u32[]{:S(2)}) %all-to-all-start.3) | async-done | bytes 1572896 | tf_op jit(solution)/shard_map/all_to_all | solution.py:275
  157.8 4.1 %shard_map.68 = bf16[4,201,16,128]{3,2,1,0:T(8,128)(2,1)} custom-call(s32[9]{0:T(128)S(1)} %pad_add_fusion.info, bf16[201,16,128]{2,1,0:T(8,128)(2,1)S(1)} %shard_map.66.near, bf16[8,24,32,128]{3,2,1,0:T(8,128)(2,1)S(1)} %all-to-all-done.3.far, bf16[208,256]{1,0:T(8,128)(2,1)S(1)} %copy-done), custom_call_target="tpu_custom_call" | custom-call | tf_op jit(solution)/shard_map/pallas_call | solution.py:253
  (4 shorter events, 0.0 us)
Async XLA Ops:
  0.0 39.1 %copy-start.1 = (bf16[256,256]{1,0:T(8,128)(2,1)S(1)}, bf16[256,256]{1,0:T(8,128)(2,1)}, u32[]{:S(2)}) copy-start(bf16[256,256]{1,0:T(8,128)(2,1)} %constant.19.clone.forward) | copy-start | bytes 393220
  0.0 39.1 %copy-start.2 = (s32[64]{0:T(128)S(1)}, s32[64]{0:T(128)}, u32[]{:S(2)}) copy-start(s32[64]{0:T(128)} %starts.1) | copy-start | bytes 772
  70.2 10.5 %collective-permute-start = (bf16[8,16,16,128]{3,2,1,0:T(8,128)(2,1)S(1)}, bf16[8,16,16,128]{3,2,1,0:T(8,128)(2,1)S(1)}, u32[]{:S(2)}, u32[]{:S(2)}) collective-permute-start(bf16[8,16,16,128]{3,2,1,0:T(8,128)(2,1)S(1)} %all_to_all.21.own), channel_id=1, source_target_pairs={{8,0},{16,8},{24,16},{32,24},{40,32},{48,40},{56,48},{64,56},{72,6... | collective-permute-start | bytes 1572872 | tf_op jit(solution)/shard_map/ppermute | solution.py:271
  83.7 32.4 %all-to-all-start.2 = ((bf16[8,16,32,128]{3,2,1,0:T(8,128)(2,1)}), bf16[8,16,32,128]{3,2,1,0:T(8,128)(2,1)S(1)}, u32[]{:S(2)}, u32[]{:S(2)}) async-start(bf16[8,16,32,128]{3,2,1,0:T(8,128)(2,1)} %shard_map.65), calls=%async_computation.2 | async-start | bytes 2097152 | tf_op jit(solution)/shard_map/all_to_all | solution.py:275
  87.2 15.1 %collective-permute-start.2 = (bf16[8,16,16,128]{3,2,1,0:T(8,128)(2,1)S(1)}, bf16[8,16,16,128]{3,2,1,0:T(8,128)(2,1)S(1)}, u32[]{:S(2)}, u32[]{:S(2)}) collective-permute-start(bf16[8,16,16,128]{3,2,1,0:T(8,128)(2,1)S(1)} %all_to_all.21.own), channel_id=1, source_target_pairs={{24,8},{40,24},{56,40},{72,56},{88,72},{104,88},{120,104},{136,120... | collective-permute-start | bytes 1572872 | tf_op jit(solution)/shard_map/ppermute | solution.py:271
  91.9 10.4 %collective-permute-start.1 = (bf16[8,16,16,128]{3,2,1,0:T(8,128)(2,1)S(1)}, bf16[8,16,16,128]{3,2,1,0:T(8,128)(2,1)S(1)}, u32[]{:S(2)}, u32[]{:S(2)}) collective-permute-start(bf16[8,16,16,128]{3,2,1,0:T(8,128)(2,1)S(1)} %collective-permute-done.next1), channel_id=1, source_target_pairs={{8,0},{24,16},{40,32},{56,48},{72,64},{88,80},{104,96},{120,112},{... | collective-permute-start | bytes 1572872 | tf_op jit(solution)/shard_map/ppermute | solution.py:271
  93.3 9.1 %collective-permute-start.3 = (bf16[3,16,16,128]{3,2,1,0:T(8,128)(2,1)S(1)}, bf16[3,16,16,128]{3,2,1,0:T(8,128)(2,1)S(1)}, u32[]{:S(2)}, u32[]{:S(2)}) collective-permute-start(bf16[3,16,16,128]{3,2,1,0:T(8,128)(2,1)S(1)} %slice.4), channel_id=1, source_target_pairs={{24,0},{32,8},{40,16},{48,24},{56,32},{64,40},{72,48},{80,56},{88,... | collective-permute-start | bytes 589832 | tf_op jit(solution)/shard_map/ppermute | solution.py:271
  106.9 13.5 %copy-start.3 = (s32[1,4]{1,0:T(1,128)S(1)}, s32[1,4]{1,0:T(1,128)}, u32[]{:S(2)}) copy-start(s32[1,4]{1,0:T(1,128)} %param.8) | copy-start | bytes 52
  106.9 14.4 %copy-start = (bf16[208,256]{1,0:T(8,128)(2,1)S(1)}, bf16[208,256]{1,0:T(8,128)(2,1)}, u32[]{:S(2)}) copy-start(bf16[208,256]{1,0:T(8,128)(2,1)} %constant.20.clone.inverse) | copy-start | bytes 319492
  116.0 41.8 %all-to-all-start.3 = ((bf16[8,24,32,128]{3,2,1,0:T(8,128)(2,1)}), bf16[8,24,32,128]{3,2,1,0:T(8,128)(2,1)S(1)}, u32[]{:S(2)}, u32[]{:S(2)}) async-start(bf16[8,24,32,128]{3,2,1,0:T(8,128)(2,1)} %shard_map.67), calls=%async_computation.3 | async-start | bytes 3145728 | tf_op jit(solution)/shard_map/all_to_all | solution.py:275

commit v3 on v2

--- a/solution.py
+++ b/solution.py
@@ -17,6 +17,9 @@
 TMAX = 4
 LANES = 128
 LAG_ROWS = 208
+PACK = 304
+LOW = PACK - 2 * CB
+UNITS = 6
 EPS = 1e-06
 MIB = 1 << 20
 
@@ -52,22 +55,25 @@
 
 def spectra_kernel(starts, traces, forward, out, seg0, seg1, white):
     rows, samples = traces.shape[1], traces.shape[2]
+    log_lanes = LANES.bit_length() - 1
     chunks = samples // LANES
+    log_chunks = chunks.bit_length() - 1
     last = traces.shape[0] * chunks - 1
     lane = lax.broadcasted_iota(jnp.int32, (rows, LANES), 1)
 
     def cut(w, carry):
         begin = starts[w]
-        first = begin // LANES
-        shift = begin % LANES
+        first = lax.shift_right_logical(begin, log_lanes)
+        shift = lax.bitwise_and(begin, LANES - 1)
+        turn = lax.bitwise_and(LANES - shift, LANES - 1)
 
         def chunk(index):
-            index = jnp.minimum(index, last)
-            at = pl.multiple_of((index % chunks) * LANES, LANES)
-            piece = traces[index // chunks, :, pl.ds(at, LANES)].astype(jnp.float32)
-            return pltpu.roll(piece, (LANES - shift) % LANES, 1)
-
-        a, b, c = chunk(first), chunk(first + 1), chunk(first + 2)
+            at = pl.multiple_of(lax.bitwise_and(index, chunks - 1) * LANES, LANES)
+            shard = lax.shift_right_logical(index, log_chunks)
+            piece = traces[shard, :, pl.ds(at, LANES)].astype(jnp.float32)
+            return pltpu.roll(piece, turn, 1)
+
+        a, b, c = chunk(first), chunk(first + 1), chunk(jnp.minimum(first + 2, last))
         inside = lane < LANES - shift
         seg0[pl.ds(w, rows, stride=NWIN), :] = jnp.where(inside, a, b)
         seg1[pl.ds(w, rows, stride=NWIN), :] = jnp.where(inside, b, c)
@@ -124,50 +130,60 @@
     return mine, jnp.concatenate([mine, turned], axis=0)
 
 
-def near_kernel(own, next1, out, held):
+def near_kernel(own, next1, out):
     bands, width, rows = own.shape[:3]
 
     def one(f, carry):
         mine, sides = both_sides(own, f)
         result = dot(sides, next1[:, f].reshape(CB, LANES), NT) * (1.0 / NWIN)
-        held[pl.ds(f, CB, stride=2 * width), :] = result[:CB]
-        held[pl.ds(width + f, CB, stride=2 * width), :] = result[CB:]
+        result = result.astype(jnp.bfloat16).reshape(2, bands, rows, LANES)
+        out[:, f] = result[0]
+        out[:, width + f] = result[1]
         return carry
 
     lax.fori_loop(0, width, one, 0, unroll=True)
-    out[...] = held[...].astype(jnp.bfloat16).reshape(out.shape)
-
-
-def far_kernel(own, next2_even, next2_odd, next3, out, held0, held1):
+
+
+def far_kernel(own, next2_even, next2_odd, next3, out, held0, held1, plain, tail):
     bands, width, rows = own.shape[:3]
-    half = rows // 2
-    tail = next3.shape[0]
     step = 2 * width
     row_index = lax.broadcasted_iota(jnp.int32, (CB, LANES), 0)
     column = lax.broadcasted_iota(jnp.int32, (CB, LANES), 1)
     after = column > row_index
-    left = lax.broadcasted_iota(jnp.int32, (bands, half, LANES), 2) < LANES // 2
-    blank = jnp.zeros((CB // 2 - tail * rows, LANES), jnp.bfloat16)
+    lane = lax.broadcasted_iota(jnp.int32, (bands, LANES), 1)
 
     def one(f, carry):
         mine, sides = both_sides(own, f)
         second = (next2_even[:, f] + next2_odd[:, f]).reshape(CB, LANES)
-        low = second[: CB // 2]
-        third = next3[:, f].reshape(tail * rows, LANES)
-        mixed = jnp.concatenate([mine, second[CB // 2 :], third, blank, low, low], axis=0)
-        result = dot(sides, mixed, NT) * (1.0 / NWIN)
+        low = second[:LOW]
+        third = next3[:, f].reshape(LOW, LANES)
+        mixed = [mine, second[LOW:], third, low, low, low[:32], low, low, low[32:], low[32:]]
+        result = dot(sides, jnp.concatenate(mixed, axis=0), NT) * (1.0 / NWIN)
         for part in range(2):
             of = result[part * CB : (part + 1) * CB]
-            shared = jnp.where(after, of[:, :CB], of[:, CB : 2 * CB])
-            split = of[:, 2 * CB :].reshape(bands, 2, half, LANES)
-            folded = jnp.where(left, split[:, 0], split[:, 1]).reshape(bands * half, LANES)
-            held0[pl.ds(part * width + f, CB, stride=step), :] = shared
-            held1[pl.ds(part * width + f, CB // 2, stride=step), :] = folded
+            at = part * width + f
+            held0[pl.ds(at, CB, stride=step), :] = jnp.where(after, of[:, :CB], of[:, CB : 2 * CB])
+            base = pl.multiple_of(at * CB, CB)
+            plain[pl.ds(base, CB), :] = of[:, 2 * CB : 3 * CB]
+            tail[pl.ds(base, CB), :] = of[:, 3 * CB :]
+
+            def row(ref, r):
+                return ref[pl.ds(base + r, bands, stride=rows), :]
+
+            for unit in range(UNITS):
+                if unit < 4:
+                    last = row(plain, 12 + unit)
+                else:
+                    pair = 12 + 2 * (unit - 4)
+                    last = jnp.where(lane < LANES - 16, row(tail, pair), row(tail, pair + 1))
+                value = jnp.where(lane < 2 * LOW, row(plain, UNITS + unit), last)
+                value = jnp.where(lane < LOW, row(plain, unit), value)
+                held1[pl.ds(unit * step + at, bands, stride=UNITS * step), :] = value
         return carry
 
     lax.fori_loop(0, width, one, 0, unroll=True)
     out[:, :rows] = held0[...].astype(jnp.bfloat16).reshape(bands, rows, step, LANES)
-    out[:, rows:] = held1[...].astype(jnp.bfloat16).reshape(bands, half, step, LANES)
+    out[:, rows:] = held1[...].astype(jnp.bfloat16).reshape(bands, UNITS, step, LANES)
 
 
 def vmem_call(kernel, out_shape, scratch, limit, *args):
@@ -181,12 +197,16 @@
     )(*args)
 
 
-def near_lag_kernel(near, inverse, out, held):
-    bands, rows, step = near.shape[:3]
+def near_lag_kernel(near, inverse, out, wide, held):
+    bands, step, rows = near.shape[:3]
+    depth = bands * step
     table = inverse[...]
+    wide[...] = near[...].astype(jnp.float32).reshape(wide.shape)
 
     def one(pair, carry):
-        pieces = [near[:, 2 * pair + k].reshape(bands * step, LANES) for k in range(2)]
+        pieces = [
+            wide[pl.ds(2 * pair + k, depth, stride=rows), :].astype(jnp.bfloat16) for k in range(2)
+        ]
         result = dot(table, jnp.concatenate(pieces, axis=1), NN)
         for k in range(2):
             value = result[:LAGS, k * LANES : (k + 1) * LANES]
@@ -197,9 +217,8 @@
     out[...] = held[...].astype(jnp.bfloat16).reshape(out.shape)
 
 
-def lag_kernel(info, near, far, inverse, out, held, done, sems):
+def lag_kernel(info, near, far, inverse, out, held, low, done, sems):
     bands, rows, step = far.shape[0], near.shape[1], far.shape[2]
-    half = rows // 2
     depth = bands * step
     first = info[2 * TMAX]
     column = lax.broadcasted_iota(jnp.int32, (LAG_ROWS, LANES), 1)
@@ -220,27 +239,38 @@
         def _():
             pltpu.make_async_copy(done.at[0], out.at[slot], sems.at[slot]).start()
 
+    def piece(row):
+        return far[:, row].reshape(depth, LANES)
+
+    def paired(row):
+        both = dot(table, jnp.concatenate([piece(row), piece(row + 1)], axis=1), NN)
+        return both[:, :LANES], both[:, LANES:]
+
+    for unit in range(0, UNITS, 2):
+        low[unit], low[unit + 1] = paired(rows + unit)
+
+    def lower(row):
+        if row < UNITS:
+            return low[row]
+        if row < 2 * UNITS:
+            return pltpu.roll(low[row - UNITS], LANES - LOW, 1)
+        extra = row - 2 * UNITS
+        start = pltpu.roll(low[extra], 32, 1)
+        end = pltpu.roll(low[4 + extra // 2], 64 - 16 * (extra % 2), 1)
+        return jnp.where(column < 32, start, end)
+
     def put(place, row, value):
         held[place, pl.ds(row, LAGS, stride=rows), :] = value[:LAGS]
 
-    def one(low_row, carry):
-        high_row = low_row + half
-        pieces = [far[:, low_row], far[:, high_row], far[:, rows + low_row]]
-        pieces = [piece.reshape(depth, LANES) for piece in pieces]
-        shared_pair = dot(table, jnp.concatenate(pieces[:2], axis=1), NN)
-        folded = dot(table, pieces[2], NN)
-        for k, row in enumerate((low_row, high_row)):
-            shared = shared_pair[:, k * LANES : (k + 1) * LANES]
+    for pair in range(0, rows, 2):
+        for row, shared in zip((pair, pair + 1), paired(pair)):
             i = first + row
             put(0, row, jnp.where(column > i, shared, 0.0))
-            turned = pltpu.roll(shared, LANES // 2, 1)
-            lower = folded if k == 0 else pltpu.roll(folded, LANES // 2, 1)
-            joined = jnp.where(column < LANES // 2, lower, turned)
+            turned = pltpu.roll(shared, LOW, 1)
+            joined = jnp.where(column < LOW, lower(row), turned)
             put(1, row, jnp.where(column <= i + RANGE - 2 * CB, joined, 0.0))
             put(2, row, jnp.where(column <= i + RANGE - 3 * CB, turned, 0.0))
-        return carry
-
-    lax.fori_loop(0, half, one, 0, unroll=True)
+
     for place, offset in enumerate((0, 2, 3)):
         done[1 + place] = held[place].astype(jnp.bfloat16).reshape(LAGS, rows, LANES)
         send(offset, done.at[1 + place])
@@ -258,6 +288,7 @@
         out_specs=pl.BlockSpec(memory_space=pl.ANY),
         scratch_shapes=[
             pltpu.VMEM((TMAX - 1, LAGS * rows, LANES), jnp.float32),
+            pltpu.VMEM((UNITS, LAG_ROWS, LANES), jnp.float32),
             pltpu.VMEM((TMAX, LAGS, rows, LANES), jnp.bfloat16),
             pltpu.SemaphoreType.DMA((TMAX,)),
         ],
@@ -286,16 +317,25 @@
     next2 = (from_ahead(next1, 1, 0), from_ahead(own, 2, 1))
     reach = -(-(RANGE - 2 * CB) // rows)
     next3 = from_ahead(own[:reach], 3)
-    tile = (bands, rows, 2 * width, LANES)
-    near = vmem_call(near_kernel, tile, [(CB * 2 * width, LANES)], 16 * MIB, own, next1)
+    near = vmem_call(near_kernel, (bands, 2 * width, rows, LANES), [], 16 * MIB, own, next1)
     near = exchanged(near, "band")
     near = vmem_call(
-        near_lag_kernel, (LAGS, rows, LANES), [(LAGS * rows, LANES)], 16 * MIB, near, inverse
+        near_lag_kernel,
+        (LAGS, rows, LANES),
+        [(WIN * rows, LANES), (LAGS * rows, LANES)],
+        16 * MIB,
+        near,
+        inverse,
     )
     far = vmem_call(
         far_kernel,
-        (bands, rows + rows // 2, 2 * width, LANES),
-        [(CB * 2 * width, LANES), (CB // 2 * 2 * width, LANES)],
+        (bands, rows + UNITS, 2 * width, LANES),
+        [
+            (CB * 2 * width, LANES),
+            (bands * UNITS * 2 * width, LANES),
+            (CB * 2 * width, LANES),
+            (CB * 2 * width, LANES),
+        ],
         24 * MIB,
         own,
         *next2,

time: 162 us -> 159 us (0.981); the launches traced: 162 us -> 157 us
  waiting for transfers between devices: 59.5 us -> 55.9 us
    all_to_all x2, waiting for transfers between devices: 44.8 us -> 41.1 us  [exchanged(): return lax.all_to_all(block, axis, split_axis=0, concat_axis=0, tiled=True)]
  transfers between devices with their start and end apart: 6 -> 6, of which waited for: 4 -> 4; matrix products, arithmetic and copies ran while one was open for 1% -> 1% of each run, Pallas kernels for 3% -> 4%
where the time goes in v3:
time: 159 us; the launch traced here: 157 us
  blocking collectives  66.4 us (42%)
  waiting for transfers between devices  55.9 us (35%)
  starting transfers between devices  17.8 us (11%)
  Pallas kernels  15 us (9%)
    all_to_all x2, blocking collectives, exchanged(): return lax.all_to_all(block, axis, split_axis=0, concat_axis=0, tiled=True)  66.4 us
    all_to_all x2, waiting for transfers between devices, exchanged(): return lax.all_to_all(block, axis, split_axis=0, concat_axis=0, tiled=True)  41.1 us
    ppermute x4, waiting for transfers between devices, from_ahead(): return lax.ppermute(block, 'chan', route)  14.8 us
    ppermute x4, starting transfers between devices, from_ahead(): return lax.ppermute(block, 'chan', route)  10.6 us
    pallas_call x3, Pallas kernels, vmem_call(): pl.pallas_call(kernel, out_shape=jax.ShapeDtypeStruct(out_shape, jnp.bflo...  8.27 us
    all_to_all x2, starting transfers between devices, exchanged(): return lax.all_to_all(block, axis, split_axis=0, concat_axis=0, tiled=True)  7.13 us
    pallas_call x1, Pallas kernels, lags(): pl.pallas_call(lag_kernel, out_shape=jax.ShapeDtypeStruct((TMAX, LAGS, ro...  4.21 us
  transfers between devices with their start and end apart: 6, of which 4 were waited for; matrix products, arithmetic and copies ran while one was open for 1% of the time, Pallas kernels for 4%

profile of v3, /device:TPU:9, one launch (start us, length us, event | category | flops | bytes accessed | tf_op | source)
XLA Modules:
  0.0 156.7 jit_solution(15987019025760535731)
XLA Ops:
  0.0 0.0 copy-start.1
  0.0 0.0 copy-start.2
  0.0 39.0 %all_to_all.20.traces = bf16[64,16,512]{2,1,0:T(8,128)(2,1)S(1)} all-to-all(bf16[64,16,512]{2,1,0:T(8,128)(2,1)} %param.6), channel_id=1, replica_groups=mesh['chan'=64,'band'=8] {'chan'}, dimensions={0} | all-to-all | bytes 2097152 | tf_op jit(solution)/shard_map/all_to_all | solution.py:306
  39.1 0.0 copy-done.1
  39.1 0.0 copy-done.2
  39.1 2.5 %shard_map.64 = bf16[8,16,16,128]{3,2,1,0:T(8,128)(2,1)S(1)} custom-call(s32[64]{0:T(128)S(1)} %copy-done.2, bf16[64,16,512]{2,1,0:T(8,128)(2,1)S(1)} %all_to_all.20.traces, bf16[256,256]{1,0:T(8,128)(2,1)S(1)} %copy-done.1), custom_call_target="tpu_custom_call" | custom-call | tf_op jit(solution)/shard_map/pallas_call | solution.py:106
  41.6 27.4 %all_to_all.21.own = bf16[8,16,16,128]{3,2,1,0:T(8,128)(2,1)S(1)} all-to-all(bf16[8,16,16,128]{3,2,1,0:T(8,128)(2,1)S(1)} %shard_map.64), channel_id=1, replica_groups=mesh['chan'=64,'band'=8] {'band'}, dimensions={0} | all-to-all | bytes 1048576 | tf_op jit(solution)/shard_map/all_to_all | solution.py:306
  68.9 2.8 %collective-permute-start = (bf16[8,16,16,128]{3,2,1,0:T(8,128)(2,1)S(1)}, bf16[8,16,16,128]{3,2,1,0:T(8,128)(2,1)S(1)}, u32[]{:S(2)}, u32[]{:S(2)}) collective-permute-start(bf16[8,16,16,128]{3,2,1,0:T(8,128)(2,1)S(1)} %all_to_all.21.own), channel_id=1, source_target_pairs={{8,0},{16,8},{24,16},{32,24},{40,32},{48,40},{56,48},{64,56},{72,6... | collective-permute-start | bytes 1572872 | tf_op jit(solution)/shard_map/ppermute | solution.py:302
  71.8 7.7 %collective-permute-done.next1 = bf16[8,16,16,128]{3,2,1,0:T(8,128)(2,1)S(1)} collective-permute-done((bf16[8,16,16,128]{3,2,1,0:T(8,128)(2,1)S(1)}, bf16[8,16,16,128]{3,2,1,0:T(8,128)(2,1)S(1)}, u32[]{:S(2)}, u32[]{:S(2)}) %collective-permute-start) | collective-permute-done | bytes 524320 | tf_op jit(solution)/shard_map/ppermute | solution.py:302
  79.4 1.5 shard_map.65
  80.9 3.6 %all-to-all-start.2 = ((bf16[8,32,16,128]{3,2,1,0:T(8,128)(2,1)}), bf16[8,32,16,128]{3,2,1,0:T(8,128)(2,1)S(1)}, u32[]{:S(2)}, u32[]{:S(2)}) async-start(bf16[8,32,16,128]{3,2,1,0:T(8,128)(2,1)} %shard_map.65), calls=%async_computation.2 | async-start | bytes 2097152 | tf_op jit(solution)/shard_map/all_to_all | solution.py:306
  84.5 4.6 %collective-permute-start.2 = (bf16[8,16,16,128]{3,2,1,0:T(8,128)(2,1)S(1)}, bf16[8,16,16,128]{3,2,1,0:T(8,128)(2,1)S(1)}, u32[]{:S(2)}, u32[]{:S(2)}) collective-permute-start(bf16[8,16,16,128]{3,2,1,0:T(8,128)(2,1)S(1)} %all_to_all.21.own), channel_id=1, source_target_pairs={{24,8},{40,24},{56,40},{72,56},{88,72},{104,88},{120,104},{136,120... | collective-permute-start | bytes 1572872 | tf_op jit(solution)/shard_map/ppermute | solution.py:302
  89.0 1.3 collective-permute-start.1
  90.4 1.9 %collective-permute-start.3 = (bf16[3,16,16,128]{3,2,1,0:T(8,128)(2,1)S(1)}, bf16[3,16,16,128]{3,2,1,0:T(8,128)(2,1)S(1)}, u32[]{:S(2)}, u32[]{:S(2)}) collective-permute-start(bf16[3,16,16,128]{3,2,1,0:T(8,128)(2,1)S(1)} %slice.4), channel_id=1, source_target_pairs={{24,0},{32,8},{40,16},{48,24},{56,32},{64,40},{72,48},{80,56},{88,... | collective-permute-start | bytes 589832 | tf_op jit(solution)/shard_map/ppermute | solution.py:302
  92.3 7.2 %collective-permute-done.3.next3 = bf16[3,16,16,128]{3,2,1,0:T(8,128)(2,1)S(1)} collective-permute-done((bf16[3,16,16,128]{3,2,1,0:T(8,128)(2,1)S(1)}, bf16[3,16,16,128]{3,2,1,0:T(8,128)(2,1)S(1)}, u32[]{:S(2)}, u32[]{:S(2)}) %collective-permute-start.3) | collective-permute-done | bytes 196640 | tf_op jit(solution)/shard_map/ppermute | solution.py:302
  99.5 0.0 collective-permute-done.2.next2_odd
  99.5 0.0 collective-permute-done.1.next2_even
  99.5 5.5 %shard_map.67 = bf16[8,22,32,128]{3,2,1,0:T(8,128)(2,1)} custom-call(bf16[8,16,16,128]{3,2,1,0:T(8,128)(2,1)S(1)} %all_to_all.21.own, bf16[8,16,16,128]{3,2,1,0:T(8,128)(2,1)S(1)} %collective-permute-done.1.next2_even, bf16[8,16,16,128]{3,2,1,0:T(8,128)(2,1)S(1)} %collective-permute-done.2.next2_odd, bf16[3,16,16,128]{3,2,1,0:T(8,128)(2,1)S(1)} %collective-permute-done.3.next3), custom_call_target="tpu_custom_call" | custom-call | tf_op jit(solution)/shard_map/pallas_call | solution.py:190
  104.9 0.0 copy-start.3
  104.9 0.0 copy-start
  104.9 8.2 %all-to-all-done.2.near = bf16[8,32,16,128]{3,2,1,0:T(8,128)(2,1)S(1)} async-done(((bf16[8,32,16,128]{3,2,1,0:T(8,128)(2,1)}), bf16[8,32,16,128]{3,2,1,0:T(8,128)(2,1)S(1)}, u32[]{:S(2)}, u32[]{:S(2)}) %all-to-all-start.2) | async-done | bytes 1048608 | tf_op jit(solution)/shard_map/all_to_all | solution.py:306
  113.2 3.6 %all-to-all-start.3 = ((bf16[8,22,32,128]{3,2,1,0:T(8,128)(2,1)}), bf16[8,22,32,128]{3,2,1,0:T(8,128)(2,1)S(1)}, u32[]{:S(2)}, u32[]{:S(2)}) async-start(bf16[8,22,32,128]{3,2,1,0:T(8,128)(2,1)} %shard_map.67), calls=%async_computation.3 | async-start | bytes 2883584 | tf_op jit(solution)/shard_map/all_to_all | solution.py:306
  117.4 0.0 copy-done.3
  117.4 0.1 fusion.1
  117.5 0.6 iota_reduce_fusion
  118.2 0.1 pad_add_fusion.info
  118.3 0.0 copy-done
  118.3 1.3 shard_map.66.near
  119.6 32.8 %all-to-all-done.3.far = bf16[8,22,32,128]{3,2,1,0:T(8,128)(2,1)S(1)} async-done(((bf16[8,22,32,128]{3,2,1,0:T(8,128)(2,1)}), bf16[8,22,32,128]{3,2,1,0:T(8,128)(2,1)S(1)}, u32[]{:S(2)}, u32[]{:S(2)}) %all-to-all-start.3) | async-done | bytes 1441824 | tf_op jit(solution)/shard_map/all_to_all | solution.py:306
  152.5 4.2 %shard_map.68 = bf16[4,201,16,128]{3,2,1,0:T(8,128)(2,1)} custom-call(s32[9]{0:T(128)S(1)} %pad_add_fusion.info, bf16[201,16,128]{2,1,0:T(8,128)(2,1)S(1)} %shard_map.66.near, bf16[8,22,32,128]{3,2,1,0:T(8,128)(2,1)S(1)} %all-to-all-done.3.far, bf16[208,256]{1,0:T(8,128)(2,1)S(1)} %copy-done), custom_call_target="tpu_custom_call" | custom-call | tf_op jit(solution)/shard_map/pallas_call | solution.py:283
  (4 shorter events, 0.0 us)
Async XLA Ops:
  0.0 39.1 %copy-start.1 = (bf16[256,256]{1,0:T(8,128)(2,1)S(1)}, bf16[256,256]{1,0:T(8,128)(2,1)}, u32[]{:S(2)}) copy-start(bf16[256,256]{1,0:T(8,128)(2,1)} %constant.19.clone.forward) | copy-start | bytes 393220
  0.0 39.1 %copy-start.2 = (s32[64]{0:T(128)S(1)}, s32[64]{0:T(128)}, u32[]{:S(2)}) copy-start(s32[64]{0:T(128)} %starts.1) | copy-start | bytes 772
  68.9 10.5 %collective-permute-start = (bf16[8,16,16,128]{3,2,1,0:T(8,128)(2,1)S(1)}, bf16[8,16,16,128]{3,2,1,0:T(8,128)(2,1)S(1)}, u32[]{:S(2)}, u32[]{:S(2)}) collective-permute-start(bf16[8,16,16,128]{3,2,1,0:T(8,128)(2,1)S(1)} %all_to_all.21.own), channel_id=1, source_target_pairs={{8,0},{16,8},{24,16},{32,24},{40,32},{48,40},{56,48},{64,56},{72,6... | collective-permute-start | bytes 1572872 | tf_op jit(solution)/shard_map/ppermute | solution.py:302
  80.9 32.3 %all-to-all-start.2 = ((bf16[8,32,16,128]{3,2,1,0:T(8,128)(2,1)}), bf16[8,32,16,128]{3,2,1,0:T(8,128)(2,1)S(1)}, u32[]{:S(2)}, u32[]{:S(2)}) async-start(bf16[8,32,16,128]{3,2,1,0:T(8,128)(2,1)} %shard_map.65), calls=%async_computation.2 | async-start | bytes 2097152 | tf_op jit(solution)/shard_map/all_to_all | solution.py:306
  84.5 15.0 %collective-permute-start.2 = (bf16[8,16,16,128]{3,2,1,0:T(8,128)(2,1)S(1)}, bf16[8,16,16,128]{3,2,1,0:T(8,128)(2,1)S(1)}, u32[]{:S(2)}, u32[]{:S(2)}) collective-permute-start(bf16[8,16,16,128]{3,2,1,0:T(8,128)(2,1)S(1)} %all_to_all.21.own), channel_id=1, source_target_pairs={{24,8},{40,24},{56,40},{72,56},{88,72},{104,88},{120,104},{136,120... | collective-permute-start | bytes 1572872 | tf_op jit(solution)/shard_map/ppermute | solution.py:302
  89.0 10.5 %collective-permute-start.1 = (bf16[8,16,16,128]{3,2,1,0:T(8,128)(2,1)S(1)}, bf16[8,16,16,128]{3,2,1,0:T(8,128)(2,1)S(1)}, u32[]{:S(2)}, u32[]{:S(2)}) collective-permute-start(bf16[8,16,16,128]{3,2,1,0:T(8,128)(2,1)S(1)} %collective-permute-done.next1), channel_id=1, source_target_pairs={{8,0},{24,16},{40,32},{56,48},{72,64},{88,80},{104,96},{120,112},{... | collective-permute-start | bytes 1572872 | tf_op jit(solution)/shard_map/ppermute | solution.py:302
  90.4 9.1 %collective-permute-start.3 = (bf16[3,16,16,128]{3,2,1,0:T(8,128)(2,1)S(1)}, bf16[3,16,16,128]{3,2,1,0:T(8,128)(2,1)S(1)}, u32[]{:S(2)}, u32[]{:S(2)}) collective-permute-start(bf16[3,16,16,128]{3,2,1,0:T(8,128)(2,1)S(1)} %slice.4), channel_id=1, source_target_pairs={{24,0},{32,8},{40,16},{48,24},{56,32},{64,40},{72,48},{80,56},{88,... | collective-permute-start | bytes 589832 | tf_op jit(solution)/shard_map/ppermute | solution.py:302
  104.9 12.5 %copy-start.3 = (s32[1,4]{1,0:T(1,128)S(1)}, s32[1,4]{1,0:T(1,128)}, u32[]{:S(2)}) copy-start(s32[1,4]{1,0:T(1,128)} %param.8) | copy-start | bytes 52
  104.9 13.3 %copy-start = (bf16[208,256]{1,0:T(8,128)(2,1)S(1)}, bf16[208,256]{1,0:T(8,128)(2,1)}, u32[]{:S(2)}) copy-start(bf16[208,256]{1,0:T(8,128)(2,1)} %constant.20.clone.inverse) | copy-start | bytes 319492
  113.2 39.3 %all-to-all-start.3 = ((bf16[8,22,32,128]{3,2,1,0:T(8,128)(2,1)}), bf16[8,22,32,128]{3,2,1,0:T(8,128)(2,1)S(1)}, u32[]{:S(2)}, u32[]{:S(2)}) async-start(bf16[8,22,32,128]{3,2,1,0:T(8,128)(2,1)} %shard_map.67), calls=%async_computation.3 | async-start | bytes 2883584 | tf_op jit(solution)/shard_map/all_to_all | solution.py:306

commit v4 on v3

--- a/solution.py
+++ b/solution.py
@@ -19,7 +19,8 @@
 LAG_ROWS = 208
 PACK = 304
 LOW = PACK - 2 * CB
-UNITS = 6
+GROUP = 16
+UNITS = 4
 EPS = 1e-06
 MIB = 1 << 20
 
@@ -144,46 +145,89 @@
     lax.fori_loop(0, width, one, 0, unroll=True)
 
 
-def far_kernel(own, next2_even, next2_odd, next3, out, held0, held1, plain, tail):
+def far_kernel(own, next2_even, next2_odd, next3, out, held0, held1, plain):
     bands, width, rows = own.shape[:3]
     step = 2 * width
     row_index = lax.broadcasted_iota(jnp.int32, (CB, LANES), 0)
     column = lax.broadcasted_iota(jnp.int32, (CB, LANES), 1)
     after = column > row_index
+    band = row_index // GROUP
+    hole = column // GROUP == band - LOW // GROUP
+    second_half = column // GROUP % 2 == 1
     lane = lax.broadcasted_iota(jnp.int32, (bands, LANES), 1)
 
     def one(f, carry):
         mine, sides = both_sides(own, f)
         second = (next2_even[:, f] + next2_odd[:, f]).reshape(CB, LANES)
-        low = second[:LOW]
         third = next3[:, f].reshape(LOW, LANES)
-        mixed = [mine, second[LOW:], third, low, low, low[:32], low, low, low[32:], low[32:]]
-        result = dot(sides, jnp.concatenate(mixed, axis=0), NT) * (1.0 / NWIN)
+        copies = LANES // GROUP
+        low = [second[k * GROUP : (k + 1) * GROUP] for k in range(3) for _ in range(copies)]
+        mixed = jnp.concatenate([mine, second[LOW:], third] + low, axis=0)
+        result = dot(sides, mixed, NT) * (1.0 / NWIN)
         for part in range(2):
             of = result[part * CB : (part + 1) * CB]
             at = part * width + f
-            held0[pl.ds(at, CB, stride=step), :] = jnp.where(after, of[:, :CB], of[:, CB : 2 * CB])
-            base = pl.multiple_of(at * CB, CB)
-            plain[pl.ds(base, CB), :] = of[:, 2 * CB : 3 * CB]
-            tail[pl.ds(base, CB), :] = of[:, 3 * CB :]
-
-            def row(ref, r):
-                return ref[pl.ds(base + r, bands, stride=rows), :]
-
+            here, there, low0, low1, low2 = (of[:, k * CB : (k + 1) * CB] for k in range(5))
+            shared = jnp.where(hole, low2, jnp.where(after, here, there))
+            held0[pl.ds(at, CB, stride=step), :] = shared
+            left = jnp.where(band == 0, low1, low0)
+            right = jnp.where(band <= 1, low2, low1)
+            base = at * CB
+            plain[pl.ds(base, CB), :] = jnp.where(second_half, right, left)
             for unit in range(UNITS):
-                if unit < 4:
-                    last = row(plain, 12 + unit)
-                else:
-                    pair = 12 + 2 * (unit - 4)
-                    last = jnp.where(lane < LANES - 16, row(tail, pair), row(tail, pair + 1))
-                value = jnp.where(lane < 2 * LOW, row(plain, UNITS + unit), last)
-                value = jnp.where(lane < LOW, row(plain, unit), value)
+                value = plain[pl.ds(base + unit + 12, bands, stride=rows), :]
+                for k in (2, 1, 0):
+                    other = plain[pl.ds(base + unit + 4 * k, bands, stride=rows), :]
+                    value = jnp.where(lane < 32 * (k + 1), other, value)
                 held1[pl.ds(unit * step + at, bands, stride=UNITS * step), :] = value
         return carry
 
     lax.fori_loop(0, width, one, 0, unroll=True)
     out[:, :rows] = held0[...].astype(jnp.bfloat16).reshape(bands, rows, step, LANES)
     out[:, rows:] = held1[...].astype(jnp.bfloat16).reshape(bands, UNITS, step, LANES)
+
+
+def local_kernel(first, mine, other, inverse, out, held):
+    bands, width, rows = mine.shape[:3]
+    copies = LANES // GROUP
+    lane = lax.broadcasted_iota(jnp.int32, (rows, LANES), 1)
+    row_index = lax.broadcasted_iota(jnp.int32, (rows, LANES), 0)
+    wanted = lane // GROUP == row_index % copies
+
+    def one(f, carry):
+        for band in range(bands):
+            rows_of = mine[band, f]
+            wide = rows_of.astype(jnp.float32)
+            turned = pltpu.roll(wide, NWIN, 1)
+            turned = jnp.where(lane < NWIN, -turned, turned).astype(jnp.bfloat16)
+            sides = jnp.concatenate([rows_of, turned], axis=0)
+            columns = jnp.concatenate([other[band, f]] * copies, axis=0)
+            result = dot(sides, columns, NT) * (1.0 / NWIN)
+            for part in range(2):
+                picked = jnp.where(wanted, result[part * rows : (part + 1) * rows], 0.0)
+                for half in range(2):
+                    line = jnp.sum(picked[half * copies : (half + 1) * copies], axis=0, keepdims=True)
+                    held[half, pl.ds(band * 2 * width + part * width + f, 1), :] = line
+        return carry
+
+    lax.fori_loop(0, width, one, 0)
+    for half in range(2):
+        result = dot(inverse[...], held[half].astype(jnp.bfloat16), NN)
+        for k in range(copies):
+            turn = lax.bitwise_and(first[0] + (LANES - GROUP * k), LANES - 1)
+            out[half * copies + k] = pltpu.roll(result, turn, 1)
+
+
+def local_lags(first, mine, other, inverse):
+    return pl.pallas_call(
+        local_kernel,
+        out_shape=jax.ShapeDtypeStruct((mine.shape[2], LAG_ROWS, LANES), jnp.float32),
+        in_specs=[pl.BlockSpec(memory_space=pltpu.SMEM)]
+        + [pl.BlockSpec(memory_space=pltpu.VMEM)] * 3,
+        out_specs=pl.BlockSpec(memory_space=pltpu.VMEM),
+        scratch_shapes=[pltpu.VMEM((2, WIN, LANES), jnp.float32)],
+        compiler_params=pltpu.CompilerParams(vmem_limit_bytes=16 * MIB),
+    )(first, mine, other, inverse)
 
 
 def vmem_call(kernel, out_shape, scratch, limit, *args):
@@ -217,7 +261,7 @@
     out[...] = held[...].astype(jnp.bfloat16).reshape(out.shape)
 
 
-def lag_kernel(info, near, far, inverse, out, held, low, done, sems):
+def lag_kernel(info, near, same, far, inverse, out, held, parts, done, sems):
     bands, rows, step = far.shape[0], near.shape[1], far.shape[2]
     depth = bands * step
     first = info[2 * TMAX]
@@ -247,17 +291,19 @@
         return both[:, :LANES], both[:, LANES:]
 
     for unit in range(0, UNITS, 2):
-        low[unit], low[unit + 1] = paired(rows + unit)
+        parts[unit], parts[unit + 1] = paired(rows + unit)
+    own_group = (column >= first) & (column < first + GROUP)
+    extra = (column >= jnp.where(first == 0, GROUP, 32)) & (column < LOW)
+    has_hole = first >= LOW
 
     def lower(row):
-        if row < UNITS:
-            return low[row]
-        if row < 2 * UNITS:
-            return pltpu.roll(low[row - UNITS], LANES - LOW, 1)
-        extra = row - 2 * UNITS
-        start = pltpu.roll(low[extra], 32, 1)
-        end = pltpu.roll(low[4 + extra // 2], 64 - 16 * (extra % 2), 1)
-        return jnp.where(column < 32, start, end)
+        unit, at = row % UNITS, 32 * (row // UNITS)
+        value = parts[unit]
+        if at:
+            value = pltpu.roll(value, LANES - at, 1)
+        turn = jnp.where(has_hole, 32 + LOW + LANES - first, LANES - at + GROUP)
+        moved = parts[jnp.where(has_hole, UNITS + row, unit)]
+        return jnp.where(extra, pltpu.roll(moved, lax.bitwise_and(turn, LANES - 1), 1), value)
 
     def put(place, row, value):
         held[place, pl.ds(row, LAGS, stride=rows), :] = value[:LAGS]
@@ -267,7 +313,9 @@
             i = first + row
             put(0, row, jnp.where(column > i, shared, 0.0))
             turned = pltpu.roll(shared, LOW, 1)
+            parts[UNITS + row] = shared
             joined = jnp.where(column < LOW, lower(row), turned)
+            joined = jnp.where(own_group, same[row], joined)
             put(1, row, jnp.where(column <= i + RANGE - 2 * CB, joined, 0.0))
             put(2, row, jnp.where(column <= i + RANGE - 3 * CB, turned, 0.0))
 
@@ -278,22 +326,27 @@
         pltpu.make_async_copy(done.at[0], out.at[slot], sems.at[slot]).wait()
 
 
-def lags(info, near, far, inverse):
+def lags(info, near, same, far, inverse):
     rows = near.shape[1]
     return pl.pallas_call(
         lag_kernel,
         out_shape=jax.ShapeDtypeStruct((TMAX, LAGS, rows, LANES), jnp.bfloat16),
-        in_specs=[pl.BlockSpec(memory_space=pltpu.SMEM)]
-        + [pl.BlockSpec(memory_space=pltpu.VMEM)] * 3,
+        in_specs=[
+            pl.BlockSpec(memory_space=pltpu.SMEM),
+            pl.BlockSpec(memory_space=pl.ANY),
+            pl.BlockSpec(memory_space=pltpu.VMEM),
+            pl.BlockSpec(memory_space=pltpu.VMEM),
+            pl.BlockSpec(memory_space=pltpu.VMEM),
+        ],
         out_specs=pl.BlockSpec(memory_space=pl.ANY),
         scratch_shapes=[
             pltpu.VMEM((TMAX - 1, LAGS * rows, LANES), jnp.float32),
-            pltpu.VMEM((UNITS, LAG_ROWS, LANES), jnp.float32),
+            pltpu.VMEM((UNITS + rows, LAG_ROWS, LANES), jnp.float32),
             pltpu.VMEM((TMAX, LAGS, rows, LANES), jnp.bfloat16),
             pltpu.SemaphoreType.DMA((TMAX,)),
         ],
         compiler_params=pltpu.CompilerParams(vmem_limit_bytes=32 * MIB),
-    )(info, near, far, inverse)
+    )(info, near, same, far, inverse)
 
 
 def from_ahead(block, distance, parity=None):
@@ -312,7 +365,8 @@
     width = HALF // bands
     forward, inverse = tables(bands)
     series = exchanged(traces, "chan")
-    own = exchanged(whitened_rows(window_starts, series, forward, bands), "band")
+    white = whitened_rows(window_starts, series, forward, bands)
+    own = exchanged(white, "band")
     next1 = from_ahead(own, 1)
     next2 = (from_ahead(next1, 1, 0), from_ahead(own, 2, 1))
     reach = -(-(RANGE - 2 * CB) // rows)
@@ -334,20 +388,22 @@
             (CB * 2 * width, LANES),
             (bands * UNITS * 2 * width, LANES),
             (CB * 2 * width, LANES),
-            (CB * 2 * width, LANES),
         ],
         24 * MIB,
         own,
         *next2,
         next3,
     )
+    white, far = lax.optimization_barrier((white, far))
+    first = (lax.axis_index("band") * rows).astype(jnp.int32)[None]
+    same = local_lags(first, white, from_ahead(white, 2), inverse)
     far = exchanged(far, "band")
     live = jnp.arange(TMAX) < tile_count[0]
     holds = (tile_offsets[0][None, :] == jnp.arange(TMAX)[:, None]) & live[None, :]
     slot_of = jnp.where(holds.any(axis=1), jnp.argmax(holds, axis=1), TMAX)
-    first = (lax.axis_index("band") * rows)[None]
     info = jnp.concatenate([slot_of, live, first]).astype(jnp.int32)
-    result = lags(info, near, far, inverse)
+    near = pltpu.with_memory_space_constraint(near, pltpu.HBM)
+    result = lags(info, near, same, far, inverse)
     return result.transpose(0, 2, 3, 1)[None]
 
 

time: 159 us -> 179 us (1.13)
  Pallas kernels: 15 us -> 43.3 us
  waiting for transfers between devices: 55.9 us -> 43.6 us
  starting transfers between devices: 17.8 us -> 21.3 us
  local copies, waits for them, and re-layouts: 0.03 us -> 1.84 us
    all_to_all x2, waiting for transfers between devices: 41.1 us -> 18 us  [exchanged(): return lax.all_to_all(block, axis, split_axis=0, concat_axis=0, tiled=True)]
    pallas_call x1, Pallas kernels: 4.21 us -> 26.6 us  [lags(): pl.pallas_call(lag_kernel, out_shape=jax.ShapeDtypeStruct((TMAX, LAGS, ro...]
    ppermute x4 -> x5, waiting for transfers between devices: 14.8 us -> 25.6 us  [from_ahead(): return lax.ppermute(block, 'chan', route)]
    pallas_call x0 -> x1, Pallas kernels: none -> 5.49 us  [local_lags(): pl.pallas_call(local_kernel, out_shape=jax.ShapeDtypeStruct((mine.shape[2...]
    ppermute x4 -> x5, starting transfers between devices: 10.6 us -> 14.2 us  [from_ahead(): return lax.ppermute(block, 'chan', route)]
    unnamed x8 -> x16, local copies, waits for them, and re-layouts: 0.01 us -> 1.82 us
  transfers between devices with their start and end apart: 6 -> 7, of which waited for: 4 -> 5; matrix products, arithmetic and copies ran while one was open for 1% -> 1% of each run, Pallas kernels for 4% -> 7%
where the time goes in v4:
time: 179 us; the launch traced here: 178 us
  blocking collectives  66.3 us (37%)
  waiting for transfers between devices  43.6 us (24%)
  Pallas kernels  43.3 us (24%)
  starting transfers between devices  21.3 us (12%)
  local copies, waits for them, and re-layouts  1.84 us (1%)
    all_to_all x2, blocking collectives, exchanged(): return lax.all_to_all(block, axis, split_axis=0, concat_axis=0, tiled=True)  66.3 us
    pallas_call x1, Pallas kernels, lags(): pl.pallas_call(lag_kernel, out_shape=jax.ShapeDtypeStruct((TMAX, LAGS, ro...  26.6 us
    ppermute x5, waiting for transfers between devices, from_ahead(): return lax.ppermute(block, 'chan', route)  25.6 us
    all_to_all x2, waiting for transfers between devices, exchanged(): return lax.all_to_all(block, axis, split_axis=0, concat_axis=0, tiled=True)  18 us
    ppermute x5, starting transfers between devices, from_ahead(): return lax.ppermute(block, 'chan', route)  14.2 us
    pallas_call x3, Pallas kernels, vmem_call(): pl.pallas_call(kernel, out_shape=jax.ShapeDtypeStruct(out_shape, jnp.bflo...  8.72 us
    all_to_all x2, starting transfers between devices, exchanged(): return lax.all_to_all(block, axis, split_axis=0, concat_axis=0, tiled=True)  7.13 us
    pallas_call x1, Pallas kernels, local_lags(): pl.pallas_call(local_kernel, out_shape=jax.ShapeDtypeStruct((mine.shape[2...  5.49 us
  transfers between devices with their start and end apart: 7, of which 5 were waited for; matrix products, arithmetic and copies ran while one was open for 1% of the time, Pallas kernels for 7%

profile of v4, /device:TPU:9, one launch (start us, length us, event | category | flops | bytes accessed | tf_op | source)
XLA Modules:
  0.0 178.2 jit_solution(11822568808133787575)
XLA Ops:
  0.0 39.0 %all_to_all.20.traces = bf16[64,16,512]{2,1,0:T(8,128)(2,1)S(1)} all-to-all(bf16[64,16,512]{2,1,0:T(8,128)(2,1)} %param.6), channel_id=1, replica_groups=mesh['chan'=64,'band'=8] {'chan'}, dimensions={0} | all-to-all | bytes 2097152 | tf_op jit(solution)/shard_map/all_to_all | solution.py:359
  39.1 0.0 copy-done.5
  39.1 0.0 copy-done.6
  39.1 2.5 %shard_map.64.mine = bf16[8,16,16,128]{3,2,1,0:T(8,128)(2,1)S(1)} custom-call(s32[64]{0:T(128)S(1)} %copy-done.6, bf16[64,16,512]{2,1,0:T(8,128)(2,1)S(1)} %all_to_all.20.traces, bf16[256,256]{1,0:T(8,128)(2,1)S(1)} %copy-done.5), custom_call_target="tpu_custom_call" | custom-call | tf_op jit(solution)/shard_map/pallas_call | solution.py:107
  41.6 27.3 %all_to_all.21.own = bf16[8,16,16,128]{3,2,1,0:T(8,128)(2,1)S(1)} all-to-all(bf16[8,16,16,128]{3,2,1,0:T(8,128)(2,1)S(1)} %shard_map.64.mine), channel_id=1, replica_groups=mesh['chan'=64,'band'=8] {'band'}, dimensions={0} | all-to-all | bytes 1048576 | tf_op jit(solution)/shard_map/all_to_all | solution.py:359
  68.8 2.9 %collective-permute-start = (bf16[8,16,16,128]{3,2,1,0:T(8,128)(2,1)S(1)}, bf16[8,16,16,128]{3,2,1,0:T(8,128)(2,1)S(1)}, u32[]{:S(2)}, u32[]{:S(2)}) collective-permute-start(bf16[8,16,16,128]{3,2,1,0:T(8,128)(2,1)S(1)} %all_to_all.21.own), channel_id=1, source_target_pairs={{8,0},{16,8},{24,16},{32,24},{40,32},{48,40},{56,48},{64,56},{72,6... | collective-permute-start | bytes 1572872 | tf_op jit(solution)/shard_map/ppermute | solution.py:355
  71.8 7.6 %collective-permute-done.next1 = bf16[8,16,16,128]{3,2,1,0:T(8,128)(2,1)S(1)} collective-permute-done((bf16[8,16,16,128]{3,2,1,0:T(8,128)(2,1)S(1)}, bf16[8,16,16,128]{3,2,1,0:T(8,128)(2,1)S(1)}, u32[]{:S(2)}, u32[]{:S(2)}) %collective-permute-start) | collective-permute-done | bytes 524320 | tf_op jit(solution)/shard_map/ppermute | solution.py:355
  79.3 1.5 shard_map.65
  80.8 3.6 %all-to-all-start.2 = ((bf16[8,32,16,128]{3,2,1,0:T(8,128)(2,1)}), bf16[8,32,16,128]{3,2,1,0:T(8,128)(2,1)S(1)}, u32[]{:S(2)}, u32[]{:S(2)}) async-start(bf16[8,32,16,128]{3,2,1,0:T(8,128)(2,1)} %shard_map.65), calls=%async_computation.2 | async-start | bytes 2097152 | tf_op jit(solution)/shard_map/all_to_all | solution.py:359
  84.3 4.7 %collective-permute-start.2 = (bf16[8,16,16,128]{3,2,1,0:T(8,128)(2,1)S(1)}, bf16[8,16,16,128]{3,2,1,0:T(8,128)(2,1)S(1)}, u32[]{:S(2)}, u32[]{:S(2)}) collective-permute-start(bf16[8,16,16,128]{3,2,1,0:T(8,128)(2,1)S(1)} %all_to_all.21.own), channel_id=1, source_target_pairs={{24,8},{40,24},{56,40},{72,56},{88,72},{104,88},{120,104},{136,120... | collective-permute-start | bytes 1572872 | tf_op jit(solution)/shard_map/ppermute | solution.py:355
  89.0 1.3 collective-permute-start.1
  90.4 1.9 %collective-permute-start.3 = (bf16[3,16,16,128]{3,2,1,0:T(8,128)(2,1)S(1)}, bf16[3,16,16,128]{3,2,1,0:T(8,128)(2,1)S(1)}, u32[]{:S(2)}, u32[]{:S(2)}) collective-permute-start(bf16[3,16,16,128]{3,2,1,0:T(8,128)(2,1)S(1)} %slice.4), channel_id=1, source_target_pairs={{24,0},{32,8},{40,16},{48,24},{56,32},{64,40},{72,48},{80,56},{88,... | collective-permute-start | bytes 589832 | tf_op jit(solution)/shard_map/ppermute | solution.py:355
  92.3 7.2 %collective-permute-done.3.next3 = bf16[3,16,16,128]{3,2,1,0:T(8,128)(2,1)S(1)} collective-permute-done((bf16[3,16,16,128]{3,2,1,0:T(8,128)(2,1)S(1)}, bf16[3,16,16,128]{3,2,1,0:T(8,128)(2,1)S(1)}, u32[]{:S(2)}, u32[]{:S(2)}) %collective-permute-start.3) | collective-permute-done | bytes 196640 | tf_op jit(solution)/shard_map/ppermute | solution.py:355
  99.4 0.0 collective-permute-done.2.next2_odd
  99.4 0.0 collective-permute-done.1.next2_even
  99.4 5.9 %shard_map.67 = bf16[8,20,32,128]{3,2,1,0:T(8,128)(2,1)} custom-call(bf16[8,16,16,128]{3,2,1,0:T(8,128)(2,1)S(1)} %all_to_all.21.own, bf16[8,16,16,128]{3,2,1,0:T(8,128)(2,1)S(1)} %collective-permute-done.1.next2_even, bf16[8,16,16,128]{3,2,1,0:T(8,128)(2,1)S(1)} %collective-permute-done.2.next2_odd, bf16[3,16,16,128]{3,2,1,0:T(8,128)(2,1)S(1)} %collective-permute-done.3.next3), custom_call_target="tpu_custom_call" | custom-call | tf_op jit(solution)/shard_map/pallas_call | solution.py:234
  105.3 7.8 %all-to-all-done.2.near = bf16[8,32,16,128]{3,2,1,0:T(8,128)(2,1)S(1)} async-done(((bf16[8,32,16,128]{3,2,1,0:T(8,128)(2,1)}), bf16[8,32,16,128]{3,2,1,0:T(8,128)(2,1)S(1)}, u32[]{:S(2)}, u32[]{:S(2)}) %all-to-all-start.2) | async-done | bytes 1048608 | tf_op jit(solution)/shard_map/all_to_all | solution.py:359
  113.1 3.6 %all-to-all-start.3 = ((bf16[8,20,32,128]{3,2,1,0:T(8,128)(2,1)}), bf16[8,20,32,128]{3,2,1,0:T(8,128)(2,1)S(1)}, u32[]{:S(2)}, u32[]{:S(2)}) async-start(bf16[8,20,32,128]{3,2,1,0:T(8,128)(2,1)} %shard_map.67), calls=%async_computation.3 | async-start | bytes 2621440 | tf_op jit(solution)/shard_map/all_to_all | solution.py:359
  117.4 0.0 copy-done.7
  117.4 0.1 fusion.1
  117.5 3.3 %collective-permute-start.4 = (bf16[8,16,16,128]{3,2,1,0:T(8,128)(2,1)S(1)}, bf16[8,16,16,128]{3,2,1,0:T(8,128)(2,1)S(1)}, u32[]{:S(2)}, u32[]{:S(2)}) collective-permute-start(bf16[8,16,16,128]{3,2,1,0:T(8,128)(2,1)S(1)} %shard_map.64.mine), channel_id=1, source_target_pairs={{16,0},{24,8},{32,16},{40,24},{48,32},{56,40},{64,48},{72,56},{80,... | collective-permute-start | bytes 1572872 | tf_op jit(solution)/shard_map/ppermute | solution.py:355
  120.9 0.7 iota_reduce_fusion
  121.6 0.1 pad_add_fusion.info
  121.6 0.0 copy-done
  121.6 10.9 %collective-permute-done.4.other = bf16[8,16,16,128]{3,2,1,0:T(8,128)(2,1)S(1)} collective-permute-done((bf16[8,16,16,128]{3,2,1,0:T(8,128)(2,1)S(1)}, bf16[8,16,16,128]{3,2,1,0:T(8,128)(2,1)S(1)}, u32[]{:S(2)}, u32[]{:S(2)}) %collective-permute-start.4) | collective-permute-done | bytes 524320 | tf_op jit(solution)/shard_map/ppermute | solution.py:355
  132.5 0.9 copy-done.3
  133.4 5.5 %shard_map.68.same = f32[16,208,128]{2,1,0:T(8,128)S(1)} custom-call(s32[1]{0:T(128)} %bitcast.2.first, bf16[8,16,16,128]{3,2,1,0:T(8,128)(2,1)S(1)} %shard_map.64.mine, bf16[8,16,16,128]{3,2,1,0:T(8,128)(2,1)S(1)} %collective-permute-done.4.other, bf16[208,256]{1,0:T(8,128)(2,1)S(1)} %copy-done.3), custom_call_target="tpu_custom_call" | custom-call | tf_op jit(solution)/shard_map/pallas_call | solution.py:222
  138.9 0.0 copy-start.4
  138.9 1.4 shard_map.66.near
  140.4 0.9 copy-done.2
  141.3 10.2 %all-to-all-done.3.far = bf16[8,20,32,128]{3,2,1,0:T(8,128)(2,1)S(1)} async-done(((bf16[8,20,32,128]{3,2,1,0:T(8,128)(2,1)}), bf16[8,20,32,128]{3,2,1,0:T(8,128)(2,1)S(1)}, u32[]{:S(2)}, u32[]{:S(2)}) %all-to-all-start.3) | async-done | bytes 1310752 | tf_op jit(solution)/shard_map/all_to_all | solution.py:359
  151.5 26.6 %shard_map.69 = bf16[4,201,16,128]{3,2,1,0:T(8,128)(2,1)} custom-call(s32[9]{0:T(128)S(1)} %pad_add_fusion.info, bf16[201,16,128]{2,1,0:T(8,128)(2,1)} %copy-done.2, f32[16,208,128]{2,1,0:T(8,128)S(1)} %shard_map.68.same, bf16[8,20,32,128]{3,2,1,0:T(8,128)(2,1)S(1)} %all-to-all-done.3.far, bf16[208,256]{1,0:T(8,128)(2,1)S(1)} %copy-done.4), custom_call_target="tpu_custom_call" | custom-call | tf_op jit(solution)/shard_map/pallas_call | solution.py:331
  (13 shorter events, 0.0 us)
Async XLA Ops:
  0.0 39.1 %copy-start.5 = (bf16[256,256]{1,0:T(8,128)(2,1)S(1)}, bf16[256,256]{1,0:T(8,128)(2,1)}, u32[]{:S(2)}) copy-start(bf16[256,256]{1,0:T(8,128)(2,1)} %constant.19.clone.forward) | copy-start | bytes 393220
  0.0 39.1 %copy-start.6 = (s32[64]{0:T(128)S(1)}, s32[64]{0:T(128)}, u32[]{:S(2)}) copy-start(s32[64]{0:T(128)} %starts.1) | copy-start | bytes 772
  68.8 10.5 %collective-permute-start = (bf16[8,16,16,128]{3,2,1,0:T(8,128)(2,1)S(1)}, bf16[8,16,16,128]{3,2,1,0:T(8,128)(2,1)S(1)}, u32[]{:S(2)}, u32[]{:S(2)}) collective-permute-start(bf16[8,16,16,128]{3,2,1,0:T(8,128)(2,1)S(1)} %all_to_all.21.own), channel_id=1, source_target_pairs={{8,0},{16,8},{24,16},{32,24},{40,32},{48,40},{56,48},{64,56},{72,6... | collective-permute-start | bytes 1572872 | tf_op jit(solution)/shard_map/ppermute | solution.py:355
  80.8 32.4 %all-to-all-start.2 = ((bf16[8,32,16,128]{3,2,1,0:T(8,128)(2,1)}), bf16[8,32,16,128]{3,2,1,0:T(8,128)(2,1)S(1)}, u32[]{:S(2)}, u32[]{:S(2)}) async-start(bf16[8,32,16,128]{3,2,1,0:T(8,128)(2,1)} %shard_map.65), calls=%async_computation.2 | async-start | bytes 2097152 | tf_op jit(solution)/shard_map/all_to_all | solution.py:359
  84.3 15.1 %collective-permute-start.2 = (bf16[8,16,16,128]{3,2,1,0:T(8,128)(2,1)S(1)}, bf16[8,16,16,128]{3,2,1,0:T(8,128)(2,1)S(1)}, u32[]{:S(2)}, u32[]{:S(2)}) collective-permute-start(bf16[8,16,16,128]{3,2,1,0:T(8,128)(2,1)S(1)} %all_to_all.21.own), channel_id=1, source_target_pairs={{24,8},{40,24},{56,40},{72,56},{88,72},{104,88},{120,104},{136,120... | collective-permute-start | bytes 1572872 | tf_op jit(solution)/shard_map/ppermute | solution.py:355
  89.0 10.4 %collective-permute-start.1 = (bf16[8,16,16,128]{3,2,1,0:T(8,128)(2,1)S(1)}, bf16[8,16,16,128]{3,2,1,0:T(8,128)(2,1)S(1)}, u32[]{:S(2)}, u32[]{:S(2)}) collective-permute-start(bf16[8,16,16,128]{3,2,1,0:T(8,128)(2,1)S(1)} %collective-permute-done.next1), channel_id=1, source_target_pairs={{8,0},{24,16},{40,32},{56,48},{72,64},{88,80},{104,96},{120,112},{... | collective-permute-start | bytes 1572872 | tf_op jit(solution)/shard_map/ppermute | solution.py:355
  90.4 9.1 %collective-permute-start.3 = (bf16[3,16,16,128]{3,2,1,0:T(8,128)(2,1)S(1)}, bf16[3,16,16,128]{3,2,1,0:T(8,128)(2,1)S(1)}, u32[]{:S(2)}, u32[]{:S(2)}) collective-permute-start(bf16[3,16,16,128]{3,2,1,0:T(8,128)(2,1)S(1)} %slice.4), channel_id=1, source_target_pairs={{24,0},{32,8},{40,16},{48,24},{56,32},{64,40},{72,48},{80,56},{88,... | collective-permute-start | bytes 589832 | tf_op jit(solution)/shard_map/ppermute | solution.py:355
  105.3 12.1 %copy-start.7 = (s32[1,4]{1,0:T(1,128)S(1)}, s32[1,4]{1,0:T(1,128)}, u32[]{:S(2)}) copy-start(s32[1,4]{1,0:T(1,128)} %param.8) | copy-start | bytes 52
  113.1 8.5 %copy-start = (bf16[8,32,16,128]{3,2,1,0:T(8,128)(2,1)}, bf16[8,32,16,128]{3,2,1,0:T(8,128)(2,1)S(1)}, u32[]{:S(2)}) copy-start(bf16[8,32,16,128]{3,2,1,0:T(8,128)(2,1)S(1)} %all-to-all-done.2.near) | copy-start | bytes 3145732
  113.1 38.3 %all-to-all-start.3 = ((bf16[8,20,32,128]{3,2,1,0:T(8,128)(2,1)}), bf16[8,20,32,128]{3,2,1,0:T(8,128)(2,1)S(1)}, u32[]{:S(2)}, u32[]{:S(2)}) async-start(bf16[8,20,32,128]{3,2,1,0:T(8,128)(2,1)} %shard_map.67), calls=%async_computation.3 | async-start | bytes 2621440 | tf_op jit(solution)/shard_map/all_to_all | solution.py:359
  117.5 15.0 %collective-permute-start.4 = (bf16[8,16,16,128]{3,2,1,0:T(8,128)(2,1)S(1)}, bf16[8,16,16,128]{3,2,1,0:T(8,128)(2,1)S(1)}, u32[]{:S(2)}, u32[]{:S(2)}) collective-permute-start(bf16[8,16,16,128]{3,2,1,0:T(8,128)(2,1)S(1)} %shard_map.64.mine), channel_id=1, source_target_pairs={{16,0},{24,8},{32,16},{40,24},{48,32},{56,40},{64,48},{72,56},{80,... | collective-permute-start | bytes 1572872 | tf_op jit(solution)/shard_map/ppermute | solution.py:355
  132.5 0.9 copy-start.3
  133.4 5.5 %copy-start.1 = (bf16[8,32,16,128]{3,2,1,0:T(8,128)(2,1)S(1)}, bf16[8,32,16,128]{3,2,1,0:T(8,128)(2,1)}, u32[]{:S(2)}) copy-start(bf16[8,32,16,128]{3,2,1,0:T(8,128)(2,1)} %copy-done) | copy-start | bytes 3145732
  138.9 12.5 %copy-start.4 = (bf16[208,256]{1,0:T(8,128)(2,1)S(1)}, bf16[208,256]{1,0:T(8,128)(2,1)}, u32[]{:S(2)}) copy-start(bf16[208,256]{1,0:T(8,128)(2,1)} %constant.20.clone.inverse) | copy-start | bytes 319492
  140.3 0.9 copy-start.2

commit v5 on v4

--- a/solution.py
+++ b/solution.py
@@ -241,10 +241,20 @@
     )(*args)
 
 
-def near_lag_kernel(near, inverse, out, wide, held):
+def first_lag_kernel(info, near, inverse, out, wide, held, done, blank, sems):
     bands, step, rows = near.shape[:3]
     depth = bands * step
     table = inverse[...]
+    blank[...] = jnp.zeros(blank.shape, jnp.bfloat16)
+
+    def copy(kind, source, act):
+        for slot in range(TMAX):
+
+            @pl.when(info[TMAX + slot] == kind)
+            def _():
+                act(pltpu.make_async_copy(source, out.at[slot], sems.at[slot]))
+
+    copy(2, blank, lambda c: c.start())
     wide[...] = near[...].astype(jnp.float32).reshape(wide.shape)
 
     def one(pair, carry):
@@ -258,30 +268,41 @@
         return carry
 
     lax.fori_loop(0, rows // 2, one, 0, unroll=True)
-    out[...] = held[...].astype(jnp.bfloat16).reshape(out.shape)
-
-
-def lag_kernel(info, near, same, far, inverse, out, held, parts, done, sems):
-    bands, rows, step = far.shape[0], near.shape[1], far.shape[2]
+    done[...] = held[...].astype(jnp.bfloat16).reshape(done.shape)
+    copy(1, done, lambda c: c.start())
+    copy(1, done, lambda c: c.wait())
+    copy(2, blank, lambda c: c.wait())
+
+
+def first_lags(info, near, inverse):
+    rows = near.shape[2]
+    return pl.pallas_call(
+        first_lag_kernel,
+        out_shape=jax.ShapeDtypeStruct((TMAX, LAGS, rows, LANES), jnp.bfloat16),
+        in_specs=[
+            pl.BlockSpec(memory_space=pltpu.SMEM),
+            pl.BlockSpec(memory_space=pltpu.VMEM),
+            pl.BlockSpec(memory_space=pltpu.VMEM),
+        ],
+        out_specs=pl.BlockSpec(memory_space=pltpu.HBM),
+        scratch_shapes=[
+            pltpu.VMEM((WIN * rows, LANES), jnp.float32),
+            pltpu.VMEM((LAGS * rows, LANES), jnp.float32),
+            pltpu.VMEM((LAGS, rows, LANES), jnp.bfloat16),
+            pltpu.VMEM((LAGS, rows, LANES), jnp.bfloat16),
+            pltpu.SemaphoreType.DMA((TMAX,)),
+        ],
+        compiler_params=pltpu.CompilerParams(vmem_limit_bytes=16 * MIB),
+    )(info, near, inverse)
+
+
+def lag_kernel(info, begun, same, far, inverse, out, held, parts, done, sems):
+    bands, rows, step = far.shape[0], same.shape[0], far.shape[2]
     depth = bands * step
     first = info[2 * TMAX]
     column = lax.broadcasted_iota(jnp.int32, (LAG_ROWS, LANES), 1)
     table = inverse[...]
-
-    def send(offset, source):
-        slot = info[offset]
-
-        @pl.when(slot < TMAX)
-        def _():
-            pltpu.make_async_copy(source, out.at[slot], sems.at[slot]).start()
-
-    send(1, near)
-    done[0] = jnp.zeros(done.shape[1:], jnp.bfloat16)
-    for slot in range(TMAX):
-
-        @pl.when(info[TMAX + slot] == 0)
-        def _():
-            pltpu.make_async_copy(done.at[0], out.at[slot], sems.at[slot]).start()
+    reaches = first + rows + RANGE > 3 * CB
 
     def piece(row):
         return far[:, row].reshape(depth, LANES)
@@ -308,45 +329,68 @@
     def put(place, row, value):
         held[place, pl.ds(row, LAGS, stride=rows), :] = value[:LAGS]
 
+    def finish(place, offset):
+        done[place] = held[place].astype(jnp.bfloat16).reshape(LAGS, rows, LANES)
+        slot = info[offset]
+
+        @pl.when(slot < TMAX)
+        def _():
+            pltpu.make_async_copy(done.at[place], out.at[slot], sems.at[place]).start()
+
+    def settle(place, offset):
+        slot = info[offset]
+
+        @pl.when(slot < TMAX)
+        def _():
+            pltpu.make_async_copy(done.at[place], out.at[slot], sems.at[place]).wait()
+
     for pair in range(0, rows, 2):
         for row, shared in zip((pair, pair + 1), paired(pair)):
-            i = first + row
-            put(0, row, jnp.where(column > i, shared, 0.0))
-            turned = pltpu.roll(shared, LOW, 1)
             parts[UNITS + row] = shared
-            joined = jnp.where(column < LOW, lower(row), turned)
-            joined = jnp.where(own_group, same[row], joined)
-            put(1, row, jnp.where(column <= i + RANGE - 2 * CB, joined, 0.0))
-            put(2, row, jnp.where(column <= i + RANGE - 3 * CB, turned, 0.0))
-
-    for place, offset in enumerate((0, 2, 3)):
-        done[1 + place] = held[place].astype(jnp.bfloat16).reshape(LAGS, rows, LANES)
-        send(offset, done.at[1 + place])
-    for slot in range(TMAX):
-        pltpu.make_async_copy(done.at[0], out.at[slot], sems.at[slot]).wait()
-
-
-def lags(info, near, same, far, inverse):
-    rows = near.shape[1]
+            put(0, row, jnp.where(column > first + row, shared, 0.0))
+    finish(0, 0)
+    for row in range(rows):
+        i = first + row
+        turned = pltpu.roll(parts[UNITS + row], LOW, 1)
+        joined = jnp.where(column < LOW, lower(row), turned)
+        joined = jnp.where(own_group, same[row], joined)
+        put(1, row, jnp.where(column <= i + RANGE - 2 * CB, joined, 0.0))
+    finish(1, 2)
+
+    @pl.when(reaches)
+    def _():
+        for row in range(rows):
+            turned = pltpu.roll(parts[UNITS + row], LOW, 1)
+            put(2, row, jnp.where(column <= first + row + RANGE - 3 * CB, turned, 0.0))
+        finish(2, 3)
+        settle(2, 3)
+
+    settle(0, 0)
+    settle(1, 2)
+
+
+def lags(info, begun, same, far, inverse):
+    rows = begun.shape[2]
     return pl.pallas_call(
         lag_kernel,
-        out_shape=jax.ShapeDtypeStruct((TMAX, LAGS, rows, LANES), jnp.bfloat16),
+        out_shape=jax.ShapeDtypeStruct(begun.shape, begun.dtype),
         in_specs=[
             pl.BlockSpec(memory_space=pltpu.SMEM),
-            pl.BlockSpec(memory_space=pl.ANY),
-            pl.BlockSpec(memory_space=pltpu.VMEM),
-            pl.BlockSpec(memory_space=pltpu.VMEM),
-            pl.BlockSpec(memory_space=pltpu.VMEM),
-        ],
-        out_specs=pl.BlockSpec(memory_space=pl.ANY),
+            pl.BlockSpec(memory_space=pltpu.HBM),
+            pl.BlockSpec(memory_space=pltpu.VMEM),
+            pl.BlockSpec(memory_space=pltpu.VMEM),
+            pl.BlockSpec(memory_space=pltpu.VMEM),
+        ],
+        out_specs=pl.BlockSpec(memory_space=pltpu.HBM),
         scratch_shapes=[
-            pltpu.VMEM((TMAX - 1, LAGS * rows, LANES), jnp.float32),
+            pltpu.VMEM((3, LAGS * rows, LANES), jnp.float32),
             pltpu.VMEM((UNITS + rows, LAG_ROWS, LANES), jnp.float32),
-            pltpu.VMEM((TMAX, LAGS, rows, LANES), jnp.bfloat16),
-            pltpu.SemaphoreType.DMA((TMAX,)),
-        ],
+            pltpu.VMEM((3, LAGS, rows, LANES), jnp.bfloat16),
+            pltpu.SemaphoreType.DMA((3,)),
+        ],
+        input_output_aliases={1: 0},
         compiler_params=pltpu.CompilerParams(vmem_limit_bytes=32 * MIB),
-    )(info, near, same, far, inverse)
+    )(info, begun, same, far, inverse)
 
 
 def from_ahead(block, distance, parity=None):
@@ -373,14 +417,6 @@
     next3 = from_ahead(own[:reach], 3)
     near = vmem_call(near_kernel, (bands, 2 * width, rows, LANES), [], 16 * MIB, own, next1)
     near = exchanged(near, "band")
-    near = vmem_call(
-        near_lag_kernel,
-        (LAGS, rows, LANES),
-        [(WIN * rows, LANES), (LAGS * rows, LANES)],
-        16 * MIB,
-        near,
-        inverse,
-    )
     far = vmem_call(
         far_kernel,
         (bands, rows + UNITS, 2 * width, LANES),
@@ -401,9 +437,12 @@
     live = jnp.arange(TMAX) < tile_count[0]
     holds = (tile_offsets[0][None, :] == jnp.arange(TMAX)[:, None]) & live[None, :]
     slot_of = jnp.where(holds.any(axis=1), jnp.argmax(holds, axis=1), TMAX)
-    info = jnp.concatenate([slot_of, live, first]).astype(jnp.int32)
-    near = pltpu.with_memory_space_constraint(near, pltpu.HBM)
-    result = lags(info, near, same, far, inverse)
+    reaches = first[0] + rows + RANGE > 3 * CB
+    blank = ~live | (holds[3] & ~reaches)
+    kind = jnp.where(blank, 2, jnp.where(holds[1], 1, 0))
+    info = jnp.concatenate([slot_of, kind, first]).astype(jnp.int32)
+    begun = first_lags(info, near, inverse)
+    result = lags(info, begun, same, far, inverse)
     return result.transpose(0, 2, 3, 1)[None]
 
 

time: 179 us -> 156 us (0.87)
  Pallas kernels: 43.3 us -> 21.9 us
  waiting for transfers between devices: 43.6 us -> 41.5 us
    pallas_call x1 -> x2, Pallas kernels: 26.6 us -> 6.54 us  [the longest x1 3.59 us: first_lags(): pl.pallas_call(first_lag_kernel, out_shape=jax.ShapeDtypeStruct((TMAX, LA...]
    all_to_all x2, waiting for transfers between devices: 18 us -> 15.8 us  [exchanged(): return lax.all_to_all(block, axis, split_axis=0, concat_axis=0, tiled=True)]
    pallas_call x3 -> x2, Pallas kernels: 8.72 us -> 7.33 us  [vmem_call(): pl.pallas_call(kernel, out_shape=jax.ShapeDtypeStruct(out_shape, jnp.bflo...]
  transfers between devices with their start and end apart: 7 -> 7, of which waited for: 5 -> 5; matrix products, arithmetic and copies ran while one was open for 1% -> 1% of each run, Pallas kernels for 7% -> 10%
where the time goes in v5:
time: 156 us; the launch traced here: 155 us
  blocking collectives  66.3 us (42%)
  waiting for transfers between devices  41.5 us (27%)
  Pallas kernels  21.9 us (14%)
  starting transfers between devices  21.3 us (14%)
  local copies, waits for them, and re-layouts  1.82 us (1%)
    all_to_all x2, blocking collectives, exchanged(): return lax.all_to_all(block, axis, split_axis=0, concat_axis=0, tiled=True)  66.3 us
    ppermute x5, waiting for transfers between devices, from_ahead(): return lax.ppermute(block, 'chan', route)  25.6 us
    all_to_all x2, waiting for transfers between devices, exchanged(): return lax.all_to_all(block, axis, split_axis=0, concat_axis=0, tiled=True)  15.8 us
    ppermute x5, starting transfers between devices, from_ahead(): return lax.ppermute(block, 'chan', route)  14.2 us
    pallas_call x2, Pallas kernels, vmem_call(): pl.pallas_call(kernel, out_shape=jax.ShapeDtypeStruct(out_shape, jnp.bflo...  7.33 us
    all_to_all x2, starting transfers between devices, exchanged(): return lax.all_to_all(block, axis, split_axis=0, concat_axis=0, tiled=True)  7.13 us
    pallas_call x1, Pallas kernels, local_lags(): pl.pallas_call(local_kernel, out_shape=jax.ShapeDtypeStruct((mine.shape[2...  5.49 us
    pallas_call x1, Pallas kernels, first_lags(): pl.pallas_call(first_lag_kernel, out_shape=jax.ShapeDtypeStruct((TMAX, LA...  3.59 us
  transfers between devices with their start and end apart: 7, of which 5 were waited for; matrix products, arithmetic and copies ran while one was open for 1% of the time, Pallas kernels for 10%

profile of v5, /device:TPU:9, one launch (start us, length us, event | category | flops | bytes accessed | tf_op | source)
XLA Modules:
  0.0 154.6 jit_solution(13429570271098655994)
XLA Ops:
  0.0 39.0 %all_to_all.20.traces = bf16[64,16,512]{2,1,0:T(8,128)(2,1)S(1)} all-to-all(bf16[64,16,512]{2,1,0:T(8,128)(2,1)} %param.6), channel_id=1, replica_groups=mesh['chan'=64,'band'=8] {'chan'}, dimensions={0} | all-to-all | bytes 2097152 | tf_op jit(solution)/shard_map/all_to_all | solution.py:403
  39.1 0.0 copy-done.5
  39.1 0.0 copy-done.6
  39.1 2.5 %shard_map.64.mine = bf16[8,16,16,128]{3,2,1,0:T(8,128)(2,1)S(1)} custom-call(s32[64]{0:T(128)S(1)} %copy-done.6, bf16[64,16,512]{2,1,0:T(8,128)(2,1)S(1)} %all_to_all.20.traces, bf16[256,256]{1,0:T(8,128)(2,1)S(1)} %copy-done.5), custom_call_target="tpu_custom_call" | custom-call | tf_op jit(solution)/shard_map/pallas_call | solution.py:107
  41.6 27.3 %all_to_all.21.own = bf16[8,16,16,128]{3,2,1,0:T(8,128)(2,1)S(1)} all-to-all(bf16[8,16,16,128]{3,2,1,0:T(8,128)(2,1)S(1)} %shard_map.64.mine), channel_id=1, replica_groups=mesh['chan'=64,'band'=8] {'band'}, dimensions={0} | all-to-all | bytes 1048576 | tf_op jit(solution)/shard_map/all_to_all | solution.py:403
  68.8 2.9 %collective-permute-start = (bf16[8,16,16,128]{3,2,1,0:T(8,128)(2,1)S(1)}, bf16[8,16,16,128]{3,2,1,0:T(8,128)(2,1)S(1)}, u32[]{:S(2)}, u32[]{:S(2)}) collective-permute-start(bf16[8,16,16,128]{3,2,1,0:T(8,128)(2,1)S(1)} %all_to_all.21.own), channel_id=1, source_target_pairs={{8,0},{16,8},{24,16},{32,24},{40,32},{48,40},{56,48},{64,56},{72,6... | collective-permute-start | bytes 1572872 | tf_op jit(solution)/shard_map/ppermute | solution.py:399
  71.8 7.6 %collective-permute-done.next1 = bf16[8,16,16,128]{3,2,1,0:T(8,128)(2,1)S(1)} collective-permute-done((bf16[8,16,16,128]{3,2,1,0:T(8,128)(2,1)S(1)}, bf16[8,16,16,128]{3,2,1,0:T(8,128)(2,1)S(1)}, u32[]{:S(2)}, u32[]{:S(2)}) %collective-permute-start) | collective-permute-done | bytes 524320 | tf_op jit(solution)/shard_map/ppermute | solution.py:399
  79.3 1.5 shard_map.65
  80.8 3.6 %all-to-all-start.2 = ((bf16[8,32,16,128]{3,2,1,0:T(8,128)(2,1)}), bf16[8,32,16,128]{3,2,1,0:T(8,128)(2,1)S(1)}, u32[]{:S(2)}, u32[]{:S(2)}) async-start(bf16[8,32,16,128]{3,2,1,0:T(8,128)(2,1)} %shard_map.65), calls=%async_computation.2 | async-start | bytes 2097152 | tf_op jit(solution)/shard_map/all_to_all | solution.py:403
  84.3 4.7 %collective-permute-start.2 = (bf16[8,16,16,128]{3,2,1,0:T(8,128)(2,1)S(1)}, bf16[8,16,16,128]{3,2,1,0:T(8,128)(2,1)S(1)}, u32[]{:S(2)}, u32[]{:S(2)}) collective-permute-start(bf16[8,16,16,128]{3,2,1,0:T(8,128)(2,1)S(1)} %all_to_all.21.own), channel_id=1, source_target_pairs={{24,8},{40,24},{56,40},{72,56},{88,72},{104,88},{120,104},{136,120... | collective-permute-start | bytes 1572872 | tf_op jit(solution)/shard_map/ppermute | solution.py:399
  89.0 1.3 collective-permute-start.1
  90.4 1.9 %collective-permute-start.3 = (bf16[3,16,16,128]{3,2,1,0:T(8,128)(2,1)S(1)}, bf16[3,16,16,128]{3,2,1,0:T(8,128)(2,1)S(1)}, u32[]{:S(2)}, u32[]{:S(2)}) collective-permute-start(bf16[3,16,16,128]{3,2,1,0:T(8,128)(2,1)S(1)} %slice.12), channel_id=1, source_target_pairs={{24,0},{32,8},{40,16},{48,24},{56,32},{64,40},{72,48},{80,56},{88,... | collective-permute-start | bytes 589832 | tf_op jit(solution)/shard_map/ppermute | solution.py:399
  92.3 7.2 %collective-permute-done.3.next3 = bf16[3,16,16,128]{3,2,1,0:T(8,128)(2,1)S(1)} collective-permute-done((bf16[3,16,16,128]{3,2,1,0:T(8,128)(2,1)S(1)}, bf16[3,16,16,128]{3,2,1,0:T(8,128)(2,1)S(1)}, u32[]{:S(2)}, u32[]{:S(2)}) %collective-permute-start.3) | collective-permute-done | bytes 196640 | tf_op jit(solution)/shard_map/ppermute | solution.py:399
  99.4 0.0 collective-permute-done.2.next2_odd
  99.4 0.0 collective-permute-done.1.next2_even
  99.5 5.9 %shard_map.67 = bf16[8,20,32,128]{3,2,1,0:T(8,128)(2,1)} custom-call(bf16[8,16,16,128]{3,2,1,0:T(8,128)(2,1)S(1)} %all_to_all.21.own, bf16[8,16,16,128]{3,2,1,0:T(8,128)(2,1)S(1)} %collective-permute-done.1.next2_even, bf16[8,16,16,128]{3,2,1,0:T(8,128)(2,1)S(1)} %collective-permute-done.2.next2_odd, bf16[3,16,16,128]{3,2,1,0:T(8,128)(2,1)S(1)} %collective-permute-done.3.next3), custom_call_target="tpu_custom_call" | custom-call | tf_op jit(solution)/shard_map/pallas_call | solution.py:234
  105.3 7.8 %all-to-all-done.2.near = bf16[8,32,16,128]{3,2,1,0:T(8,128)(2,1)S(1)} async-done(((bf16[8,32,16,128]{3,2,1,0:T(8,128)(2,1)}), bf16[8,32,16,128]{3,2,1,0:T(8,128)(2,1)S(1)}, u32[]{:S(2)}, u32[]{:S(2)}) %all-to-all-start.2) | async-done | bytes 1048608 | tf_op jit(solution)/shard_map/all_to_all | solution.py:403
  113.1 3.6 %all-to-all-start.3 = ((bf16[8,20,32,128]{3,2,1,0:T(8,128)(2,1)}), bf16[8,20,32,128]{3,2,1,0:T(8,128)(2,1)S(1)}, u32[]{:S(2)}, u32[]{:S(2)}) async-start(bf16[8,20,32,128]{3,2,1,0:T(8,128)(2,1)} %shard_map.67), calls=%async_computation.3 | async-start | bytes 2621440 | tf_op jit(solution)/shard_map/all_to_all | solution.py:403
  117.4 0.0 copy-done.7
  117.4 0.1 fusion.3
  117.5 3.3 %collective-permute-start.4 = (bf16[8,16,16,128]{3,2,1,0:T(8,128)(2,1)S(1)}, bf16[8,16,16,128]{3,2,1,0:T(8,128)(2,1)S(1)}, u32[]{:S(2)}, u32[]{:S(2)}) collective-permute-start(bf16[8,16,16,128]{3,2,1,0:T(8,128)(2,1)S(1)} %shard_map.64.mine), channel_id=1, source_target_pairs={{16,0},{24,8},{32,16},{40,24},{48,32},{56,40},{64,48},{72,56},{80,... | collective-permute-start | bytes 1572872 | tf_op jit(solution)/shard_map/ppermute | solution.py:399
  120.9 0.7 iota_reduce_fusion
  121.5 0.1 pad_add_fusion.info
  121.6 10.9 %collective-permute-done.4.other = bf16[8,16,16,128]{3,2,1,0:T(8,128)(2,1)S(1)} collective-permute-done((bf16[8,16,16,128]{3,2,1,0:T(8,128)(2,1)S(1)}, bf16[8,16,16,128]{3,2,1,0:T(8,128)(2,1)S(1)}, u32[]{:S(2)}, u32[]{:S(2)}) %collective-permute-start.4) | collective-permute-done | bytes 524320 | tf_op jit(solution)/shard_map/ppermute | solution.py:399
  132.5 0.9 copy-done.2
  133.4 5.5 %shard_map.68.same = f32[16,208,128]{2,1,0:T(8,128)S(1)} custom-call(s32[1]{0:T(128)} %bitcast.4.first, bf16[8,16,16,128]{3,2,1,0:T(8,128)(2,1)S(1)} %shard_map.64.mine, bf16[8,16,16,128]{3,2,1,0:T(8,128)(2,1)S(1)} %collective-permute-done.4.other, bf16[208,256]{1,0:T(8,128)(2,1)S(1)} %copy-done.2), custom_call_target="tpu_custom_call" | custom-call | tf_op jit(solution)/shard_map/pallas_call | solution.py:222
  138.9 0.0 copy-done.1
  138.9 0.0 copy-start.3
  138.9 0.9 copy-done.3
  139.8 3.6 %shard_map.66.begun = bf16[4,201,16,128]{3,2,1,0:T(8,128)(2,1)} custom-call(s32[9]{0:T(128)S(1)} %pad_add_fusion.info, bf16[8,32,16,128]{3,2,1,0:T(8,128)(2,1)S(1)} %copy-done.1, bf16[208,256]{1,0:T(8,128)(2,1)S(1)} %copy-done.3), custom_call_target="tpu_custom_call" | custom-call | tf_op jit(solution)/shard_map/pallas_call | solution.py:279
  143.4 8.0 %all-to-all-done.3.far = bf16[8,20,32,128]{3,2,1,0:T(8,128)(2,1)S(1)} async-done(((bf16[8,20,32,128]{3,2,1,0:T(8,128)(2,1)}), bf16[8,20,32,128]{3,2,1,0:T(8,128)(2,1)S(1)}, u32[]{:S(2)}, u32[]{:S(2)}) %all-to-all-start.3) | async-done | bytes 1310752 | tf_op jit(solution)/shard_map/all_to_all | solution.py:403
  151.5 2.9 %shard_map.69 = bf16[4,201,16,128]{3,2,1,0:T(8,128)(2,1)} custom-call(s32[9]{0:T(128)S(1)} %pad_add_fusion.info, bf16[4,201,16,128]{3,2,1,0:T(8,128)(2,1)} %shard_map.66.begun, f32[16,208,128]{2,1,0:T(8,128)S(1)} %shard_map.68.same, bf16[8,20,32,128]{3,2,1,0:T(8,128)(2,1)S(1)} %all-to-all-done.3.far, ...), custom_call_target="tpu_custom_call", output_to_operand_aliasing={{}: (1, {})} | custom-call | tf_op jit(solution)/shard_map/pallas_call | solution.py:374
  (12 shorter events, 0.0 us)
Async XLA Ops:
  0.0 39.1 %copy-start.5 = (bf16[256,256]{1,0:T(8,128)(2,1)S(1)}, bf16[256,256]{1,0:T(8,128)(2,1)}, u32[]{:S(2)}) copy-start(bf16[256,256]{1,0:T(8,128)(2,1)} %constant.29.clone.forward) | copy-start | bytes 393220
  0.0 39.1 %copy-start.6 = (s32[64]{0:T(128)S(1)}, s32[64]{0:T(128)}, u32[]{:S(2)}) copy-start(s32[64]{0:T(128)} %starts.1) | copy-start | bytes 772
  68.8 10.5 %collective-permute-start = (bf16[8,16,16,128]{3,2,1,0:T(8,128)(2,1)S(1)}, bf16[8,16,16,128]{3,2,1,0:T(8,128)(2,1)S(1)}, u32[]{:S(2)}, u32[]{:S(2)}) collective-permute-start(bf16[8,16,16,128]{3,2,1,0:T(8,128)(2,1)S(1)} %all_to_all.21.own), channel_id=1, source_target_pairs={{8,0},{16,8},{24,16},{32,24},{40,32},{48,40},{56,48},{64,56},{72,6... | collective-permute-start | bytes 1572872 | tf_op jit(solution)/shard_map/ppermute | solution.py:399
  80.8 32.4 %all-to-all-start.2 = ((bf16[8,32,16,128]{3,2,1,0:T(8,128)(2,1)}), bf16[8,32,16,128]{3,2,1,0:T(8,128)(2,1)S(1)}, u32[]{:S(2)}, u32[]{:S(2)}) async-start(bf16[8,32,16,128]{3,2,1,0:T(8,128)(2,1)} %shard_map.65), calls=%async_computation.2 | async-start | bytes 2097152 | tf_op jit(solution)/shard_map/all_to_all | solution.py:403
  84.3 15.1 %collective-permute-start.2 = (bf16[8,16,16,128]{3,2,1,0:T(8,128)(2,1)S(1)}, bf16[8,16,16,128]{3,2,1,0:T(8,128)(2,1)S(1)}, u32[]{:S(2)}, u32[]{:S(2)}) collective-permute-start(bf16[8,16,16,128]{3,2,1,0:T(8,128)(2,1)S(1)} %all_to_all.21.own), channel_id=1, source_target_pairs={{24,8},{40,24},{56,40},{72,56},{88,72},{104,88},{120,104},{136,120... | collective-permute-start | bytes 1572872 | tf_op jit(solution)/shard_map/ppermute | solution.py:399
  89.0 10.4 %collective-permute-start.1 = (bf16[8,16,16,128]{3,2,1,0:T(8,128)(2,1)S(1)}, bf16[8,16,16,128]{3,2,1,0:T(8,128)(2,1)S(1)}, u32[]{:S(2)}, u32[]{:S(2)}) collective-permute-start(bf16[8,16,16,128]{3,2,1,0:T(8,128)(2,1)S(1)} %collective-permute-done.next1), channel_id=1, source_target_pairs={{8,0},{24,16},{40,32},{56,48},{72,64},{88,80},{104,96},{120,112},{... | collective-permute-start | bytes 1572872 | tf_op jit(solution)/shard_map/ppermute | solution.py:399
  90.4 9.1 %collective-permute-start.3 = (bf16[3,16,16,128]{3,2,1,0:T(8,128)(2,1)S(1)}, bf16[3,16,16,128]{3,2,1,0:T(8,128)(2,1)S(1)}, u32[]{:S(2)}, u32[]{:S(2)}) collective-permute-start(bf16[3,16,16,128]{3,2,1,0:T(8,128)(2,1)S(1)} %slice.12), channel_id=1, source_target_pairs={{24,0},{32,8},{40,16},{48,24},{56,32},{64,40},{72,48},{80,56},{88,... | collective-permute-start | bytes 589832 | tf_op jit(solution)/shard_map/ppermute | solution.py:399
  105.3 12.1 %copy-start.7 = (s32[1,4]{1,0:T(1,128)S(1)}, s32[1,4]{1,0:T(1,128)}, u32[]{:S(2)}) copy-start(s32[1,4]{1,0:T(1,128)} %param.8) | copy-start | bytes 52
  113.1 8.5 %copy-start = (bf16[8,32,16,128]{3,2,1,0:T(8,128)(2,1)}, bf16[8,32,16,128]{3,2,1,0:T(8,128)(2,1)S(1)}, u32[]{:S(2)}) copy-start(bf16[8,32,16,128]{3,2,1,0:T(8,128)(2,1)S(1)} %all-to-all-done.2.near) | copy-start | bytes 3145732
  113.1 38.3 %all-to-all-start.3 = ((bf16[8,20,32,128]{3,2,1,0:T(8,128)(2,1)}), bf16[8,20,32,128]{3,2,1,0:T(8,128)(2,1)S(1)}, u32[]{:S(2)}, u32[]{:S(2)}) async-start(bf16[8,20,32,128]{3,2,1,0:T(8,128)(2,1)} %shard_map.67), calls=%async_computation.3 | async-start | bytes 2621440 | tf_op jit(solution)/shard_map/all_to_all | solution.py:403
  117.5 15.0 %collective-permute-start.4 = (bf16[8,16,16,128]{3,2,1,0:T(8,128)(2,1)S(1)}, bf16[8,16,16,128]{3,2,1,0:T(8,128)(2,1)S(1)}, u32[]{:S(2)}, u32[]{:S(2)}) collective-permute-start(bf16[8,16,16,128]{3,2,1,0:T(8,128)(2,1)S(1)} %shard_map.64.mine), channel_id=1, source_target_pairs={{16,0},{24,8},{32,16},{40,24},{48,32},{56,40},{64,48},{72,56},{80,... | collective-permute-start | bytes 1572872 | tf_op jit(solution)/shard_map/ppermute | solution.py:399
  132.5 0.9 copy-start.2
  133.4 5.5 %copy-start.1 = (bf16[8,32,16,128]{3,2,1,0:T(8,128)(2,1)S(1)}, bf16[8,32,16,128]{3,2,1,0:T(8,128)(2,1)}, u32[]{:S(2)}) copy-start(bf16[8,32,16,128]{3,2,1,0:T(8,128)(2,1)} %copy-done) | copy-start | bytes 3145732
  138.9 0.9 copy-start.3
  139.8 11.6 %copy-start.4 = (bf16[208,256]{1,0:T(8,128)(2,1)S(1)}, bf16[208,256]{1,0:T(8,128)(2,1)}, u32[]{:S(2)}) copy-start(bf16[208,256]{1,0:T(8,128)(2,1)} %constant.30.clone.inverse) | copy-start | bytes 319492

commit v6 on v5

--- a/solution.py
+++ b/solution.py
@@ -98,7 +98,7 @@
         return carry
 
     lax.fori_loop(0, rows // 2, transform, 0, unroll=True)
-    out[...] = white[...].astype(jnp.bfloat16).reshape(out.shape)
+    out[...] = white[: HALF * rows].astype(jnp.bfloat16).reshape(out.shape)
 
 
 def whitened_rows(starts, series, forward, bands):
@@ -114,9 +114,9 @@
         ],
         out_specs=pl.BlockSpec(memory_space=pltpu.VMEM),
         scratch_shapes=[
-            pltpu.VMEM((rows * NWIN, LANES), jnp.float32),
-            pltpu.VMEM((rows * NWIN, LANES), jnp.float32),
-            pltpu.VMEM((HALF * rows, LANES), jnp.float32),
+            pltpu.VMEM(((rows + 1) * NWIN, LANES), jnp.float32),
+            pltpu.VMEM(((rows + 1) * NWIN, LANES), jnp.float32),
+            pltpu.VMEM(((HALF + 1) * rows, LANES), jnp.float32),
         ],
         compiler_params=pltpu.CompilerParams(vmem_limit_bytes=16 * MIB),
     )(starts, series, forward)
@@ -183,8 +183,8 @@
         return carry
 
     lax.fori_loop(0, width, one, 0, unroll=True)
-    out[:, :rows] = held0[...].astype(jnp.bfloat16).reshape(bands, rows, step, LANES)
-    out[:, rows:] = held1[...].astype(jnp.bfloat16).reshape(bands, UNITS, step, LANES)
+    out[:, :rows] = held0[: CB * step].astype(jnp.bfloat16).reshape(bands, rows, step, LANES)
+    out[:, rows:] = held1[: bands * UNITS * step].astype(jnp.bfloat16).reshape(bands, UNITS, step, LANES)
 
 
 def local_kernel(first, mine, other, inverse, out, held):
@@ -255,7 +255,7 @@
                 act(pltpu.make_async_copy(source, out.at[slot], sems.at[slot]))
 
     copy(2, blank, lambda c: c.start())
-    wide[...] = near[...].astype(jnp.float32).reshape(wide.shape)
+    wide[: depth * rows] = near[...].astype(jnp.float32).reshape(depth * rows, LANES)
 
     def one(pair, carry):
         pieces = [
@@ -268,7 +268,7 @@
         return carry
 
     lax.fori_loop(0, rows // 2, one, 0, unroll=True)
-    done[...] = held[...].astype(jnp.bfloat16).reshape(done.shape)
+    done[...] = held[: LAGS * rows].astype(jnp.bfloat16).reshape(done.shape)
     copy(1, done, lambda c: c.start())
     copy(1, done, lambda c: c.wait())
     copy(2, blank, lambda c: c.wait())
@@ -286,8 +286,8 @@
         ],
         out_specs=pl.BlockSpec(memory_space=pltpu.HBM),
         scratch_shapes=[
-            pltpu.VMEM((WIN * rows, LANES), jnp.float32),
-            pltpu.VMEM((LAGS * rows, LANES), jnp.float32),
+            pltpu.VMEM(((WIN + 1) * rows, LANES), jnp.float32),
+            pltpu.VMEM(((LAGS + 1) * rows, LANES), jnp.float32),
             pltpu.VMEM((LAGS, rows, LANES), jnp.bfloat16),
             pltpu.VMEM((LAGS, rows, LANES), jnp.bfloat16),
             pltpu.SemaphoreType.DMA((TMAX,)),
@@ -330,7 +330,8 @@
         held[place, pl.ds(row, LAGS, stride=rows), :] = value[:LAGS]
 
     def finish(place, offset):
-        done[place] = held[place].astype(jnp.bfloat16).reshape(LAGS, rows, LANES)
+        values = held[place, : LAGS * rows]
+        done[place] = values.astype(jnp.bfloat16).reshape(LAGS, rows, LANES)
         slot = info[offset]
 
         @pl.when(slot < TMAX)
@@ -383,7 +384,7 @@
         ],
         out_specs=pl.BlockSpec(memory_space=pltpu.HBM),
         scratch_shapes=[
-            pltpu.VMEM((3, LAGS * rows, LANES), jnp.float32),
+            pltpu.VMEM((3, (LAGS + 1) * rows, LANES), jnp.float32),
             pltpu.VMEM((UNITS + rows, LAG_ROWS, LANES), jnp.float32),
             pltpu.VMEM((3, LAGS, rows, LANES), jnp.bfloat16),
             pltpu.SemaphoreType.DMA((3,)),
@@ -421,9 +422,9 @@
         far_kernel,
         (bands, rows + UNITS, 2 * width, LANES),
         [
-            (CB * 2 * width, LANES),
-            (bands * UNITS * 2 * width, LANES),
-            (CB * 2 * width, LANES),
+            ((CB + 1) * 2 * width, LANES),
+            ((bands + 1) * UNITS * 2 * width, LANES),
+            ((CB + 1) * 2 * width, LANES),
         ],
         24 * MIB,
         own,

time: 156 us -> 156 us (level)
  transfers between devices with their start and end apart: 7 -> 7, of which waited for: 5 -> 5; matrix products, arithmetic and copies ran while one was open for 1% -> 1% of each run, Pallas kernels for 10% -> 9%
where the time goes in v6:
time: 156 us; the launch traced here: 155 us
  blocking collectives  66.3 us (42%)
  waiting for transfers between devices  42 us (27%)
  Pallas kernels  22.2 us (14%)
  starting transfers between devices  21.3 us (14%)
  local copies, waits for them, and re-layouts  1.82 us (1%)
    all_to_all x2, blocking collectives, exchanged(): return lax.all_to_all(block, axis, split_axis=0, concat_axis=0, tiled=True)  66.3 us
    ppermute x5, waiting for transfers between devices, from_ahead(): return lax.ppermute(block, 'chan', route)  25.6 us
    all_to_all x2, waiting for transfers between devices, exchanged(): return lax.all_to_all(block, axis, split_axis=0, concat_axis=0, tiled=True)  16.4 us
    ppermute x5, starting transfers between devices, from_ahead(): return lax.ppermute(block, 'chan', route)  14.2 us
    pallas_call x2, Pallas kernels, vmem_call(): pl.pallas_call(kernel, out_shape=jax.ShapeDtypeStruct(out_shape, jnp.bflo...  7.33 us
    all_to_all x2, starting transfers between devices, exchanged(): return lax.all_to_all(block, axis, split_axis=0, concat_axis=0, tiled=True)  7.13 us
    pallas_call x1, Pallas kernels, local_lags(): pl.pallas_call(local_kernel, out_shape=jax.ShapeDtypeStruct((mine.shape[2...  5.49 us
    pallas_call x1, Pallas kernels, lags(): pl.pallas_call(lag_kernel, out_shape=jax.ShapeDtypeStruct(begun.shape, be...  3.83 us
  transfers between devices with their start and end apart: 7, of which 5 were waited for; matrix products, arithmetic and copies ran while one was open for 1% of the time, Pallas kernels for 9%

profile of v6, /device:TPU:9, one launch (start us, length us, event | category | flops | bytes accessed | tf_op | source)
XLA Modules:
  0.0 155.4 jit_solution(6209161747867385842)
XLA Ops:
  0.0 39.0 %all_to_all.20.traces = bf16[64,16,512]{2,1,0:T(8,128)(2,1)S(1)} all-to-all(bf16[64,16,512]{2,1,0:T(8,128)(2,1)} %param.6), channel_id=1, replica_groups=mesh['chan'=64,'band'=8] {'chan'}, dimensions={0} | all-to-all | bytes 2097152 | tf_op jit(solution)/shard_map/all_to_all | solution.py:404
  39.1 0.0 copy-done.5
  39.1 2.5 %shard_map.64.mine = bf16[8,16,16,128]{3,2,1,0:T(8,128)(2,1)S(1)} custom-call(s32[64]{0:T(128)S(1)} %copy-done.6, bf16[64,16,512]{2,1,0:T(8,128)(2,1)S(1)} %all_to_all.20.traces, bf16[256,256]{1,0:T(8,128)(2,1)S(1)} %copy-done.5), custom_call_target="tpu_custom_call" | custom-call | tf_op jit(solution)/shard_map/pallas_call | solution.py:107
  41.5 27.3 %all_to_all.21.own = bf16[8,16,16,128]{3,2,1,0:T(8,128)(2,1)S(1)} all-to-all(bf16[8,16,16,128]{3,2,1,0:T(8,128)(2,1)S(1)} %shard_map.64.mine), channel_id=1, replica_groups=mesh['chan'=64,'band'=8] {'band'}, dimensions={0} | all-to-all | bytes 1048576 | tf_op jit(solution)/shard_map/all_to_all | solution.py:404
  68.8 2.9 %collective-permute-start = (bf16[8,16,16,128]{3,2,1,0:T(8,128)(2,1)S(1)}, bf16[8,16,16,128]{3,2,1,0:T(8,128)(2,1)S(1)}, u32[]{:S(2)}, u32[]{:S(2)}) collective-permute-start(bf16[8,16,16,128]{3,2,1,0:T(8,128)(2,1)S(1)} %all_to_all.21.own), channel_id=1, source_target_pairs={{8,0},{16,8},{24,16},{32,24},{40,32},{48,40},{56,48},{64,56},{72,6... | collective-permute-start | bytes 1572872 | tf_op jit(solution)/shard_map/ppermute | solution.py:400
  71.7 7.6 %collective-permute-done.next1 = bf16[8,16,16,128]{3,2,1,0:T(8,128)(2,1)S(1)} collective-permute-done((bf16[8,16,16,128]{3,2,1,0:T(8,128)(2,1)S(1)}, bf16[8,16,16,128]{3,2,1,0:T(8,128)(2,1)S(1)}, u32[]{:S(2)}, u32[]{:S(2)}) %collective-permute-start) | collective-permute-done | bytes 524320 | tf_op jit(solution)/shard_map/ppermute | solution.py:400
  79.3 1.5 shard_map.65
  80.8 3.6 %all-to-all-start.2 = ((bf16[8,32,16,128]{3,2,1,0:T(8,128)(2,1)}), bf16[8,32,16,128]{3,2,1,0:T(8,128)(2,1)S(1)}, u32[]{:S(2)}, u32[]{:S(2)}) async-start(bf16[8,32,16,128]{3,2,1,0:T(8,128)(2,1)} %shard_map.65), calls=%async_computation.2 | async-start | bytes 2097152 | tf_op jit(solution)/shard_map/all_to_all | solution.py:404
  84.3 4.7 %collective-permute-start.2 = (bf16[8,16,16,128]{3,2,1,0:T(8,128)(2,1)S(1)}, bf16[8,16,16,128]{3,2,1,0:T(8,128)(2,1)S(1)}, u32[]{:S(2)}, u32[]{:S(2)}) collective-permute-start(bf16[8,16,16,128]{3,2,1,0:T(8,128)(2,1)S(1)} %all_to_all.21.own), channel_id=1, source_target_pairs={{24,8},{40,24},{56,40},{72,56},{88,72},{104,88},{120,104},{136,120... | collective-permute-start | bytes 1572872 | tf_op jit(solution)/shard_map/ppermute | solution.py:400
  89.0 1.3 collective-permute-start.1
  90.3 1.9 %collective-permute-start.3 = (bf16[3,16,16,128]{3,2,1,0:T(8,128)(2,1)S(1)}, bf16[3,16,16,128]{3,2,1,0:T(8,128)(2,1)S(1)}, u32[]{:S(2)}, u32[]{:S(2)}) collective-permute-start(bf16[3,16,16,128]{3,2,1,0:T(8,128)(2,1)S(1)} %slice.12), channel_id=1, source_target_pairs={{24,0},{32,8},{40,16},{48,24},{56,32},{64,40},{72,48},{80,56},{88,... | collective-permute-start | bytes 589832 | tf_op jit(solution)/shard_map/ppermute | solution.py:400
  92.3 7.2 %collective-permute-done.3.next3 = bf16[3,16,16,128]{3,2,1,0:T(8,128)(2,1)S(1)} collective-permute-done((bf16[3,16,16,128]{3,2,1,0:T(8,128)(2,1)S(1)}, bf16[3,16,16,128]{3,2,1,0:T(8,128)(2,1)S(1)}, u32[]{:S(2)}, u32[]{:S(2)}) %collective-permute-start.3) | collective-permute-done | bytes 196640 | tf_op jit(solution)/shard_map/ppermute | solution.py:400
  99.4 0.0 collective-permute-done.2.next2_odd
  99.4 0.0 collective-permute-done.1.next2_even
  99.4 5.9 %shard_map.67 = bf16[8,20,32,128]{3,2,1,0:T(8,128)(2,1)} custom-call(bf16[8,16,16,128]{3,2,1,0:T(8,128)(2,1)S(1)} %all_to_all.21.own, bf16[8,16,16,128]{3,2,1,0:T(8,128)(2,1)S(1)} %collective-permute-done.1.next2_even, bf16[8,16,16,128]{3,2,1,0:T(8,128)(2,1)S(1)} %collective-permute-done.2.next2_odd, bf16[3,16,16,128]{3,2,1,0:T(8,128)(2,1)S(1)} %collective-permute-done.3.next3), custom_call_target="tpu_custom_call" | custom-call | tf_op jit(solution)/shard_map/pallas_call | solution.py:234
  105.3 7.8 %all-to-all-done.2.near = bf16[8,32,16,128]{3,2,1,0:T(8,128)(2,1)S(1)} async-done(((bf16[8,32,16,128]{3,2,1,0:T(8,128)(2,1)}), bf16[8,32,16,128]{3,2,1,0:T(8,128)(2,1)S(1)}, u32[]{:S(2)}, u32[]{:S(2)}) %all-to-all-start.2) | async-done | bytes 1048608 | tf_op jit(solution)/shard_map/all_to_all | solution.py:404
  113.1 3.6 %all-to-all-start.3 = ((bf16[8,20,32,128]{3,2,1,0:T(8,128)(2,1)}), bf16[8,20,32,128]{3,2,1,0:T(8,128)(2,1)S(1)}, u32[]{:S(2)}, u32[]{:S(2)}) async-start(bf16[8,20,32,128]{3,2,1,0:T(8,128)(2,1)} %shard_map.67), calls=%async_computation.3 | async-start | bytes 2621440 | tf_op jit(solution)/shard_map/all_to_all | solution.py:404
  117.4 0.0 copy-done.7
  117.4 0.1 fusion.3
  117.5 3.3 %collective-permute-start.4 = (bf16[8,16,16,128]{3,2,1,0:T(8,128)(2,1)S(1)}, bf16[8,16,16,128]{3,2,1,0:T(8,128)(2,1)S(1)}, u32[]{:S(2)}, u32[]{:S(2)}) collective-permute-start(bf16[8,16,16,128]{3,2,1,0:T(8,128)(2,1)S(1)} %shard_map.64.mine), channel_id=1, source_target_pairs={{16,0},{24,8},{32,16},{40,24},{48,32},{56,40},{64,48},{72,56},{80,... | collective-permute-start | bytes 1572872 | tf_op jit(solution)/shard_map/ppermute | solution.py:400
  120.8 0.7 iota_reduce_fusion
  121.5 0.1 pad_add_fusion.info
  121.6 10.9 %collective-permute-done.4.other = bf16[8,16,16,128]{3,2,1,0:T(8,128)(2,1)S(1)} collective-permute-done((bf16[8,16,16,128]{3,2,1,0:T(8,128)(2,1)S(1)}, bf16[8,16,16,128]{3,2,1,0:T(8,128)(2,1)S(1)}, u32[]{:S(2)}, u32[]{:S(2)}) %collective-permute-start.4) | collective-permute-done | bytes 524320 | tf_op jit(solution)/shard_map/ppermute | solution.py:400
  132.5 0.9 copy-done.2
  133.4 5.5 %shard_map.68.same = f32[16,208,128]{2,1,0:T(8,128)S(1)} custom-call(s32[1]{0:T(128)} %bitcast.4.first, bf16[8,16,16,128]{3,2,1,0:T(8,128)(2,1)S(1)} %shard_map.64.mine, bf16[8,16,16,128]{3,2,1,0:T(8,128)(2,1)S(1)} %collective-permute-done.4.other, bf16[208,256]{1,0:T(8,128)(2,1)S(1)} %copy-done.2), custom_call_target="tpu_custom_call" | custom-call | tf_op jit(solution)/shard_map/pallas_call | solution.py:222
  138.9 0.0 copy-done.1
  138.9 0.0 copy-start.3
  138.9 0.9 copy-done.3
  139.8 3.1 %shard_map.66.begun = bf16[4,201,16,128]{3,2,1,0:T(8,128)(2,1)} custom-call(s32[9]{0:T(128)S(1)} %pad_add_fusion.info, bf16[8,32,16,128]{3,2,1,0:T(8,128)(2,1)S(1)} %copy-done.1, bf16[208,256]{1,0:T(8,128)(2,1)S(1)} %copy-done.3), custom_call_target="tpu_custom_call" | custom-call | tf_op jit(solution)/shard_map/pallas_call | solution.py:279
  142.9 8.6 %all-to-all-done.3.far = bf16[8,20,32,128]{3,2,1,0:T(8,128)(2,1)S(1)} async-done(((bf16[8,20,32,128]{3,2,1,0:T(8,128)(2,1)}), bf16[8,20,32,128]{3,2,1,0:T(8,128)(2,1)S(1)}, u32[]{:S(2)}, u32[]{:S(2)}) %all-to-all-start.3) | async-done | bytes 1310752 | tf_op jit(solution)/shard_map/all_to_all | solution.py:404
  151.4 0.0 copy-done.4
  151.4 3.8 %shard_map.69 = bf16[4,201,16,128]{3,2,1,0:T(8,128)(2,1)} custom-call(s32[9]{0:T(128)S(1)} %pad_add_fusion.info, bf16[4,201,16,128]{3,2,1,0:T(8,128)(2,1)} %shard_map.66.begun, f32[16,208,128]{2,1,0:T(8,128)S(1)} %shard_map.68.same, bf16[8,20,32,128]{3,2,1,0:T(8,128)(2,1)S(1)} %all-to-all-done.3.far, ...), custom_call_target="tpu_custom_call", output_to_operand_aliasing={{}: (1, {})} | custom-call | tf_op jit(solution)/shard_map/pallas_call | solution.py:375
  (12 shorter events, 0.0 us)
Async XLA Ops:
  0.0 39.1 %copy-start.5 = (bf16[256,256]{1,0:T(8,128)(2,1)S(1)}, bf16[256,256]{1,0:T(8,128)(2,1)}, u32[]{:S(2)}) copy-start(bf16[256,256]{1,0:T(8,128)(2,1)} %constant.29.clone.forward) | copy-start | bytes 393220
  0.0 39.1 %copy-start.6 = (s32[64]{0:T(128)S(1)}, s32[64]{0:T(128)}, u32[]{:S(2)}) copy-start(s32[64]{0:T(128)} %starts.1) | copy-start | bytes 772
  68.8 10.5 %collective-permute-start = (bf16[8,16,16,128]{3,2,1,0:T(8,128)(2,1)S(1)}, bf16[8,16,16,128]{3,2,1,0:T(8,128)(2,1)S(1)}, u32[]{:S(2)}, u32[]{:S(2)}) collective-permute-start(bf16[8,16,16,128]{3,2,1,0:T(8,128)(2,1)S(1)} %all_to_all.21.own), channel_id=1, source_target_pairs={{8,0},{16,8},{24,16},{32,24},{40,32},{48,40},{56,48},{64,56},{72,6... | collective-permute-start | bytes 1572872 | tf_op jit(solution)/shard_map/ppermute | solution.py:400
  80.8 32.4 %all-to-all-start.2 = ((bf16[8,32,16,128]{3,2,1,0:T(8,128)(2,1)}), bf16[8,32,16,128]{3,2,1,0:T(8,128)(2,1)S(1)}, u32[]{:S(2)}, u32[]{:S(2)}) async-start(bf16[8,32,16,128]{3,2,1,0:T(8,128)(2,1)} %shard_map.65), calls=%async_computation.2 | async-start | bytes 2097152 | tf_op jit(solution)/shard_map/all_to_all | solution.py:404
  84.3 15.1 %collective-permute-start.2 = (bf16[8,16,16,128]{3,2,1,0:T(8,128)(2,1)S(1)}, bf16[8,16,16,128]{3,2,1,0:T(8,128)(2,1)S(1)}, u32[]{:S(2)}, u32[]{:S(2)}) collective-permute-start(bf16[8,16,16,128]{3,2,1,0:T(8,128)(2,1)S(1)} %all_to_all.21.own), channel_id=1, source_target_pairs={{24,8},{40,24},{56,40},{72,56},{88,72},{104,88},{120,104},{136,120... | collective-permute-start | bytes 1572872 | tf_op jit(solution)/shard_map/ppermute | solution.py:400
  89.0 10.4 %collective-permute-start.1 = (bf16[8,16,16,128]{3,2,1,0:T(8,128)(2,1)S(1)}, bf16[8,16,16,128]{3,2,1,0:T(8,128)(2,1)S(1)}, u32[]{:S(2)}, u32[]{:S(2)}) collective-permute-start(bf16[8,16,16,128]{3,2,1,0:T(8,128)(2,1)S(1)} %collective-permute-done.next1), channel_id=1, source_target_pairs={{8,0},{24,16},{40,32},{56,48},{72,64},{88,80},{104,96},{120,112},{... | collective-permute-start | bytes 1572872 | tf_op jit(solution)/shard_map/ppermute | solution.py:400
  90.3 9.1 %collective-permute-start.3 = (bf16[3,16,16,128]{3,2,1,0:T(8,128)(2,1)S(1)}, bf16[3,16,16,128]{3,2,1,0:T(8,128)(2,1)S(1)}, u32[]{:S(2)}, u32[]{:S(2)}) collective-permute-start(bf16[3,16,16,128]{3,2,1,0:T(8,128)(2,1)S(1)} %slice.12), channel_id=1, source_target_pairs={{24,0},{32,8},{40,16},{48,24},{56,32},{64,40},{72,48},{80,56},{88,... | collective-permute-start | bytes 589832 | tf_op jit(solution)/shard_map/ppermute | solution.py:400
  105.3 12.1 %copy-start.7 = (s32[1,4]{1,0:T(1,128)S(1)}, s32[1,4]{1,0:T(1,128)}, u32[]{:S(2)}) copy-start(s32[1,4]{1,0:T(1,128)} %param.8) | copy-start | bytes 52
  113.1 8.5 %copy-start = (bf16[8,32,16,128]{3,2,1,0:T(8,128)(2,1)}, bf16[8,32,16,128]{3,2,1,0:T(8,128)(2,1)S(1)}, u32[]{:S(2)}) copy-start(bf16[8,32,16,128]{3,2,1,0:T(8,128)(2,1)S(1)} %all-to-all-done.2.near) | copy-start | bytes 3145732
  113.1 38.3 %all-to-all-start.3 = ((bf16[8,20,32,128]{3,2,1,0:T(8,128)(2,1)}), bf16[8,20,32,128]{3,2,1,0:T(8,128)(2,1)S(1)}, u32[]{:S(2)}, u32[]{:S(2)}) async-start(bf16[8,20,32,128]{3,2,1,0:T(8,128)(2,1)} %shard_map.67), calls=%async_computation.3 | async-start | bytes 2621440 | tf_op jit(solution)/shard_map/all_to_all | solution.py:404
  117.5 15.0 %collective-permute-start.4 = (bf16[8,16,16,128]{3,2,1,0:T(8,128)(2,1)S(1)}, bf16[8,16,16,128]{3,2,1,0:T(8,128)(2,1)S(1)}, u32[]{:S(2)}, u32[]{:S(2)}) collective-permute-start(bf16[8,16,16,128]{3,2,1,0:T(8,128)(2,1)S(1)} %shard_map.64.mine), channel_id=1, source_target_pairs={{16,0},{24,8},{32,16},{40,24},{48,32},{56,40},{64,48},{72,56},{80,... | collective-permute-start | bytes 1572872 | tf_op jit(solution)/shard_map/ppermute | solution.py:400
  132.5 0.9 copy-start.2
  133.4 5.5 %copy-start.1 = (bf16[8,32,16,128]{3,2,1,0:T(8,128)(2,1)S(1)}, bf16[8,32,16,128]{3,2,1,0:T(8,128)(2,1)}, u32[]{:S(2)}) copy-start(bf16[8,32,16,128]{3,2,1,0:T(8,128)(2,1)} %copy-done) | copy-start | bytes 3145732
  138.9 0.9 copy-start.3
  139.8 11.6 %copy-start.4 = (bf16[208,256]{1,0:T(8,128)(2,1)S(1)}, bf16[208,256]{1,0:T(8,128)(2,1)}, u32[]{:S(2)}) copy-start(bf16[208,256]{1,0:T(8,128)(2,1)} %constant.30.clone.inverse) | copy-start | bytes 319492

commit v7 on v6

--- a/solution.py
+++ b/solution.py
@@ -123,9 +123,9 @@
 
 
 def both_sides(own, f):
-    mine = own[:, f].reshape(CB, LANES)
+    mine = own[:, f].reshape(own.shape[0] * own.shape[2], LANES)
     wide = mine.astype(jnp.float32)
-    lane = lax.broadcasted_iota(jnp.int32, (CB, LANES), 1)
+    lane = lax.broadcasted_iota(jnp.int32, mine.shape, 1)
     turned = pltpu.roll(wide, NWIN, 1)
     turned = jnp.where(lane < NWIN, -turned, turned).astype(jnp.bfloat16)
     return mine, jnp.concatenate([mine, turned], axis=0)
@@ -143,6 +143,22 @@
         return carry
 
     lax.fori_loop(0, width, one, 0, unroll=True)
+
+
+def near_cross(own, next1):
+    bands, width, rows = own.shape[:3]
+    part = bands // 2
+    return pl.pallas_call(
+        near_kernel,
+        out_shape=jax.ShapeDtypeStruct((bands, 2 * width, rows, LANES), jnp.bfloat16),
+        grid=(2,),
+        in_specs=[
+            pl.BlockSpec((part, width, rows, LANES), lambda g: (g, 0, 0, 0)),
+            pl.BlockSpec(own.shape, lambda g: (0, 0, 0, 0)),
+        ],
+        out_specs=pl.BlockSpec((part, 2 * width, rows, LANES), lambda g: (g, 0, 0, 0)),
+        compiler_params=pltpu.CompilerParams(vmem_limit_bytes=16 * MIB),
+    )(own, next1)
 
 
 def far_kernel(own, next2_even, next2_odd, next3, out, held0, held1, plain):
@@ -416,7 +432,7 @@
     next2 = (from_ahead(next1, 1, 0), from_ahead(own, 2, 1))
     reach = -(-(RANGE - 2 * CB) // rows)
     next3 = from_ahead(own[:reach], 3)
-    near = vmem_call(near_kernel, (bands, 2 * width, rows, LANES), [], 16 * MIB, own, next1)
+    near = near_cross(own, next1)
     near = exchanged(near, "band")
     far = vmem_call(
         far_kernel,

time: 156 us -> 156 us (level)
    pallas_call x0 -> x1, Pallas kernels: none -> 1.81 us  [near_cross(): pl.pallas_call(near_kernel, out_shape=jax.ShapeDtypeStruct((bands, 2 * wi...]
    pallas_call x2 -> x1, Pallas kernels: 7.33 us -> 5.87 us  [vmem_call(): pl.pallas_call(kernel, out_shape=jax.ShapeDtypeStruct(out_shape, jnp.bflo...]
  transfers between devices with their start and end apart: 7 -> 7, of which waited for: 5 -> 5; matrix products, arithmetic and copies ran while one was open for 1% -> 1% of each run, Pallas kernels for 9% -> 10%
where the time goes in v7:
time: 156 us; the launch traced here: 155 us
  blocking collectives  66.3 us (42%)
  waiting for transfers between devices  41.5 us (27%)
  Pallas kernels  22.2 us (14%)
  starting transfers between devices  21.3 us (14%)
  local copies, waits for them, and re-layouts  1.82 us (1%)
    all_to_all x2, blocking collectives, exchanged(): return lax.all_to_all(block, axis, split_axis=0, concat_axis=0, tiled=True)  66.3 us
    ppermute x5, waiting for transfers between devices, from_ahead(): return lax.ppermute(block, 'chan', route)  25.6 us
    all_to_all x2, waiting for transfers between devices, exchanged(): return lax.all_to_all(block, axis, split_axis=0, concat_axis=0, tiled=True)  15.9 us
    ppermute x5, starting transfers between devices, from_ahead(): return lax.ppermute(block, 'chan', route)  14.2 us
    all_to_all x2, starting transfers between devices, exchanged(): return lax.all_to_all(block, axis, split_axis=0, concat_axis=0, tiled=True)  7.13 us
    pallas_call x1, Pallas kernels, vmem_call(): pl.pallas_call(kernel, out_shape=jax.ShapeDtypeStruct(out_shape, jnp.bflo...  5.87 us
    pallas_call x1, Pallas kernels, local_lags(): pl.pallas_call(local_kernel, out_shape=jax.ShapeDtypeStruct((mine.shape[2...  5.49 us
    pallas_call x1, Pallas kernels, first_lags(): pl.pallas_call(first_lag_kernel, out_shape=jax.ShapeDtypeStruct((TMAX, LA...  3.59 us
  transfers between devices with their start and end apart: 7, of which 5 were waited for; matrix products, arithmetic and copies ran while one was open for 1% of the time, Pallas kernels for 10%

profile of v7, /device:TPU:9, one launch (start us, length us, event | category | flops | bytes accessed | tf_op | source)
XLA Modules:
  0.0 154.9 jit_solution(11494541095805993451)
XLA Ops:
  0.0 39.0 %all_to_all.20.traces = bf16[64,16,512]{2,1,0:T(8,128)(2,1)S(1)} all-to-all(bf16[64,16,512]{2,1,0:T(8,128)(2,1)} %param.6), channel_id=1, replica_groups=mesh['chan'=64,'band'=8] {'chan'}, dimensions={0} | all-to-all | bytes 2097152 | tf_op jit(solution)/shard_map/all_to_all | solution.py:420
  39.1 0.0 copy-done.5
  39.1 0.0 copy-done.6
  39.1 2.5 %shard_map.64.mine = bf16[8,16,16,128]{3,2,1,0:T(8,128)(2,1)S(1)} custom-call(s32[64]{0:T(128)S(1)} %copy-done.6, bf16[64,16,512]{2,1,0:T(8,128)(2,1)S(1)} %all_to_all.20.traces, bf16[256,256]{1,0:T(8,128)(2,1)S(1)} %copy-done.5), custom_call_target="tpu_custom_call" | custom-call | tf_op jit(solution)/shard_map/pallas_call | solution.py:107
  41.5 27.3 %all_to_all.21.own = bf16[8,16,16,128]{3,2,1,0:T(8,128)(2,1)S(1)} all-to-all(bf16[8,16,16,128]{3,2,1,0:T(8,128)(2,1)S(1)} %shard_map.64.mine), channel_id=1, replica_groups=mesh['chan'=64,'band'=8] {'band'}, dimensions={0} | all-to-all | bytes 1048576 | tf_op jit(solution)/shard_map/all_to_all | solution.py:420
  68.8 2.9 %collective-permute-start = (bf16[8,16,16,128]{3,2,1,0:T(8,128)(2,1)S(1)}, bf16[8,16,16,128]{3,2,1,0:T(8,128)(2,1)S(1)}, u32[]{:S(2)}, u32[]{:S(2)}) collective-permute-start(bf16[8,16,16,128]{3,2,1,0:T(8,128)(2,1)S(1)} %all_to_all.21.own), channel_id=1, source_target_pairs={{8,0},{16,8},{24,16},{32,24},{40,32},{48,40},{56,48},{64,56},{72,6... | collective-permute-start | bytes 1572872 | tf_op jit(solution)/shard_map/ppermute | solution.py:416
  71.7 7.6 %collective-permute-done.next1 = bf16[8,16,16,128]{3,2,1,0:T(8,128)(2,1)S(1)} collective-permute-done((bf16[8,16,16,128]{3,2,1,0:T(8,128)(2,1)S(1)}, bf16[8,16,16,128]{3,2,1,0:T(8,128)(2,1)S(1)}, u32[]{:S(2)}, u32[]{:S(2)}) %collective-permute-start) | collective-permute-done | bytes 524320 | tf_op jit(solution)/shard_map/ppermute | solution.py:416
  79.3 1.8 %shard_map.65 = bf16[8,32,16,128]{3,2,1,0:T(8,128)(2,1)} custom-call(bf16[8,16,16,128]{3,2,1,0:T(8,128)(2,1)S(1)} %all_to_all.21.own, bf16[8,16,16,128]{3,2,1,0:T(8,128)(2,1)S(1)} %collective-permute-done.next1), custom_call_target="tpu_custom_call" | custom-call | tf_op jit(solution)/shard_map/pallas_call | solution.py:151
  81.1 3.6 %all-to-all-start.2 = ((bf16[8,32,16,128]{3,2,1,0:T(8,128)(2,1)}), bf16[8,32,16,128]{3,2,1,0:T(8,128)(2,1)S(1)}, u32[]{:S(2)}, u32[]{:S(2)}) async-start(bf16[8,32,16,128]{3,2,1,0:T(8,128)(2,1)} %shard_map.65), calls=%async_computation.2 | async-start | bytes 2097152 | tf_op jit(solution)/shard_map/all_to_all | solution.py:420
  84.7 4.7 %collective-permute-start.2 = (bf16[8,16,16,128]{3,2,1,0:T(8,128)(2,1)S(1)}, bf16[8,16,16,128]{3,2,1,0:T(8,128)(2,1)S(1)}, u32[]{:S(2)}, u32[]{:S(2)}) collective-permute-start(bf16[8,16,16,128]{3,2,1,0:T(8,128)(2,1)S(1)} %all_to_all.21.own), channel_id=1, source_target_pairs={{24,8},{40,24},{56,40},{72,56},{88,72},{104,88},{120,104},{136,120... | collective-permute-start | bytes 1572872 | tf_op jit(solution)/shard_map/ppermute | solution.py:416
  89.3 1.3 collective-permute-start.1
  90.7 1.9 %collective-permute-start.3 = (bf16[3,16,16,128]{3,2,1,0:T(8,128)(2,1)S(1)}, bf16[3,16,16,128]{3,2,1,0:T(8,128)(2,1)S(1)}, u32[]{:S(2)}, u32[]{:S(2)}) collective-permute-start(bf16[3,16,16,128]{3,2,1,0:T(8,128)(2,1)S(1)} %slice.12), channel_id=1, source_target_pairs={{24,0},{32,8},{40,16},{48,24},{56,32},{64,40},{72,48},{80,56},{88,... | collective-permute-start | bytes 589832 | tf_op jit(solution)/shard_map/ppermute | solution.py:416
  92.6 7.2 %collective-permute-done.3.next3 = bf16[3,16,16,128]{3,2,1,0:T(8,128)(2,1)S(1)} collective-permute-done((bf16[3,16,16,128]{3,2,1,0:T(8,128)(2,1)S(1)}, bf16[3,16,16,128]{3,2,1,0:T(8,128)(2,1)S(1)}, u32[]{:S(2)}, u32[]{:S(2)}) %collective-permute-start.3) | collective-permute-done | bytes 196640 | tf_op jit(solution)/shard_map/ppermute | solution.py:416
  99.8 0.0 collective-permute-done.2.next2_odd
  99.8 0.0 collective-permute-done.1.next2_even
  99.8 5.9 %shard_map.67 = bf16[8,20,32,128]{3,2,1,0:T(8,128)(2,1)} custom-call(bf16[8,16,16,128]{3,2,1,0:T(8,128)(2,1)S(1)} %all_to_all.21.own, bf16[8,16,16,128]{3,2,1,0:T(8,128)(2,1)S(1)} %collective-permute-done.1.next2_even, bf16[8,16,16,128]{3,2,1,0:T(8,128)(2,1)S(1)} %collective-permute-done.2.next2_odd, bf16[3,16,16,128]{3,2,1,0:T(8,128)(2,1)S(1)} %collective-permute-done.3.next3), custom_call_target="tpu_custom_call" | custom-call | tf_op jit(solution)/shard_map/pallas_call | solution.py:250
  105.7 7.8 %all-to-all-done.2.near = bf16[8,32,16,128]{3,2,1,0:T(8,128)(2,1)S(1)} async-done(((bf16[8,32,16,128]{3,2,1,0:T(8,128)(2,1)}), bf16[8,32,16,128]{3,2,1,0:T(8,128)(2,1)S(1)}, u32[]{:S(2)}, u32[]{:S(2)}) %all-to-all-start.2) | async-done | bytes 1048608 | tf_op jit(solution)/shard_map/all_to_all | solution.py:420
  113.5 3.6 %all-to-all-start.3 = ((bf16[8,20,32,128]{3,2,1,0:T(8,128)(2,1)}), bf16[8,20,32,128]{3,2,1,0:T(8,128)(2,1)S(1)}, u32[]{:S(2)}, u32[]{:S(2)}) async-start(bf16[8,20,32,128]{3,2,1,0:T(8,128)(2,1)} %shard_map.67), calls=%async_computation.3 | async-start | bytes 2621440 | tf_op jit(solution)/shard_map/all_to_all | solution.py:420
  117.7 0.0 copy-done.7
  117.7 0.1 fusion.3
  117.8 3.3 %collective-permute-start.4 = (bf16[8,16,16,128]{3,2,1,0:T(8,128)(2,1)S(1)}, bf16[8,16,16,128]{3,2,1,0:T(8,128)(2,1)S(1)}, u32[]{:S(2)}, u32[]{:S(2)}) collective-permute-start(bf16[8,16,16,128]{3,2,1,0:T(8,128)(2,1)S(1)} %shard_map.64.mine), channel_id=1, source_target_pairs={{16,0},{24,8},{32,16},{40,24},{48,32},{56,40},{64,48},{72,56},{80,... | collective-permute-start | bytes 1572872 | tf_op jit(solution)/shard_map/ppermute | solution.py:416
  121.2 0.7 iota_reduce_fusion
  121.8 0.1 pad_add_fusion.info
  121.9 0.0 copy-done
  121.9 10.9 %collective-permute-done.4.other = bf16[8,16,16,128]{3,2,1,0:T(8,128)(2,1)S(1)} collective-permute-done((bf16[8,16,16,128]{3,2,1,0:T(8,128)(2,1)S(1)}, bf16[8,16,16,128]{3,2,1,0:T(8,128)(2,1)S(1)}, u32[]{:S(2)}, u32[]{:S(2)}) %collective-permute-start.4) | collective-permute-done | bytes 524320 | tf_op jit(solution)/shard_map/ppermute | solution.py:416
  132.8 0.9 copy-done.2
  133.7 5.5 %shard_map.68.same = f32[16,208,128]{2,1,0:T(8,128)S(1)} custom-call(s32[1]{0:T(128)} %bitcast.4.first, bf16[8,16,16,128]{3,2,1,0:T(8,128)(2,1)S(1)} %shard_map.64.mine, bf16[8,16,16,128]{3,2,1,0:T(8,128)(2,1)S(1)} %collective-permute-done.4.other, bf16[208,256]{1,0:T(8,128)(2,1)S(1)} %copy-done.2), custom_call_target="tpu_custom_call" | custom-call | tf_op jit(solution)/shard_map/pallas_call | solution.py:238
  139.3 0.0 copy-start.3
  139.3 0.9 copy-done.3
  140.2 3.6 %shard_map.66.begun = bf16[4,201,16,128]{3,2,1,0:T(8,128)(2,1)} custom-call(s32[9]{0:T(128)S(1)} %pad_add_fusion.info, bf16[8,32,16,128]{3,2,1,0:T(8,128)(2,1)S(1)} %copy-done.1, bf16[208,256]{1,0:T(8,128)(2,1)S(1)} %copy-done.3), custom_call_target="tpu_custom_call" | custom-call | tf_op jit(solution)/shard_map/pallas_call | solution.py:295
  143.8 8.0 %all-to-all-done.3.far = bf16[8,20,32,128]{3,2,1,0:T(8,128)(2,1)S(1)} async-done(((bf16[8,20,32,128]{3,2,1,0:T(8,128)(2,1)}), bf16[8,20,32,128]{3,2,1,0:T(8,128)(2,1)S(1)}, u32[]{:S(2)}, u32[]{:S(2)}) %all-to-all-start.3) | async-done | bytes 1310752 | tf_op jit(solution)/shard_map/all_to_all | solution.py:420
  151.8 2.9 %shard_map.69 = bf16[4,201,16,128]{3,2,1,0:T(8,128)(2,1)} custom-call(s32[9]{0:T(128)S(1)} %pad_add_fusion.info, bf16[4,201,16,128]{3,2,1,0:T(8,128)(2,1)} %shard_map.66.begun, f32[16,208,128]{2,1,0:T(8,128)S(1)} %shard_map.68.same, bf16[8,20,32,128]{3,2,1,0:T(8,128)(2,1)S(1)} %all-to-all-done.3.far, ...), custom_call_target="tpu_custom_call", output_to_operand_aliasing={{}: (1, {})} | custom-call | tf_op jit(solution)/shard_map/pallas_call | solution.py:391
  (12 shorter events, 0.0 us)
Async XLA Ops:
  0.0 39.1 %copy-start.5 = (bf16[256,256]{1,0:T(8,128)(2,1)S(1)}, bf16[256,256]{1,0:T(8,128)(2,1)}, u32[]{:S(2)}) copy-start(bf16[256,256]{1,0:T(8,128)(2,1)} %constant.29.clone.forward) | copy-start | bytes 393220
  0.0 39.1 %copy-start.6 = (s32[64]{0:T(128)S(1)}, s32[64]{0:T(128)}, u32[]{:S(2)}) copy-start(s32[64]{0:T(128)} %starts.1) | copy-start | bytes 772
  68.8 10.5 %collective-permute-start = (bf16[8,16,16,128]{3,2,1,0:T(8,128)(2,1)S(1)}, bf16[8,16,16,128]{3,2,1,0:T(8,128)(2,1)S(1)}, u32[]{:S(2)}, u32[]{:S(2)}) collective-permute-start(bf16[8,16,16,128]{3,2,1,0:T(8,128)(2,1)S(1)} %all_to_all.21.own), channel_id=1, source_target_pairs={{8,0},{16,8},{24,16},{32,24},{40,32},{48,40},{56,48},{64,56},{72,6... | collective-permute-start | bytes 1572872 | tf_op jit(solution)/shard_map/ppermute | solution.py:416
  81.1 32.4 %all-to-all-start.2 = ((bf16[8,32,16,128]{3,2,1,0:T(8,128)(2,1)}), bf16[8,32,16,128]{3,2,1,0:T(8,128)(2,1)S(1)}, u32[]{:S(2)}, u32[]{:S(2)}) async-start(bf16[8,32,16,128]{3,2,1,0:T(8,128)(2,1)} %shard_map.65), calls=%async_computation.2 | async-start | bytes 2097152 | tf_op jit(solution)/shard_map/all_to_all | solution.py:420
  84.7 15.1 %collective-permute-start.2 = (bf16[8,16,16,128]{3,2,1,0:T(8,128)(2,1)S(1)}, bf16[8,16,16,128]{3,2,1,0:T(8,128)(2,1)S(1)}, u32[]{:S(2)}, u32[]{:S(2)}) collective-permute-start(bf16[8,16,16,128]{3,2,1,0:T(8,128)(2,1)S(1)} %all_to_all.21.own), channel_id=1, source_target_pairs={{24,8},{40,24},{56,40},{72,56},{88,72},{104,88},{120,104},{136,120... | collective-permute-start | bytes 1572872 | tf_op jit(solution)/shard_map/ppermute | solution.py:416
  89.3 10.4 %collective-permute-start.1 = (bf16[8,16,16,128]{3,2,1,0:T(8,128)(2,1)S(1)}, bf16[8,16,16,128]{3,2,1,0:T(8,128)(2,1)S(1)}, u32[]{:S(2)}, u32[]{:S(2)}) collective-permute-start(bf16[8,16,16,128]{3,2,1,0:T(8,128)(2,1)S(1)} %collective-permute-done.next1), channel_id=1, source_target_pairs={{8,0},{24,16},{40,32},{56,48},{72,64},{88,80},{104,96},{120,112},{... | collective-permute-start | bytes 1572872 | tf_op jit(solution)/shard_map/ppermute | solution.py:416
  90.7 9.1 %collective-permute-start.3 = (bf16[3,16,16,128]{3,2,1,0:T(8,128)(2,1)S(1)}, bf16[3,16,16,128]{3,2,1,0:T(8,128)(2,1)S(1)}, u32[]{:S(2)}, u32[]{:S(2)}) collective-permute-start(bf16[3,16,16,128]{3,2,1,0:T(8,128)(2,1)S(1)} %slice.12), channel_id=1, source_target_pairs={{24,0},{32,8},{40,16},{48,24},{56,32},{64,40},{72,48},{80,56},{88,... | collective-permute-start | bytes 589832 | tf_op jit(solution)/shard_map/ppermute | solution.py:416
  105.6 12.1 %copy-start.7 = (s32[1,4]{1,0:T(1,128)S(1)}, s32[1,4]{1,0:T(1,128)}, u32[]{:S(2)}) copy-start(s32[1,4]{1,0:T(1,128)} %param.8) | copy-start | bytes 52
  113.5 8.5 %copy-start = (bf16[8,32,16,128]{3,2,1,0:T(8,128)(2,1)}, bf16[8,32,16,128]{3,2,1,0:T(8,128)(2,1)S(1)}, u32[]{:S(2)}) copy-start(bf16[8,32,16,128]{3,2,1,0:T(8,128)(2,1)S(1)} %all-to-all-done.2.near) | copy-start | bytes 3145732
  113.5 38.3 %all-to-all-start.3 = ((bf16[8,20,32,128]{3,2,1,0:T(8,128)(2,1)}), bf16[8,20,32,128]{3,2,1,0:T(8,128)(2,1)S(1)}, u32[]{:S(2)}, u32[]{:S(2)}) async-start(bf16[8,20,32,128]{3,2,1,0:T(8,128)(2,1)} %shard_map.67), calls=%async_computation.3 | async-start | bytes 2621440 | tf_op jit(solution)/shard_map/all_to_all | solution.py:420
  117.8 15.0 %collective-permute-start.4 = (bf16[8,16,16,128]{3,2,1,0:T(8,128)(2,1)S(1)}, bf16[8,16,16,128]{3,2,1,0:T(8,128)(2,1)S(1)}, u32[]{:S(2)}, u32[]{:S(2)}) collective-permute-start(bf16[8,16,16,128]{3,2,1,0:T(8,128)(2,1)S(1)} %shard_map.64.mine), channel_id=1, source_target_pairs={{16,0},{24,8},{32,16},{40,24},{48,32},{56,40},{64,48},{72,56},{80,... | collective-permute-start | bytes 1572872 | tf_op jit(solution)/shard_map/ppermute | solution.py:416
  132.8 0.9 copy-start.2
  133.7 5.5 %copy-start.1 = (bf16[8,32,16,128]{3,2,1,0:T(8,128)(2,1)S(1)}, bf16[8,32,16,128]{3,2,1,0:T(8,128)(2,1)}, u32[]{:S(2)}) copy-start(bf16[8,32,16,128]{3,2,1,0:T(8,128)(2,1)} %copy-done) | copy-start | bytes 3145732
  139.3 0.9 copy-start.3
  140.2 11.6 %copy-start.4 = (bf16[208,256]{1,0:T(8,128)(2,1)S(1)}, bf16[208,256]{1,0:T(8,128)(2,1)}, u32[]{:S(2)}) copy-start(bf16[208,256]{1,0:T(8,128)(2,1)} %constant.30.clone.inverse) | copy-start | bytes 319492
